TPU v7x, 512 devices: a whole 4x4x16 slice. The times are simulated.
512 devices in a mesh: tm: 4 (over x), obs: 128 (over z, y, core).
Axes of the slice: x: 4, y: 4, z: 16, core: 2. Of those that a mesh axis runs over, the one named last changes fastest.
Arguments:
- control: float32 [3, 4, 256, 512], P(None, 'tm', 'obs'), may hold values from -6 to 6
- diffusivity: float32 [256, 512], P('obs'), may hold values from 0.2 to 1
- footprints: bfloat16 [512, 4, 128, 4096], P('obs', None, None, 'tm'), may hold values from -0.046875 to 0.046875
- tile_lists: int32 [512, 4], P('obs'), may hold values from 0 to 127, as said below
- tile_counts: int32 [512], P('obs'), may hold values from 1 to 4, as said below
- measured: float32 [3, 65536], P(None, 'obs'), may hold values from -4 to 4
- weight: float32 [3, 65536], P(None, 'obs'), may hold values from 0.5 to 4
Outputs:
- gradient: float32 [3, 4, 256, 512], P(None, 'tm', 'obs')
- residual: float32 [3, 65536], P(None, 'obs')
Inputs may be any that keep to these rules, and one draw needn't show every extreme that they name: `tile_lists`: entry 0 of block b's list is tile b // 4, the tile of the block's own device; the 4 entries of one list are distinct; entries at positions tile_counts[b] or later are padding. `tile_counts`: the first block of every device has a full list.
All inputs are finite; a program needn't handle non-finite values.
Results may differ from a plain program's by a relative error of at most 0.002.
Values may be sent and summed in bfloat16 or wider, within the bound.
No kernel may reach another device: no remote copies, remote signals or barrier semaphores. Data moves between devices by JAX's collectives and lax.ppermute only.
A program may use at most 64 MiB of HBM per device.

v0:
```python
import jax
import jax.numpy as jnp
from jax import lax
from jax.sharding import PartitionSpec as P

ND = 2


def padded(cells, sides, width):
    for axis, dim in sides:
        count = lax.axis_size(axis)
        ends = count - 1
        head = lax.slice_in_dim(cells, 0, width, axis=dim)
        tail = lax.slice_in_dim(cells, cells.shape[dim] - width, cells.shape[dim], axis=dim)
        cells = jnp.concatenate(
            [
                lax.ppermute(tail, axis, [(i, (i + 1) % count) for i in range(ends)]),
                cells,
                lax.ppermute(head, axis, [((i + 1) % count, i) for i in range(ends)]),
            ],
            axis=dim,
        )
    return cells


def diffuse_once(fields, conduct):
    middle = fields[:, 1:-1]
    conduct_mid = conduct[1:-1]
    zero_col = jnp.zeros_like(conduct_mid[:, :1])
    conduct_left = jnp.concatenate([zero_col, conduct_mid[:, :-1]], axis=1)
    conduct_right = jnp.concatenate([conduct_mid[:, 1:], zero_col], axis=1)
    zero_field = jnp.zeros_like(middle[:, :, :1])
    left_values = jnp.concatenate([zero_field, middle[:, :, :-1]], axis=2)
    right_values = jnp.concatenate([middle[:, :, 1:], zero_field], axis=2)
    return (
        middle
        + 0.0625 * (conduct_mid + conduct[:-2]) * (fields[:, :-2] - middle)
        + 0.0625 * (conduct_mid + conduct[2:]) * (fields[:, 2:] - middle)
        + 0.0625 * (conduct_mid + conduct_left) * (left_values - middle)
        + 0.0625 * (conduct_mid + conduct_right) * (right_values - middle)
    )


def shards(control, diffusivity, footprints, tile_lists, tile_counts, measured, weight):
    tracer_count, slab_steps, tile_rows, grid_width = control.shape
    blocks_here, ref_count = tile_lists.shape
    tile_total = lax.axis_size("obs")
    slot_cells = slab_steps * tile_rows * grid_width
    field_count = tracer_count * slab_steps
    fields = control.reshape(field_count, tile_rows, grid_width)
    valid = jnp.arange(ref_count, dtype=jnp.int32)[None, :] < tile_counts[:, None]
    flat_ids = tile_lists.reshape(-1)
    flat_valid = valid.reshape(-1)
    tile_numbers = jnp.arange(tile_total, dtype=jnp.int32)
    selector = (flat_ids[:, None] == tile_numbers[None, :]) & flat_valid[:, None]
    selector_full = selector.astype(jnp.float32)
    diff_rims = padded(diffusivity, (("obs", 0),), ND)

    def spread(values):
        for repeat in range(ND):
            extended = padded(values, (("obs", 1),), 1)
            values = diffuse_once(extended, diff_rims[ND - 1 : ND + 1 + tile_rows])
        return values

    flux_half = spread(fields).astype(jnp.bfloat16)
    own_panel = flux_half.reshape(1, tracer_count * slot_cells)
    block_rows = lax.all_gather(own_panel, "obs", axis=0, tiled=True)
    owners = jnp.arange(block_rows.shape[0], dtype=jnp.int32)
    chooser = ((flat_ids[:, None] == owners[None, :]) & flat_valid[:, None]).astype(jnp.bfloat16)
    chosen = jnp.dot(chooser, block_rows, preferred_element_type=jnp.float32)
    chosen_half = chosen.astype(jnp.bfloat16).reshape(
        blocks_here, ref_count, tracer_count, slot_cells
    )
    partial_value = jnp.einsum(
        "bkin,bkcn->cbi", footprints, chosen_half, preferred_element_type=jnp.float32
    )
    predicted = lax.psum(partial_value, "tm").reshape(tracer_count, -1)
    residual = (predicted - measured) * weight
    residual_half = residual.astype(jnp.bfloat16).reshape(tracer_count, blocks_here, -1)
    adjoint = jnp.einsum(
        "bkin,cbi->bkcn", footprints, residual_half, preferred_element_type=jnp.float32
    )
    adjoint = adjoint.reshape(blocks_here * ref_count, tracer_count * slot_cells)
    returned = lax.psum_scatter(
        jnp.dot(
            selector_full.T,
            adjoint,
            precision=lax.Precision.HIGHEST,
            preferred_element_type=jnp.float32,
        ),
        "obs",
        scatter_dimension=0,
        tiled=True,
    )
    returned = returned.reshape(field_count, tile_rows, grid_width)
    returned = spread(returned)
    gradient = control + returned.reshape(control.shape)
    return (gradient, residual)


def solution(mesh):
    placed = (
        P(None, "tm", "obs", None),
        P("obs", None),
        P("obs", None, None, "tm"),
        P("obs", None),
        P("obs"),
        P(None, "obs"),
        P(None, "obs"),
    )
    return jax.shard_map(
        shards,
        mesh=mesh,
        in_specs=placed,
        out_specs=(P(None, "tm", "obs", None), P(None, "obs")),
        check_vma=False,
    )
```

profile of v0, /device:TPU:1, one launch (start us, length us, event | category | flops | bytes accessed | tf_op | source)
XLA Modules:
  0.0 532.8 jit_solution(17579860208562711567)
XLA Ops:
  7.2 0.0 all-reduce.13.cloned.1.call-start
  7.2 4.6 collective-permute-start
  11.8 5.5 %collective-permute-start.2 = (f32[2,512]{1,0:T(2,128)}, f32[2,512]{1,0:T(2,128)S(1)}, u32[]{:S(2)}, u32[]{:S(2)}) collective-permute-start(f32[2,512]{1,0:T(2,128)} %param.8), channel_id=1, source_target_pairs={{1,0},{2,1},{3,2},{4,3},{5,4},{6,5},{7,6},{8,7},{9,8},{10,9},{11,1... | collective-permute-start | bytes 12296 | tf_op jit(solution)/shard_map/ppermute | solution.py:19
  17.3 0.8 fusion.57
  18.1 1.9 collective-permute-start.1
  20.0 2.4 collective-permute-start.3
  22.4 0.8 fusion.58
  23.3 0.9 fusion.56
  24.1 0.7 iota_compare_fusion.1
  24.9 0.1 lt.23
  25.0 0.8 eq.8
  25.7 0.0 collective-permute-done
  25.7 0.0 collective-permute-done.2
  25.7 0.9 fusion.42
  26.6 0.0 collective-permute-done.1
  26.6 0.0 collective-permute-done.3
  26.6 0.9 fusion.30
  27.5 3.2 collective-permute-start.4
  30.7 1.9 collective-permute-start.5
  32.6 0.1 fusion.55
  32.7 2.9 collective-permute-done.5
  35.7 0.1 fusion.34
  35.8 113.6 %all-gather = bf16[128,1,3072]{2,1,0:T(2,128)(2,1)S(1)} all-gather(bf16[1,1,3072]{2,1,0:T(2,128)(2,1)S(1)} %reshape.56), channel_id=1, replica_groups=mesh['tm'=4,'obs'=128] {'obs'}, dimensions={0}, use_global_device_ids=true | all-gather | bytes 792576 | tf_op jit(solution)/shard_map/all_gather | solution.py:67
  149.4 0.3 convolution_convert_fusion
  149.7 0.2 reshape.50
  149.9 3.4 convolution_bitcast_fusion
  153.2 8.6 %psum.7 = f32[3,512]{1,0:T(4,128)S(1)} all-reduce(f32[3,512]{1,0:T(4,128)S(1)} %convolution_bitcast_fusion), channel_id=1, replica_groups=mesh['tm'=4,'obs'=128] {'tm'}, use_global_device_ids=true, to_apply=%region_0.0 | all-reduce | flops 1536 | bytes 12288 | tf_op jit(solution)/shard_map/psum | solution.py:77
  161.9 0.0 copy-start.1
  161.9 0.0 copy-start
  161.9 2.8 fusion.43
  164.7 0.1 copy.15
  164.9 2.0 fusion.36
  166.9 0.0 all-reduce.13.cloned.1.call-update
  166.9 1.3 dynamic-slice
  168.2 337.9 %all-reduce.13.cloned.1.call-done = f32[128,3072]{1,0:T(8,128)} async-done(((f32[128,3072]{1,0:T(8,128)}), f32[128,3072]{1,0:T(8,128)}) %all-reduce.13.cloned.1.call-update) | async-done | bytes 1572880
  506.1 1.6 dynamic-slice_reduce_fusion
  507.7 5.6 %collective-permute-start.6 = (f32[3,1,512]{2,1,0:T(1,128)S(1)}, f32[3,1,512]{2,1,0:T(1,128)S(1)}, u32[]{:S(2)}, u32[]{:S(2)}) collective-permute-start(f32[3,1,512]{2,1,0:T(1,128)S(1)} %get-tuple-element.8), channel_id=1, source_target_pairs={{0,1},{1,2},{2,3},{3,4},{4,5},{5,6},{6,7},{7,8},{8,9},{9,10},{10,1... | collective-permute-start | bytes 18440 | tf_op jit(solution)/shard_map/ppermute | solution.py:17
  513.3 1.9 collective-permute-start.7
  515.3 0.1 fusion.52
  515.3 0.0 collective-permute-done.6
  515.4 2.9 collective-permute-done.7
  518.3 0.1 fusion.14
  518.4 1.9 collective-permute-start.8
  520.3 2.4 collective-permute-start.9
  522.7 0.1 fusion.51
  522.8 0.0 collective-permute-done.8
  522.8 2.5 collective-permute-done.9
  525.3 0.7 bitcast_add_fusion
  (13 shorter events, 0.1 us)
Async XLA Ops:
  7.2 498.9 %all-reduce.13.cloned.1.call-start = ((), (), s32[]{:S(2)}) async-start(), calls=%async_computation | async-start | bytes 3145728
  7.2 18.5 %collective-permute-start = (f32[2,512]{1,0:T(2,128)}, f32[2,512]{1,0:T(2,128)S(1)}, u32[]{:S(2)}, u32[]{:S(2)}) collective-permute-start(f32[2,512]{1,0:T(2,128)} %param.8), channel_id=1, source_target_pairs={{0,1},{1,2},{2,3},{3,4},{4,5},{5,6},{6,7},{7,8},{8,9},{9,10},{10,1... | collective-permute-start | bytes 12296 | tf_op jit(solution)/shard_map/ppermute | solution.py:17
  11.8 13.9 %collective-permute-start.2 = (f32[2,512]{1,0:T(2,128)}, f32[2,512]{1,0:T(2,128)S(1)}, u32[]{:S(2)}, u32[]{:S(2)}) collective-permute-start(f32[2,512]{1,0:T(2,128)} %param.8), channel_id=1, source_target_pairs={{1,0},{2,1},{3,2},{4,3},{5,4},{6,5},{7,6},{8,7},{9,8},{10,9},{11,1... | collective-permute-start | bytes 12296 | tf_op jit(solution)/shard_map/ppermute | solution.py:19
  18.1 8.5 %collective-permute-start.1 = (f32[3,1,512]{2,1,0:T(1,128)S(1)}, f32[3,1,512]{2,1,0:T(1,128)S(1)}, u32[]{:S(2)}, u32[]{:S(2)}) collective-permute-start(f32[3,1,512]{2,1,0:T(1,128)S(1)} %get-tuple-element.16), channel_id=1, source_target_pairs={{0,1},{1,2},{2,3},{3,4},{4,5},{5,6},{6,7},{7,8},{8,9},{9,10},{10,1... | collective-permute-start | bytes 18440 | tf_op jit(solution)/shard_map/ppermute | solution.py:17
  20.0 6.6 %collective-permute-start.3 = (f32[3,1,512]{2,1,0:T(1,128)S(1)}, f32[3,1,512]{2,1,0:T(1,128)S(1)}, u32[]{:S(2)}, u32[]{:S(2)}) collective-permute-start(f32[3,1,512]{2,1,0:T(1,128)S(1)} %get-tuple-element.17), channel_id=1, source_target_pairs={{1,0},{2,1},{3,2},{4,3},{5,4},{6,5},{7,6},{8,7},{9,8},{10,9},{11,1... | collective-permute-start | bytes 18440 | tf_op jit(solution)/shard_map/ppermute | solution.py:19
  27.5 5.2 collective-permute-start.4
  30.7 4.9 collective-permute-start.5
  149.4 12.4 %copy-start.2 = (f32[3,512]{1,0:T(4,128)S(1)}, f32[3,512]{1,0:T(4,128)}, u32[]{:S(2)}) copy-start(f32[3,512]{1,0:T(4,128)} %param.13) | copy-start | bytes 18436
  149.4 12.5 %copy-start.3 = (f32[3,512]{1,0:T(4,128)S(1)}, f32[3,512]{1,0:T(4,128)}, u32[]{:S(2)}) copy-start(f32[3,512]{1,0:T(4,128)} %param.12) | copy-start | bytes 18436
  161.9 353.5 %copy-start.1 = (f32[3,512]{1,0:T(4,128)}, f32[3,512]{1,0:T(4,128)S(1)}, u32[]{:S(2)}) copy-start(f32[3,512]{1,0:T(4,128)S(1)} %subtract_multiply_fusion) | copy-start | bytes 18436
  161.9 363.4 %copy-start = (f32[3,1,2,512]{3,2,1,0:T(2,128)S(1)}, f32[3,1,2,512]{3,2,1,0:T(2,128)}, u32[]{:S(2)}) copy-start(f32[3,1,2,512]{3,2,1,0:T(2,128)} %param.7) | copy-start | bytes 36868
  507.7 7.6 %collective-permute-start.6 = (f32[3,1,512]{2,1,0:T(1,128)S(1)}, f32[3,1,512]{2,1,0:T(1,128)S(1)}, u32[]{:S(2)}, u32[]{:S(2)}) collective-permute-start(f32[3,1,512]{2,1,0:T(1,128)S(1)} %get-tuple-element.8), channel_id=1, source_target_pairs={{0,1},{1,2},{2,3},{3,4},{4,5},{5,6},{6,7},{7,8},{8,9},{9,10},{10,1... | collective-permute-start | bytes 18440 | tf_op jit(solution)/shard_map/ppermute | solution.py:17
  513.3 4.9 collective-permute-start.7
  518.4 4.4 collective-permute-start.8
  520.3 4.9 collective-permute-start.9
Sparse Core Ops, SparseCore 0:
  167.0 339.0 all-reduce.12
where the time goes:
time: 536 us; the launch traced here: 533 us
  waiting for transfers between devices  346 us (65%)
  blocking collectives  122 us (23%)
  starting transfers between devices  31.4 us (6%)
  between operations  14.2 us (3%)
  matrix products  8.57 us (2%)
  local copies, waits for them, and re-layouts  6.77 us (1%)
    unnamed x2, waiting for transfers between devices  338 us
    all_gather x1, blocking collectives, shards(): block_rows = lax.all_gather(own_panel, 'obs', axis=0, tiled=True)  114 us
    ppermute x5, starting transfers between devices, padded(): lax.ppermute(tail, axis, [(i, (i + 1) % count) for i in range(ends)])  17.2 us
    ppermute x5, starting transfers between devices, padded(): lax.ppermute(head, axis, [((i + 1) % count, i) for i in range(ends)])  14.1 us
  transfers between devices with their start and end apart: 11, of which 4 were waited for; matrix products, arithmetic and copies ran while one was open for 1% of the time, Pallas kernels for 0%

commit v1 on v0

v1 whole, which is shorter than its diff:
```python
import jax
import jax.numpy as jnp
from jax import lax
from jax.sharding import Mesh, PartitionSpec as P

ZN, YN, CN = 16, 4, 2
OBS = ("z", "y", "c")


def sweep(fields, conduct):
    middle = fields[:, 1:-1]
    conduct_mid = conduct[1:-1]
    zero_col = jnp.zeros_like(conduct_mid[:, :1])
    conduct_left = jnp.concatenate([zero_col, conduct_mid[:, :-1]], axis=1)
    conduct_right = jnp.concatenate([conduct_mid[:, 1:], zero_col], axis=1)
    zero_field = jnp.zeros_like(middle[:, :, :1])
    left_values = jnp.concatenate([zero_field, middle[:, :, :-1]], axis=2)
    right_values = jnp.concatenate([middle[:, :, 1:], zero_field], axis=2)
    return (
        middle
        + 0.0625 * (conduct_mid + conduct[:-2]) * (fields[:, :-2] - middle)
        + 0.0625 * (conduct_mid + conduct[2:]) * (fields[:, 2:] - middle)
        + 0.0625 * (conduct_mid + conduct_left) * (left_values - middle)
        + 0.0625 * (conduct_mid + conduct_right) * (right_values - middle)
    )


def with_neighbours(own, core, tiles):
    mate = lax.ppermute(own, "c", [(0, 1), (1, 0)])
    pairs = [(i, i + 1) for i in range(1, tiles - 1, 2)]
    other = lax.ppermute(own, OBS, pairs + [(b, a) for a, b in pairs])
    before = jnp.where(core == 0, other, mate)
    after = jnp.where(core == 0, mate, other)
    return jnp.concatenate([before, own, after], axis=1)


def two_sweeps(fields, conduct, inside):
    return sweep(sweep(fields, conduct) * inside, conduct[1:-1])


def shards(control, diffusivity, footprints, tile_lists, tile_counts, measured, weight):
    tracers = control.shape[0]
    blocks, refs = tile_lists.shape
    tiles = ZN * YN * CN
    cells = control.shape[1] * control.shape[2] * control.shape[3]
    core = lax.axis_index("c")
    here = lax.axis_index(OBS)
    fields = control.reshape(tracers, 2, -1)

    ext = with_neighbours(jnp.concatenate([fields, diffusivity[None]], axis=0), core, tiles)
    conduct = ext[tracers]
    row = jnp.arange(4, dtype=jnp.int32)[:, None]
    inside = (((row > 0) | (here > 0)) & ((row < 3) | (here < tiles - 1))).astype(jnp.float32)
    flux_half = two_sweeps(ext[:tracers], conduct, inside).astype(jnp.bfloat16)

    own_panel = flux_half.reshape(1, tracers * cells)
    by_z = lax.all_to_all(jnp.broadcast_to(own_panel, (ZN, tracers * cells)), "z", 0, 0, tiled=True)
    by_y = lax.all_to_all(jnp.broadcast_to(by_z[None], (YN,) + by_z.shape), "y", 0, 0, tiled=True)
    panels = lax.all_gather(by_y.reshape(YN * ZN, tracers * cells), "c", axis=0, tiled=True)

    slot = jnp.arange(tiles, dtype=jnp.int32)
    owner = (slot % ZN) * (YN * CN) + (slot // ZN) % YN * CN + slot // (ZN * YN)
    valid = (jnp.arange(refs, dtype=jnp.int32)[None, :] < tile_counts[:, None]).reshape(-1)
    picks = (tile_lists.reshape(-1)[:, None] == owner[None, :]) & valid[:, None]
    chosen = jnp.dot(picks.astype(jnp.bfloat16), panels, preferred_element_type=jnp.float32)
    chosen = chosen.astype(jnp.bfloat16).reshape(blocks, refs, tracers, cells)
    part = jnp.einsum("bkin,bkcn->cbi", footprints, chosen, preferred_element_type=jnp.float32)
    predicted = lax.psum(part, "tm").reshape(tracers, -1)
    residual = (predicted - measured) * weight
    residual_half = residual.astype(jnp.bfloat16).reshape(tracers, blocks, -1)

    adjoint = jnp.einsum("bkin,cbi->bkcn", footprints, residual_half, preferred_element_type=jnp.float32)
    adjoint = adjoint.reshape(blocks * refs, tracers * cells)
    dense = jnp.dot(
        picks.astype(jnp.float32).T, adjoint, precision=lax.Precision.HIGHEST, preferred_element_type=jnp.float32
    )
    over_c = lax.all_to_all(dense.reshape(CN, YN * ZN, -1), "c", 0, 0, tiled=True).sum(axis=0)
    over_y = lax.all_to_all(over_c.reshape(YN, ZN, -1), "y", 0, 0, tiled=True).sum(axis=0)
    over_z = lax.all_to_all(over_y.astype(jnp.bfloat16), "z", 0, 0, tiled=True)
    total = over_z.astype(jnp.float32).sum(axis=0).reshape(fields.shape)

    spread = two_sweeps(with_neighbours(total, core, tiles), conduct, inside)
    return control + spread.reshape(control.shape), residual


def solution(mesh):
    fine = Mesh(mesh.devices.reshape(mesh.shape["tm"], ZN, YN, CN), ("tm",) + OBS)
    placed = (
        P(None, "tm", OBS, None),
        P(OBS, None),
        P(OBS, None, None, "tm"),
        P(OBS, None),
        P(OBS),
        P(None, OBS),
        P(None, OBS),
    )
    return jax.shard_map(
        shards,
        mesh=fine,
        in_specs=placed,
        out_specs=(P(None, "tm", OBS, None), P(None, OBS)),
        check_vma=False,
    )
```

time: 536 us -> 127 us (0.24)
  waiting for transfers between devices: 346 us -> 9.33 us
  blocking collectives: 122 us -> 70.5 us
  between operations: 14.2 us -> 0.9 us
  starting transfers between devices: 31.4 us -> 24.5 us
  other arithmetic: 3.39 us -> 9.48 us
    unnamed x2 -> x0, waiting for transfers between devices: 338 us -> none
    all_gather x1, blocking collectives: 114 us -> 4.63 us  [shards(): lax.all_gather(by_y.reshape(YN * ZN, tracers * cells), 'c', axis=0, tiled...]
    all_to_all x0 -> x4, blocking collectives: none -> 57.3 us  [the longest x1 21.2 us: shards(): lax.all_to_all(jnp.broadcast_to(own_panel, (ZN, tracers * cells)), 'z', 0...]
    ppermute x10 -> x4, starting transfers between devices: 31.4 us -> 17.5 us  [the longest x2 13.5 us: with_neighbours(): mate = lax.ppermute(own, 'c', [(0, 1), (1, 0)])]
    all_to_all x0 -> x1, starting transfers between devices: none -> 6.99 us  [shards(): lax.all_to_all(jnp.broadcast_to(by_z[None], (YN,) + by_z.shape), 'y', 0,...]
  transfers between devices with their start and end apart: 11 -> 5, of which waited for: 4 -> 3; matrix products, arithmetic and copies ran while one was open for 1% -> 3% of each run, Pallas kernels for 0% -> 0%
where the time goes in v1:
time: 127 us; the launch traced here: 126 us
  blocking collectives  70.5 us (56%)
  starting transfers between devices  24.5 us (19%)
  other arithmetic  9.48 us (7%)
  waiting for transfers between devices  9.33 us (7%)
  matrix products  7.36 us (6%)
  local copies, waits for them, and re-layouts  4.1 us (3%)
    all_to_all x1, blocking collectives, shards(): lax.all_to_all(jnp.broadcast_to(own_panel, (ZN, tracers * cells)), 'z', 0...  21.2 us
    all_to_all x1, blocking collectives, shards(): over_z = lax.all_to_all(over_y.astype(jnp.bfloat16), 'z', 0, 0, tiled=True)  14.7 us
    all_to_all x1, blocking collectives, shards(): lax.all_to_all(over_c.reshape(YN, ZN, -1), 'y', 0, 0, tiled=True)  14.4 us
    ppermute x2, starting transfers between devices, with_neighbours(): mate = lax.ppermute(own, 'c', [(0, 1), (1, 0)])  13.5 us
    psum x1, blocking collectives, shards(): predicted = lax.psum(part, 'tm').reshape(tracers, -1)  8.57 us
    all_to_all x1, blocking collectives, shards(): lax.all_to_all(dense.reshape(CN, YN * ZN, -1), 'c', 0, 0, tiled=True)  7.02 us
    all_to_all x1, starting transfers between devices, shards(): lax.all_to_all(jnp.broadcast_to(by_z[None], (YN,) + by_z.shape), 'y', 0,...  6.99 us
    all_to_all x1, waiting for transfers between devices, shards(): lax.all_to_all(jnp.broadcast_to(by_z[None], (YN,) + by_z.shape), 'y', 0,...  4.91 us
  transfers between devices with their start and end apart: 5, of which 3 were waited for; matrix products, arithmetic and copies ran while one was open for 3% of the time, Pallas kernels for 0%

profile of v1, /device:TPU:1, one launch (start us, length us, event | category | flops | bytes accessed | tf_op | source)
XLA Modules:
  0.0 126.2 jit_solution(13711642190260254408)
XLA Ops:
  0.6 0.7 pad_maximum_fusion.3
  1.4 8.8 %collective-permute-start.1 = (f32[4,2,512]{2,1,0:T(2,128)S(1)}, f32[4,2,512]{2,1,0:T(2,128)S(1)}, u32[]{:S(2)}, u32[]{:S(2)}) collective-permute-start(f32[4,2,512]{2,1,0:T(2,128)S(1)} %pad_maximum_fusion.3), channel_id=1, source_target_pairs={{0,1},{1,0},{2,3},{3,2},{4,5},{5,4},{6,7},{7,6},{8,9},{9,8},{10,11... | collective-permute-start | bytes 49160 | tf_op jit(solution)/shard_map/ppermute | solution.py:29
  10.2 1.9 %collective-permute-start = (f32[4,2,512]{2,1,0:T(2,128)S(1)}, f32[4,2,512]{2,1,0:T(2,128)S(1)}, u32[]{:S(2)}, u32[]{:S(2)}) collective-permute-start(f32[4,2,512]{2,1,0:T(2,128)S(1)} %pad_maximum_fusion.3), channel_id=1, source_target_pairs={{1,2},{3,4},{5,6},{7,8},{9,10},{11,12},{13,14},{15,16},{17,18},{19... | collective-permute-start | bytes 49160 | tf_op jit(solution)/shard_map/ppermute | solution.py:31
  12.1 0.8 fusion.64
  12.9 0.8 add_multiply_fusion.3
  13.7 1.5 %collective-permute-done = f32[4,2,512]{2,1,0:T(2,128)S(1)} collective-permute-done((f32[4,2,512]{2,1,0:T(2,128)S(1)}, f32[4,2,512]{2,1,0:T(2,128)S(1)}, u32[]{:S(2)}, u32[]{:S(2)}) %collective-permute-start) | collective-permute-done | bytes 16416 | tf_op jit(solution)/shard_map/ppermute | solution.py:31
  15.2 0.8 fusion.43
  16.0 0.8 fusion.33
  16.8 0.8 pad_maximum_fusion
  17.6 0.8 maximum_maximum_fusion
  18.4 0.7 fusion.31
  19.2 0.1 fusion.59
  19.3 0.1 add_multiply_fusion.1
  19.4 0.1 fusion.4
  19.4 0.1 fusion.62
  19.5 0.1 fusion.39
  19.6 0.1 broadcast_in_dim.12
  19.7 0.5 broadcast.260
  20.3 1.2 reduce.1
  21.5 21.2 %all_to_all.27 = bf16[16,2,1536]{2,1,0:T(2,128)(2,1)S(1)} all-to-all(bf16[16,2,1536]{2,1,0:T(2,128)(2,1)S(1)} %reshape.178), channel_id=1, replica_groups=mesh['tm'=4,'z'=16,'y'=4,'c'=2] {'z'}, dimensions={0} | all-to-all | bytes 196608 | tf_op jit(solution)/shard_map/all_to_all | solution.py:57
  42.7 0.1 reshape.179
  42.8 0.8 broadcast_in_dim.14
  43.6 7.0 %all-to-all-start.1 = ((bf16[4,16,3072]{2,1,0:T(8,128)(2,1)}), bf16[4,16,3072]{2,1,0:T(8,128)(2,1)S(1)}, u32[]{:S(2)}, u32[]{:S(2)}) async-start(bf16[4,16,3072]{2,1,0:T(8,128)(2,1)} %broadcast_in_dim.14), calls=%async_computation.1 | async-start | bytes 786432 | tf_op jit(solution)/shard_map/all_to_all | solution.py:58
  50.6 0.7 iota_compare_fusion
  51.3 0.8 eq.37
  52.1 0.1 lt.51
  52.2 4.9 %all-to-all-done.1 = bf16[4,16,3072]{2,1,0:T(8,128)(2,1)S(1)} async-done(((bf16[4,16,3072]{2,1,0:T(8,128)(2,1)}), bf16[4,16,3072]{2,1,0:T(8,128)(2,1)S(1)}, u32[]{:S(2)}, u32[]{:S(2)}) %all-to-all-start.1) | async-done | bytes 393248 | tf_op jit(solution)/shard_map/all_to_all | solution.py:58
  57.1 4.6 %all_gather.3 = bf16[128,3072]{1,0:T(8,128)(2,1)S(1)} all-gather(bf16[64,3072]{1,0:T(8,128)(2,1)S(1)} %bitcast.52), channel_id=1, replica_groups=mesh['tm'=4,'z'=16,'y'=4,'c'=2] {'c'}, dimensions={0}, use_global_device_ids=true | all-gather | bytes 1179648 | tf_op jit(solution)/shard_map/all_gather | solution.py:59
  61.7 0.3 convolution_convert_fusion
  62.0 0.2 reshape.167
  62.2 3.4 %convolution_bitcast_fusion.1 = f32[3,512]{1,0:T(4,128)S(1)} fusion(bf16[4,4,3,1024]{3,2,1,0:T(4,128)(2,1)S(1)} %reshape.167, bf16[4,4,128,1024]{3,2,1,0:T(8,128)(2,1)} %param.9), kind=kOutput, calls=%fused_computation.2 | convolution fusion | flops 12582912 | bytes 4298752 | tf_op jit(solution)/shard_map/bkin,bkcn->cbi/dot_general | solution.py:67
  65.5 8.6 %psum.7 = f32[3,512]{1,0:T(4,128)S(1)} all-reduce(f32[3,512]{1,0:T(4,128)S(1)} %convolution_bitcast_fusion.1), channel_id=1, replica_groups=mesh['tm'=4,'z'=16,'y'=4,'c'=2] {'tm'}, use_global_device_ids=true, to_apply=%region_0.1 | all-reduce | flops 1536 | bytes 12288 | tf_op jit(solution)/shard_map/psum | solution.py:68
  74.2 2.8 %convolution_bitcast_fusion = f32[4,4,3,1024]{3,2,1,0:T(4,128)S(1)} fusion(bf16[4,4,128,1024]{3,2,1,0:T(8,128)(2,1)} %param.9, f32[3,512]{1,0:T(4,128)S(1)} %subtract_multiply_fusion), kind=kOutput, calls=%fused_computation.1 | convolution fusion | flops 12584448 | bytes 4397056 | tf_op jit(solution)/shard_map/bkin,cbi->bkcn/dot_general | solution.py:72
  77.0 0.2 reshape.176
  77.2 0.9 fusion.14
  78.1 7.0 %all_to_all.28 = f32[2,64,3072]{2,1,0:T(8,128)S(1)} all-to-all(f32[2,64,3072]{2,1,0:T(8,128)S(1)} %fusion.14), channel_id=1, replica_groups=mesh['tm'=4,'z'=16,'y'=4,'c'=2] {'c'}, dimensions={0} | all-to-all | bytes 3145728 | tf_op jit(solution)/shard_map/all_to_all | solution.py:77
  85.1 0.2 reduce_sum.27
  85.3 14.4 %all_to_all.29 = f32[4,16,3072]{2,1,0:T(8,128)S(1)} all-to-all(f32[4,16,3072]{2,1,0:T(8,128)S(1)} %bitcast.51), channel_id=1, replica_groups=mesh['tm'=4,'z'=16,'y'=4,'c'=2] {'y'}, dimensions={0} | all-to-all | bytes 1572864 | tf_op jit(solution)/shard_map/all_to_all | solution.py:78
  99.8 0.7 reduce.2
  100.5 14.7 %all_to_all.30 = bf16[16,2,1536]{2,1,0:T(2,128)(2,1)S(1)} all-to-all(bf16[16,2,1536]{2,1,0:T(2,128)(2,1)S(1)} %reshape.180), channel_id=1, replica_groups=mesh['tm'=4,'z'=16,'y'=4,'c'=2] {'z'}, dimensions={0} | all-to-all | bytes 196608 | tf_op jit(solution)/shard_map/all_to_all | solution.py:79
  115.2 0.2 convert_reduce_fusion
  115.4 4.7 %collective-permute-start.3 = (f32[3,2,512]{2,1,0:T(2,128)S(1)}, f32[3,2,512]{2,1,0:T(2,128)S(1)}, u32[]{:S(2)}, u32[]{:S(2)}) collective-permute-start(f32[3,2,512]{2,1,0:T(2,128)S(1)} %reshape.172), channel_id=1, source_target_pairs={{0,1},{1,0},{2,3},{3,2},{4,5},{5,4},{6,7},{7,6},{8,9},{9,8},{10,11... | collective-permute-start | bytes 36872 | tf_op jit(solution)/shard_map/ppermute | solution.py:29
  120.2 2.1 %collective-permute-start.2 = (f32[3,2,512]{2,1,0:T(2,128)S(1)}, f32[3,2,512]{2,1,0:T(2,128)S(1)}, u32[]{:S(2)}, u32[]{:S(2)}) collective-permute-start(f32[3,2,512]{2,1,0:T(2,128)S(1)} %reshape.172), channel_id=1, source_target_pairs={{1,2},{3,4},{5,6},{7,8},{9,10},{11,12},{13,14},{15,16},{17,18},{19... | collective-permute-start | bytes 36872 | tf_op jit(solution)/shard_map/ppermute | solution.py:31
  122.3 2.9 %collective-permute-done.2 = f32[3,2,512]{2,1,0:T(2,128)S(1)} collective-permute-done((f32[3,2,512]{2,1,0:T(2,128)S(1)}, f32[3,2,512]{2,1,0:T(2,128)S(1)}, u32[]{:S(2)}, u32[]{:S(2)}) %collective-permute-start.2) | collective-permute-done | bytes 12320 | tf_op jit(solution)/shard_map/ppermute | solution.py:31
  125.2 0.1 fusion.60
  125.3 0.1 fusion.12
  125.4 0.1 fusion.61
  125.5 0.7 bitcast_add_fusion
  (25 shorter events, 0.4 us)
Async XLA Ops:
  1.4 12.3 %collective-permute-start.1 = (f32[4,2,512]{2,1,0:T(2,128)S(1)}, f32[4,2,512]{2,1,0:T(2,128)S(1)}, u32[]{:S(2)}, u32[]{:S(2)}) collective-permute-start(f32[4,2,512]{2,1,0:T(2,128)S(1)} %pad_maximum_fusion.3), channel_id=1, source_target_pairs={{0,1},{1,0},{2,3},{3,2},{4,5},{5,4},{6,7},{7,6},{8,9},{9,8},{10,11... | collective-permute-start | bytes 49160 | tf_op jit(solution)/shard_map/ppermute | solution.py:29
  10.2 5.1 %collective-permute-start = (f32[4,2,512]{2,1,0:T(2,128)S(1)}, f32[4,2,512]{2,1,0:T(2,128)S(1)}, u32[]{:S(2)}, u32[]{:S(2)}) collective-permute-start(f32[4,2,512]{2,1,0:T(2,128)S(1)} %pad_maximum_fusion.3), channel_id=1, source_target_pairs={{1,2},{3,4},{5,6},{7,8},{9,10},{11,12},{13,14},{15,16},{17,18},{19... | collective-permute-start | bytes 49160 | tf_op jit(solution)/shard_map/ppermute | solution.py:31
  43.6 13.5 %all-to-all-start.1 = ((bf16[4,16,3072]{2,1,0:T(8,128)(2,1)}), bf16[4,16,3072]{2,1,0:T(8,128)(2,1)S(1)}, u32[]{:S(2)}, u32[]{:S(2)}) async-start(bf16[4,16,3072]{2,1,0:T(8,128)(2,1)} %broadcast_in_dim.14), calls=%async_computation.1 | async-start | bytes 786432 | tf_op jit(solution)/shard_map/all_to_all | solution.py:58
  57.1 17.0 %copy-start.2 = (f32[3,512]{1,0:T(4,128)S(1)}, f32[3,512]{1,0:T(4,128)}, u32[]{:S(2)}) copy-start(f32[3,512]{1,0:T(4,128)} %param.13) | copy-start | bytes 18436
  57.1 17.0 %copy-start.3 = (f32[3,512]{1,0:T(4,128)S(1)}, f32[3,512]{1,0:T(4,128)}, u32[]{:S(2)}) copy-start(f32[3,512]{1,0:T(4,128)} %param.12) | copy-start | bytes 18436
  74.1 10.9 %copy-start.1 = (f32[3,512]{1,0:T(4,128)}, f32[3,512]{1,0:T(4,128)S(1)}, u32[]{:S(2)}) copy-start(f32[3,512]{1,0:T(4,128)S(1)} %subtract_multiply_fusion) | copy-start | bytes 18436
  78.1 47.4 %copy-start = (f32[3,1,2,512]{3,2,1,0:T(2,128)S(1)}, f32[3,1,2,512]{3,2,1,0:T(2,128)}, u32[]{:S(2)}) copy-start(f32[3,1,2,512]{3,2,1,0:T(2,128)} %param.7) | copy-start | bytes 36868
  115.4 6.8 %collective-permute-start.3 = (f32[3,2,512]{2,1,0:T(2,128)S(1)}, f32[3,2,512]{2,1,0:T(2,128)S(1)}, u32[]{:S(2)}, u32[]{:S(2)}) collective-permute-start(f32[3,2,512]{2,1,0:T(2,128)S(1)} %reshape.172), channel_id=1, source_target_pairs={{0,1},{1,0},{2,3},{3,2},{4,5},{5,4},{6,7},{7,6},{8,9},{9,8},{10,11... | collective-permute-start | bytes 36872 | tf_op jit(solution)/shard_map/ppermute | solution.py:29
  120.2 5.0 %collective-permute-start.2 = (f32[3,2,512]{2,1,0:T(2,128)S(1)}, f32[3,2,512]{2,1,0:T(2,128)S(1)}, u32[]{:S(2)}, u32[]{:S(2)}) collective-permute-start(f32[3,2,512]{2,1,0:T(2,128)S(1)} %reshape.172), channel_id=1, source_target_pairs={{1,2},{3,4},{5,6},{7,8},{9,10},{11,12},{13,14},{15,16},{17,18},{19... | collective-permute-start | bytes 36872 | tf_op jit(solution)/shard_map/ppermute | solution.py:31

commit v2 on v1

v2 whole, which is shorter than its diff:
```python
import jax
import jax.numpy as jnp
from jax import lax
from jax.experimental import pallas as pl
from jax.experimental.pallas import tpu as pltpu
from jax.sharding import Mesh, PartitionSpec as P

ZN, YN, CN = 16, 4, 2
OBS = ("z", "y", "c")
TILES = ZN * YN * CN
TRACERS, ROWS, WIDTH = 3, 2, 512
LANES = 128
CHUNKS = WIDTH // LANES
SUB = ROWS * CHUNKS
CELLS = ROWS * WIDTH
BLOCKS, REFS, SIGHTS = 4, 4, 128
ENTRIES = BLOCKS * REFS
PAY = TRACERS * LANES
F32, BF16 = jnp.float32, jnp.bfloat16


VMEM = pl.BlockSpec(memory_space=pltpu.VMEM)
SMEM = pl.BlockSpec(memory_space=pltpu.SMEM)


def call(body, out, ins, scratch=(), name=None):
    return pl.pallas_call(
        body,
        out_shape=out,
        in_specs=ins,
        out_specs=jax.tree.map(lambda _: VMEM, out),
        scratch_shapes=list(scratch),
        name=name,
    )


def shape(*dims, dtype=F32):
    return jax.ShapeDtypeStruct(dims, dtype)


def block(value, t):
    return value[:, t * LANES : (t + 1) * LANES]


def pack_kernel(control, diffusivity, lists, counts, out):
    def rows(read):
        return jnp.concatenate([read(s // CHUNKS, s % CHUNKS * LANES) for s in range(SUB)], axis=0)

    for t in range(TRACERS):
        out[:, t * LANES : (t + 1) * LANES] = rows(lambda r, at, t=t: control[t, 0, r : r + 1, at : at + LANES])
    out[:, TRACERS * LANES : 4 * LANES] = rows(lambda r, at: diffusivity[r : r + 1, at : at + LANES])
    lane = lax.broadcasted_iota(jnp.int32, (1, LANES), 1)
    ids = jnp.full((1, LANES), -1, jnp.int32)
    for b in range(BLOCKS):
        for k in range(REFS):
            ids = jnp.where((lane == b * REFS + k) & (k < counts[b]), lists[b, k], ids)
    out[:, 4 * LANES :] = jnp.broadcast_to(ids.astype(F32), (SUB, LANES))


def around(both, other, core, t):
    own = both[core, :, t * LANES : (t + 1) * LANES]
    mate = both[1 - core, :, t * LANES : (t + 1) * LANES]
    far = other[:, t * LANES : (t + 1) * LANES]
    first = core == 0
    return jnp.concatenate([jnp.where(first, far, mate), own, jnp.where(first, mate, far)], axis=0)


class Sweeps:
    def __init__(self, conduct, here):
        whole = conduct.shape
        self.rows = whole[0]
        sub = lax.broadcasted_iota(jnp.int32, whole, 0)
        self.lane = lax.broadcasted_iota(jnp.int32, whole, 1)
        self.chunk = sub % CHUNKS
        grid_row = sub // CHUNKS - ROWS
        self.inside = ((grid_row >= 0) | (here > 0)) & ((grid_row < ROWS) | (here < TILES - 1))
        self.factors = [0.0625 * (conduct + nb) for nb in self.neighbours(conduct)]

    def neighbours(self, v):
        n = self.rows
        up = pltpu.roll(v, CHUNKS, 0)
        down = pltpu.roll(v, n - CHUNKS, 0)
        left = pltpu.roll(v, 1, 1)
        left = jnp.where(self.lane == 0, jnp.where(self.chunk == 0, 0.0, pltpu.roll(left, 1, 0)), left)
        right = pltpu.roll(v, LANES - 1, 1)
        right = jnp.where(
            self.lane == LANES - 1, jnp.where(self.chunk == CHUNKS - 1, 0.0, pltpu.roll(right, n - 1, 0)), right
        )
        return up, down, left, right

    def once(self, v):
        total = v
        for factor, nb in zip(self.factors, self.neighbours(v)):
            total = total + factor * (nb - v)
        return total

    def twice(self, v):
        return self.once(jnp.where(self.inside, self.once(v), 0.0))[SUB : 2 * SUB]


def flux_kernel(both, other, out):
    core, here = lax.axis_index("c"), lax.axis_index(OBS)
    sweeps = Sweeps(around(both, other, core, TRACERS), here)
    half = jnp.concatenate([sweeps.twice(around(both, other, core, t)) for t in range(TRACERS)], axis=1).astype(BF16)
    for z in range(ZN):
        out[z] = half


def diagonal():
    row = lax.broadcasted_iota(jnp.int32, (SUB, CELLS), 0)
    lane = lax.broadcasted_iota(jnp.int32, (SUB, CELLS), 1)
    return row == lane // LANES


def predict_kernel(panels, footprints, lists, counts, out):
    match = diagonal()
    for b in range(BLOCKS):
        total = None
        for k in range(REFS):
            tile = lists[b, k]
            slot = tile % CN * (YN * ZN) + tile // CN % YN * ZN + tile // (CN * YN)
            panel = panels[slot].astype(F32)
            take = match & (k < counts[b])
            left = jnp.concatenate(
                [jnp.where(take, jnp.concatenate([block(panel, t)] * SUB, axis=1), 0.0) for t in range(TRACERS)], axis=0
            ).astype(BF16)
            term = lax.dot_general(left, footprints[b, k], (((1,), (1,)), ((), ())), preferred_element_type=F32)
            total = term if total is None else total + term
        for t in range(TRACERS):
            out[t : t + 1, b * SIGHTS : (b + 1) * SIGHTS] = jnp.sum(
                total[t * SUB : (t + 1) * SUB], axis=0, keepdims=True
            )


def adjoint_kernel(predicted, measured, weight, footprints, residual, out):
    misfit = (predicted[...] - measured[...]) * weight[...]
    residual[...] = misfit
    row = lax.broadcasted_iota(jnp.int32, (SUB, LANES), 0)
    for b in range(BLOCKS):
        own = misfit[:, b * SIGHTS : (b + 1) * SIGHTS]
        left = jnp.concatenate(
            [jnp.broadcast_to(own[t : t + 1], (SUB, SIGHTS)) for t in range(TRACERS)], axis=0
        ).astype(BF16)
        for k in range(REFS):
            full = jnp.dot(left, footprints[b, k], preferred_element_type=F32)
            for t in range(TRACERS):
                mine = full[t * SUB : (t + 1) * SUB]
                value = block(mine, 0)
                for q in range(1, SUB):
                    value = jnp.where(row == q, block(mine, q), value)
                out[b * REFS + k, :, t * LANES : (t + 1) * LANES] = value


def place_kernel(entries, ids, out):
    core = lax.axis_index("c")
    out[...] = jnp.zeros_like(out)
    for c in range(CN):
        for e in range(ENTRIES):
            tile = ids[c, e]

            @pl.when((tile >= 0) & (tile % CN == core))
            def _(tile=tile, at=c * ENTRIES + e):
                y, z = tile // CN % YN, tile // (CN * YN)
                out[y, z] = out[y, z] + entries[at]


def final_kernel(total_both, total_other, both, other, out):
    core, here = lax.axis_index("c"), lax.axis_index(OBS)
    sweeps = Sweeps(around(both, other, core, TRACERS), here)
    for t in range(TRACERS):
        value = both[core, :, t * LANES : (t + 1) * LANES] + sweeps.twice(around(total_both, total_other, core, t))
        for s in range(SUB):
            r, at = s // CHUNKS, s % CHUNKS * LANES
            out[t, 0, r : r + 1, at : at + LANES] = value[s : s + 1]


def neighbours(own):
    pairs = [(i, i + 1) for i in range(1, TILES - 1, 2)]
    other = lax.ppermute(own, OBS, pairs + [(b, a) for a, b in pairs])
    return lax.all_gather(own, "c"), other


def shards(control, diffusivity, footprints, tile_lists, tile_counts, measured, weight):
    own = call(pack_kernel, shape(SUB, 5 * LANES), [VMEM, VMEM, SMEM, SMEM], name="pack")(
        control, diffusivity, tile_lists, tile_counts
    )
    both, other = neighbours(own)
    ids = both[:, 0, 4 * LANES : 4 * LANES + ENTRIES].astype(jnp.int32)
    flux = call(flux_kernel, shape(ZN, SUB, PAY, dtype=BF16), [VMEM] * 2, name="flux")(both, other)

    by_z = lax.all_to_all(flux, "z", 0, 0, tiled=True)
    by_y = lax.all_to_all(jnp.broadcast_to(by_z[None], (YN,) + by_z.shape), "y", 0, 0, tiled=True)
    panels = lax.all_gather(by_y.reshape(YN * ZN, SUB, PAY), "c", axis=0, tiled=True)

    part = call(predict_kernel, shape(TRACERS, BLOCKS * SIGHTS), [VMEM, VMEM, SMEM, SMEM], name="predict")(
        panels, footprints, tile_lists, tile_counts
    )
    predicted = lax.psum(part, "tm")
    residual, entries = call(
        adjoint_kernel, (shape(TRACERS, BLOCKS * SIGHTS), shape(ENTRIES, SUB, PAY)), [VMEM] * 4, name="adjoint"
    )(predicted, measured, weight, footprints)

    chip = lax.all_gather(entries, "c", axis=0, tiled=True)
    dense = call(place_kernel, shape(YN, ZN, SUB, PAY), [VMEM, SMEM], name="place")(chip, ids)
    over_y = lax.all_to_all(dense, "y", 0, 0, tiled=True).sum(axis=0)
    total = lax.all_to_all(over_y, "z", 0, 0, tiled=True).sum(axis=0)

    total_both, total_other = neighbours(total)
    gradient = call(final_kernel, shape(*control.shape), [VMEM] * 4, name="final")(total_both, total_other, both, other)
    return gradient, residual


def solution(mesh):
    fine = Mesh(mesh.devices.reshape(mesh.shape["tm"], ZN, YN, CN), ("tm",) + OBS)
    placed = (
        P(None, "tm", OBS, None),
        P(OBS, None),
        P(OBS, None, None, "tm"),
        P(OBS, None),
        P(OBS),
        P(None, OBS),
        P(None, OBS),
    )
    return jax.shard_map(
        shards,
        mesh=fine,
        in_specs=placed,
        out_specs=(P(None, "tm", OBS, None), P(None, OBS)),
        check_vma=False,
    )
```

time: 127 us -> 128 us (level)
  blocking collectives: 70.5 us -> 86.3 us
  Pallas kernels: 0 us -> 15.3 us
  starting transfers between devices: 24.5 us -> 15.6 us
  other arithmetic: 9.48 us -> 1.34 us
  matrix products: 7.36 us -> 0 us
  waiting for transfers between devices: 9.33 us -> 4.95 us
  local copies, waits for them, and re-layouts: 4.1 us -> 1.99 us
    all_gather x1 -> x4, blocking collectives: 4.63 us -> 20.3 us  [the longest x2 7.9 us: neighbours(): return (lax.all_gather(own, 'c'), other)]
    pallas_call x0 -> x6, Pallas kernels: none -> 15.3 us  [the longest x1 4.54 us: shards(): call(predict_kernel, shape(TRACERS, BLOCKS * SIGHTS), [VMEM, VMEM, SMEM,...]
    dot_general x4 -> x0, matrix products: 7.36 us -> none  [the longest x1 3.38 us: shards(): jnp.einsum('bkin,bkcn->cbi', footprints, chosen, preferred_element_type=j...]
    ppermute x4 -> x2, starting transfers between devices: 17.5 us -> 11.8 us  [neighbours(): other = lax.ppermute(own, OBS, pairs + [(b, a) for a, b in pairs])]
    ppermute x4 -> x2, waiting for transfers between devices: 4.42 us -> 0.01 us  [neighbours(): other = lax.ppermute(own, OBS, pairs + [(b, a) for a, b in pairs])]
    mul x8 -> x0, other arithmetic: 3.33 us -> none  [the longest x2 1.6 us: sweep(): 0.0625 * (conduct_mid + conduct[:-2]) * (fields[:, :-2] - middle)]
    all_to_all x1, starting transfers between devices: 6.99 us -> 3.79 us  [shards(): lax.all_to_all(jnp.broadcast_to(by_z[None], (YN,) + by_z.shape), 'y', 0,...]
    concatenate x4 -> x0, other arithmetic: 2.34 us -> none  [the longest x3 1.6 us: with_neighbours(): return jnp.concatenate([before, own, after], axis=1)]
  transfers between devices with their start and end apart: 5 -> 3, of which waited for: 3 -> 1; matrix products, arithmetic and copies ran while one was open for 3% -> 1% of each run, Pallas kernels for 0% -> 0%
where the time goes in v2:
time: 128 us; the launch traced here: 126 us
  blocking collectives  86.3 us (67%)
  starting transfers between devices  15.6 us (12%)
  Pallas kernels  15.3 us (12%)
  waiting for transfers between devices  4.95 us (4%)
  local copies, waits for them, and re-layouts  1.99 us (2%)
  other arithmetic  1.34 us (1%)
    all_to_all x1, blocking collectives, shards(): by_z = lax.all_to_all(flux, 'z', 0, 0, tiled=True)  25.1 us
    all_to_all x1, blocking collectives, shards(): total = lax.all_to_all(over_y, 'z', 0, 0, tiled=True).sum(axis=0)  16.1 us
    all_to_all x1, blocking collectives, shards(): over_y = lax.all_to_all(dense, 'y', 0, 0, tiled=True).sum(axis=0)  15.5 us
    ppermute x2, starting transfers between devices, neighbours(): other = lax.ppermute(own, OBS, pairs + [(b, a) for a, b in pairs])  11.8 us
    psum x1, blocking collectives, shards(): predicted = lax.psum(part, 'tm')  9.26 us
    all_gather x2, blocking collectives, neighbours(): return (lax.all_gather(own, 'c'), other)  7.9 us
    all_gather x1, blocking collectives, shards(): chip = lax.all_gather(entries, 'c', axis=0, tiled=True)  6.64 us
    all_gather x1, blocking collectives, shards(): lax.all_gather(by_y.reshape(YN * ZN, SUB, PAY), 'c', axis=0, tiled=True)  5.75 us
  transfers between devices with their start and end apart: 3, of which 1 were waited for; matrix products, arithmetic and copies ran while one was open for 1% of the time, Pallas kernels for 0%

profile of v2, /device:TPU:1, one launch (start us, length us, event | category | flops | bytes accessed | tf_op | source)
XLA Modules:
  0.0 126.1 jit_solution(3803997005446729162)
XLA Ops:
  0.6 1.5 %pack.1 = f32[8,640]{1,0:T(8,128)} custom-call(f32[3,1,2,512]{3,2,1,0:T(2,128)} %control.1, f32[2,512]{1,0:T(2,128)} %diffusivity.1, s32[4,4]{1,0:T(4,128)} %lists.3, s32[4]{0:T(128)} %counts.3), custom_call_target="tpu_custom_call" | custom-call | tf_op jit(solution)/shard_map/pack/pallas_call | solution.py:184
  2.1 4.6 %collective-permute-start = (f32[8,640]{1,0:T(8,128)}, f32[8,640]{1,0:T(8,128)S(1)}, u32[]{:S(2)}, u32[]{:S(2)}) collective-permute-start(f32[8,640]{1,0:T(8,128)} %pack.1), channel_id=1, source_target_pairs={{1,2},{3,4},{5,6},{7,8},{9,10},{11,12},{13,14},{15,16},{17,18},{19... | collective-permute-start | bytes 61448 | tf_op jit(solution)/shard_map/ppermute | solution.py:179
  6.7 5.9 %all-gather = f32[16,640]{1,0:T(8,128)} all-gather(f32[8,640]{1,0:T(8,128)} %pack.1), channel_id=2, replica_groups=mesh['tm'=4,'z'=16,'y'=4,'c'=2] {'c'}, dimensions={0}, use_global_device_ids=true | all-gather | bytes 61440 | tf_op jit(solution)/shard_map/all_gather | solution.py:180
  12.6 0.0 collective-permute-done.other
  12.6 0.0 copy-start
  12.6 0.6 copy-done
  13.2 1.6 %flux.1 = bf16[16,8,384]{2,1,0:T(8,128)(2,1)} custom-call(f32[2,8,640]{2,1,0:T(8,128)} %bitcast.5, f32[8,640]{1,0:T(8,128)} %copy-done), custom_call_target="tpu_custom_call" | custom-call | tf_op jit(solution)/shard_map/flux/pallas_call | solution.py:189
  14.8 25.1 %all_to_all.20 = bf16[16,8,384]{2,1,0:T(8,128)(2,1)S(1)} all-to-all(bf16[16,8,384]{2,1,0:T(8,128)(2,1)} %flux.1), channel_id=1, replica_groups=mesh['tm'=4,'z'=16,'y'=4,'c'=2] {'z'}, dimensions={0} | all-to-all | bytes 196608 | tf_op jit(solution)/shard_map/all_to_all | solution.py:191
  40.0 0.8 broadcast_in_dim.2
  40.7 3.8 %all-to-all-start.1 = ((bf16[4,16,8,384]{3,2,1,0:T(8,128)(2,1)}), bf16[4,16,8,384]{3,2,1,0:T(8,128)(2,1)S(1)}, u32[]{:S(2)}, u32[]{:S(2)}) async-start(bf16[4,16,8,384]{3,2,1,0:T(8,128)(2,1)} %broadcast_in_dim.2), calls=%async_computation.1 | async-start | bytes 786432 | tf_op jit(solution)/shard_map/all_to_all | solution.py:192
  44.5 1.3 %slice_convert_fusion = s32[2,1,16]{2,1,0:T(1,128)} fusion(f32[2,8,640]{2,1,0:T(8,128)} %bitcast.6), kind=kLoop, calls=%fused_computation | loop fusion | flops 32 | bytes 256 | tf_op jit(solution)/shard_map/convert_element_type | solution.py:188
  45.8 4.9 %all-to-all-done.1 = bf16[4,16,8,384]{3,2,1,0:T(8,128)(2,1)S(1)} async-done(((bf16[4,16,8,384]{3,2,1,0:T(8,128)(2,1)}), bf16[4,16,8,384]{3,2,1,0:T(8,128)(2,1)S(1)}, u32[]{:S(2)}, u32[]{:S(2)}) %all-to-all-start.1) | async-done | bytes 393248 | tf_op jit(solution)/shard_map/all_to_all | solution.py:192
  50.8 5.7 %all_gather.20.panels = bf16[128,8,384]{2,1,0:T(8,128)(2,1)} all-gather(bf16[64,8,384]{2,1,0:T(8,128)(2,1)S(1)} %bitcast.4), channel_id=1, replica_groups=mesh['tm'=4,'z'=16,'y'=4,'c'=2] {'c'}, dimensions={0}, use_global_device_ids=true | all-gather | bytes 1179648 | tf_op jit(solution)/shard_map/all_gather | solution.py:193
  56.5 4.5 %predict.1 = f32[3,512]{1,0:T(4,128)} custom-call(bf16[128,8,384]{2,1,0:T(8,128)(2,1)} %all_gather.20.panels, bf16[4,4,128,1024]{3,2,1,0:T(8,128)(2,1)} %footprints.3, s32[4,4]{1,0:T(4,128)} %lists.3, s32[4]{0:T(128)} %counts.3), custom_call_target="tpu_custom_call" | custom-call | tf_op jit(solution)/shard_map/predict/pallas_call | solution.py:195
  61.1 9.3 %psum.7.predicted = f32[3,512]{1,0:T(4,128)} all-reduce(f32[3,512]{1,0:T(4,128)} %predict.1), channel_id=1, replica_groups=mesh['tm'=4,'z'=16,'y'=4,'c'=2] {'tm'}, use_global_device_ids=true, to_apply=%region_0.0 | all-reduce | flops 1536 | bytes 12288 | tf_op jit(solution)/shard_map/psum | solution.py:198
  70.3 3.6 %adjoint.1 = (f32[3,512]{1,0:T(4,128)}, f32[16,8,384]{2,1,0:T(8,128)}) custom-call(f32[3,512]{1,0:T(4,128)} %psum.7.predicted, f32[3,512]{1,0:T(4,128)} %measured.1, f32[3,512]{1,0:T(4,128)} %weight.1, bf16[4,4,128,1024]{3,2,1,0:T(8,128)(2,1)} %footprints.3), custom_call_target="tpu_custom_call" | custom-call | tf_op jit(solution)/shard_map/adjoint/pallas_call | solution.py:199
  73.9 6.6 %all_gather.21.entries = f32[32,8,384]{2,1,0:T(8,128)} all-gather(f32[16,8,384]{2,1,0:T(8,128)} %get-tuple-element.4), channel_id=1, replica_groups=mesh['tm'=4,'z'=16,'y'=4,'c'=2] {'c'}, dimensions={0}, use_global_device_ids=true | all-gather | bytes 589824 | tf_op jit(solution)/shard_map/all_gather | solution.py:203
  80.6 2.5 %place.1 = f32[4,16,8,384]{3,2,1,0:T(8,128)} custom-call(f32[32,8,384]{2,1,0:T(8,128)} %all_gather.21.entries, s32[2,16]{1,0:T(2,128)} %bitcast.9), custom_call_target="tpu_custom_call" | custom-call | tf_op jit(solution)/shard_map/place/pallas_call | solution.py:204
  83.0 15.5 %all_to_all.21 = f32[4,16,8,384]{3,2,1,0:T(8,128)S(1)} all-to-all(f32[4,16,8,384]{3,2,1,0:T(8,128)} %place.1), channel_id=1, replica_groups=mesh['tm'=4,'z'=16,'y'=4,'c'=2] {'y'}, dimensions={0} | all-to-all | bytes 1572864 | tf_op jit(solution)/shard_map/all_to_all | solution.py:205
  98.6 16.1 %all_to_all.22 = f32[16,8,384]{2,1,0:T(8,128)S(1)} all-to-all(f32[16,8,384]{2,1,0:T(8,128)S(1)} %reduce_sum.18), channel_id=1, replica_groups=mesh['tm'=4,'z'=16,'y'=4,'c'=2] {'z'}, dimensions={0} | all-to-all | bytes 393216 | tf_op jit(solution)/shard_map/all_to_all | solution.py:206
  114.7 7.2 %collective-permute-start.1 = (f32[8,384]{1,0:T(8,128)S(1)}, f32[8,384]{1,0:T(8,128)S(1)}, u32[]{:S(2)}, u32[]{:S(2)}) collective-permute-start(f32[8,384]{1,0:T(8,128)S(1)} %reduce_sum.19), channel_id=1, source_target_pairs={{1,2},{3,4},{5,6},{7,8},{9,10},{11,12},{13,14},{15,16},{17,18},{19... | collective-permute-start | bytes 36872 | tf_op jit(solution)/shard_map/ppermute | solution.py:179
  121.9 2.0 %all-gather.1 = f32[16,384]{1,0:T(8,128)} all-gather(f32[8,384]{1,0:T(8,128)S(1)} %reduce_sum.19), channel_id=3, replica_groups=mesh['tm'=4,'z'=16,'y'=4,'c'=2] {'c'}, dimensions={0}, use_global_device_ids=true | all-gather | bytes 36864 | tf_op jit(solution)/shard_map/all_gather | solution.py:180
  123.9 0.0 collective-permute-done.1.total_other
  123.9 0.0 copy-start.1
  123.9 0.6 copy-done.1
  124.5 1.6 %final.1 = f32[3,1,2,512]{3,2,1,0:T(2,128)} custom-call(f32[2,8,384]{2,1,0:T(8,128)} %bitcast.8, f32[8,384]{1,0:T(8,128)} %copy-done.1, f32[2,8,640]{2,1,0:T(8,128)} %bitcast.7, f32[8,640]{1,0:T(8,128)} %copy-done), custom_call_target="tpu_custom_call" | custom-call | tf_op jit(solution)/shard_map/final/pallas_call | solution.py:209
  (2 shorter events, 0.1 us)
Async XLA Ops:
  2.1 10.5 %collective-permute-start = (f32[8,640]{1,0:T(8,128)}, f32[8,640]{1,0:T(8,128)S(1)}, u32[]{:S(2)}, u32[]{:S(2)}) collective-permute-start(f32[8,640]{1,0:T(8,128)} %pack.1), channel_id=1, source_target_pairs={{1,2},{3,4},{5,6},{7,8},{9,10},{11,12},{13,14},{15,16},{17,18},{19... | collective-permute-start | bytes 61448 | tf_op jit(solution)/shard_map/ppermute | solution.py:179
  12.6 0.6 copy-start
  40.7 10.0 %all-to-all-start.1 = ((bf16[4,16,8,384]{3,2,1,0:T(8,128)(2,1)}), bf16[4,16,8,384]{3,2,1,0:T(8,128)(2,1)S(1)}, u32[]{:S(2)}, u32[]{:S(2)}) async-start(bf16[4,16,8,384]{3,2,1,0:T(8,128)(2,1)} %broadcast_in_dim.2), calls=%async_computation.1 | async-start | bytes 786432 | tf_op jit(solution)/shard_map/all_to_all | solution.py:192
  114.7 9.2 %collective-permute-start.1 = (f32[8,384]{1,0:T(8,128)S(1)}, f32[8,384]{1,0:T(8,128)S(1)}, u32[]{:S(2)}, u32[]{:S(2)}) collective-permute-start(f32[8,384]{1,0:T(8,128)S(1)} %reduce_sum.19), channel_id=1, source_target_pairs={{1,2},{3,4},{5,6},{7,8},{9,10},{11,12},{13,14},{15,16},{17,18},{19... | collective-permute-start | bytes 36872 | tf_op jit(solution)/shard_map/ppermute | solution.py:179
  123.9 0.6 copy-start.1

commit v3 on v2

v3 whole, which is shorter than its diff:
```python
import jax
import jax.numpy as jnp
from jax import lax
from jax.experimental import pallas as pl
from jax.experimental.pallas import tpu as pltpu
from jax.sharding import Mesh, PartitionSpec as P

ZN, YN, CN = 16, 4, 2
OBS = ("z", "y", "c")
TILES = ZN * YN * CN
TRACERS, ROWS, WIDTH = 3, 2, 512
LANES = 128
CHUNKS = WIDTH // LANES
SUB = ROWS * CHUNKS
CELLS = ROWS * WIDTH
BLOCKS, REFS, SIGHTS = 4, 4, 128
ENTRIES = BLOCKS * REFS
PAY = TRACERS * LANES
F32, BF16 = jnp.float32, jnp.bfloat16


VMEM = pl.BlockSpec(memory_space=pltpu.VMEM)
SMEM = pl.BlockSpec(memory_space=pltpu.SMEM)
MIB = 1 << 20


def call(body, out, ins, mib, scratch=(), name=None):
    return pl.pallas_call(
        body,
        out_shape=out,
        in_specs=ins,
        out_specs=jax.tree.map(lambda _: VMEM, out),
        scratch_shapes=list(scratch),
        compiler_params=pltpu.CompilerParams(vmem_limit_bytes=mib * MIB),
        name=name,
    )


def shape(*dims, dtype=F32):
    return jax.ShapeDtypeStruct(dims, dtype)


def block(value, t):
    return value[:, t * LANES : (t + 1) * LANES]


IDS, SEEN = 4, 5
PACK = 8 * LANES


def seen_row(which, t, b):
    at = (which * TRACERS + t) * BLOCKS + b
    return at % SUB, (SEEN + at // SUB) * LANES


def pack_kernel(control, diffusivity, measured, weight, lists, counts, out):
    def rows(read):
        return jnp.concatenate([read(s // CHUNKS, s % CHUNKS * LANES) for s in range(SUB)], axis=0)

    for t in range(TRACERS):
        out[:, t * LANES : (t + 1) * LANES] = rows(lambda r, at, t=t: control[t, 0, r : r + 1, at : at + LANES])
    out[:, TRACERS * LANES : 4 * LANES] = rows(lambda r, at: diffusivity[r : r + 1, at : at + LANES])
    lane = lax.broadcasted_iota(jnp.int32, (1, LANES), 1)
    ids = jnp.full((1, LANES), -1, jnp.int32)
    for b in range(BLOCKS):
        for k in range(REFS):
            ids = jnp.where((lane == b * REFS + k) & (k < counts[b]), lists[b, k], ids)
    out[:, IDS * LANES : SEEN * LANES] = jnp.broadcast_to(ids.astype(F32), (SUB, LANES))
    for which, ref in enumerate((measured, weight)):
        for t in range(TRACERS):
            for b in range(BLOCKS):
                r, at = seen_row(which, t, b)
                out[r : r + 1, at : at + LANES] = ref[t : t + 1, b * SIGHTS : (b + 1) * SIGHTS]


def around(both, other, core, t):
    own = both[core, :, t * LANES : (t + 1) * LANES]
    mate = both[1 - core, :, t * LANES : (t + 1) * LANES]
    far = other[:, t * LANES : (t + 1) * LANES]
    first = core == 0
    return jnp.concatenate([jnp.where(first, far, mate), own, jnp.where(first, mate, far)], axis=0)


class Sweeps:
    def __init__(self, conduct, here):
        whole = conduct.shape
        self.rows = whole[0]
        sub = lax.broadcasted_iota(jnp.int32, whole, 0)
        self.lane = lax.broadcasted_iota(jnp.int32, whole, 1)
        self.chunk = sub % CHUNKS
        grid_row = sub // CHUNKS - ROWS
        self.inside = ((grid_row >= 0) | (here > 0)) & ((grid_row < ROWS) | (here < TILES - 1))
        self.factors = [0.0625 * (conduct + nb) for nb in self.neighbours(conduct)]

    def neighbours(self, v):
        n = self.rows
        up = pltpu.roll(v, CHUNKS, 0)
        down = pltpu.roll(v, n - CHUNKS, 0)
        left = pltpu.roll(v, 1, 1)
        left = jnp.where(self.lane == 0, jnp.where(self.chunk == 0, 0.0, pltpu.roll(left, 1, 0)), left)
        right = pltpu.roll(v, LANES - 1, 1)
        right = jnp.where(
            self.lane == LANES - 1, jnp.where(self.chunk == CHUNKS - 1, 0.0, pltpu.roll(right, n - 1, 0)), right
        )
        return up, down, left, right

    def once(self, v):
        total = v
        for factor, nb in zip(self.factors, self.neighbours(v)):
            total = total + factor * (nb - v)
        return total

    def twice(self, v):
        return self.once(jnp.where(self.inside, self.once(v), 0.0))[SUB : 2 * SUB]


def flux_kernel(both, other, out):
    core, here = lax.axis_index("c"), lax.axis_index(OBS)
    sweeps = Sweeps(around(both, other, core, TRACERS), here)
    half = jnp.concatenate([sweeps.twice(around(both, other, core, t)) for t in range(TRACERS)], axis=1).astype(BF16)
    for z in range(ZN):
        out[z] = half


def diagonal():
    row = lax.broadcasted_iota(jnp.int32, (SUB, CELLS), 0)
    lane = lax.broadcasted_iota(jnp.int32, (SUB, CELLS), 1)
    return row == lane // LANES


def predict_kernel(panels, own, mate, ids, out, total):
    core = lax.axis_index("c")
    match = diagonal()
    for source, c in ((own, core), (mate, 1 - core)):
        for b in range(BLOCKS):
            total[...] = jnp.zeros_like(total)
            for k in range(REFS):
                tile = ids[c, b * REFS + k]

                @pl.when((tile >= 0) & (tile % CN == core))
                def _(tile=tile, source=source, b=b, k=k):
                    panel = panels[tile // CN % YN, tile // (CN * YN)].astype(F32)
                    left = jnp.concatenate(
                        [
                            jnp.where(match, jnp.concatenate([block(panel, t)] * SUB, axis=1), 0.0)
                            for t in range(TRACERS)
                        ],
                        axis=0,
                    ).astype(BF16)
                    total[...] += lax.dot_general(
                        left, source[b, k], (((1,), (1,)), ((), ())), preferred_element_type=F32
                    )

            for t in range(TRACERS):
                row = jnp.sum(total[t * SUB : (t + 1) * SUB], axis=0, keepdims=True)
                out[0, pl.ds(t * SUB + c * BLOCKS + b, 1), :] = row
    whole = out[0]
    for peer in range(1, out.shape[0]):
        out[peer] = whole


def adjoint_kernel(parts, both, own, mate, ids, residual, out, misfit):
    core = lax.axis_index("c")
    whole = parts[0]
    for peer in range(1, parts.shape[0]):
        whole = whole + parts[peer]

    def seen(which):
        rows = []
        for t in range(TRACERS):
            for c in range(CN):
                for b in range(BLOCKS):
                    r, at = seen_row(which, t, b)
                    rows.append(both[c, r : r + 1, at : at + LANES])
        return jnp.concatenate(rows, axis=0)

    misfit[...] = (whole - seen(0)) * seen(1)
    for t in range(TRACERS):
        for b in range(BLOCKS):
            residual[t : t + 1, b * SIGHTS : (b + 1) * SIGHTS] = misfit[pl.ds(t * SUB + core * BLOCKS + b, 1), :]
    out[...] = jnp.zeros_like(out)
    row = lax.broadcasted_iota(jnp.int32, (SUB, LANES), 0)
    for source, c in ((own, core), (mate, 1 - core)):
        for b in range(BLOCKS):
            left = jnp.concatenate(
                [
                    jnp.broadcast_to(misfit[pl.ds(t * SUB + c * BLOCKS + b, 1), :], (SUB, SIGHTS))
                    for t in range(TRACERS)
                ],
                axis=0,
            ).astype(BF16)
            for k in range(REFS):
                tile = ids[c, b * REFS + k]

                @pl.when((tile >= 0) & (tile % CN == core))
                def _(tile=tile, source=source, b=b, k=k, left=left):
                    full = jnp.dot(left, source[b, k], preferred_element_type=F32)
                    values = []
                    for t in range(TRACERS):
                        mine = full[t * SUB : (t + 1) * SUB]
                        value = block(mine, 0)
                        for q in range(1, SUB):
                            value = jnp.where(row == q, block(mine, q), value)
                        values.append(value)
                    y, z = tile // CN % YN, tile // (CN * YN)
                    out[y, z] = out[y, z] + jnp.concatenate(values, axis=1)


def final_kernel(total_both, total_other, both, other, out):
    core, here = lax.axis_index("c"), lax.axis_index(OBS)
    sweeps = Sweeps(around(both, other, core, TRACERS), here)
    for t in range(TRACERS):
        value = both[core, :, t * LANES : (t + 1) * LANES] + sweeps.twice(around(total_both, total_other, core, t))
        for s in range(SUB):
            r, at = s // CHUNKS, s % CHUNKS * LANES
            out[t, 0, r : r + 1, at : at + LANES] = value[s : s + 1]


def neighbours(own, width):
    pairs = [(i, i + 1) for i in range(1, TILES - 1, 2)]
    other = lax.ppermute(own[:, :width], OBS, pairs + [(b, a) for a, b in pairs])
    return lax.all_gather(own, "c"), other


def shards(control, diffusivity, footprints, tile_lists, tile_counts, measured, weight):
    own = call(pack_kernel, shape(SUB, PACK), [VMEM] * 4 + [SMEM] * 2, 1, name="pack")(
        control, diffusivity, measured, weight, tile_lists, tile_counts
    )
    both, other = neighbours(own, IDS * LANES)
    mate = lax.ppermute(footprints, "c", [(0, 1), (1, 0)])
    ids = both[:, 0, IDS * LANES : IDS * LANES + ENTRIES].astype(jnp.int32)
    flux = call(flux_kernel, shape(ZN, SUB, PAY, dtype=BF16), [VMEM] * 2, 2, name="flux")(both, other)

    by_z = lax.all_to_all(flux, "z", 0, 0, tiled=True)
    panels = lax.all_to_all(jnp.broadcast_to(by_z[None], (YN,) + by_z.shape), "y", 0, 0, tiled=True)

    peers = lax.axis_size("tm") * CN
    part = call(
        predict_kernel,
        shape(peers, TRACERS * SUB, LANES),
        [VMEM] * 3 + [SMEM],
        12,
        [pltpu.VMEM((TRACERS * SUB, LANES), F32)],
        name="predict",
    )(panels, footprints, mate, ids)
    parts = lax.all_to_all(part, ("tm", "c"), 0, 0, tiled=True)
    residual, dense = call(
        adjoint_kernel,
        (shape(TRACERS, BLOCKS * SIGHTS), shape(YN, ZN, SUB, PAY)),
        [VMEM] * 4 + [SMEM],
        12,
        [pltpu.VMEM((TRACERS * SUB, LANES), F32)],
        name="adjoint",
    )(parts, both, footprints, mate, ids)

    over_y = lax.all_to_all(dense, "y", 0, 0, tiled=True).sum(axis=0)
    total = lax.all_to_all(over_y, "z", 0, 0, tiled=True).sum(axis=0)

    total_both, total_other = neighbours(total, PAY)
    gradient = call(final_kernel, shape(*control.shape), [VMEM] * 4, 2, name="final")(
        total_both, total_other, both, other
    )
    return gradient, residual


def solution(mesh):
    fine = Mesh(mesh.devices.reshape(mesh.shape["tm"], ZN, YN, CN), ("tm",) + OBS)
    placed = (
        P(None, "tm", OBS, None),
        P(OBS, None),
        P(OBS, None, None, "tm"),
        P(OBS, None),
        P(OBS),
        P(None, OBS),
        P(None, OBS),
    )
    return jax.shard_map(
        shards,
        mesh=fine,
        in_specs=placed,
        out_specs=(P(None, "tm", OBS, None), P(None, OBS)),
        check_vma=False,
    )
```

time: 128 us -> 120 us (0.938)
  blocking collectives: 86.3 us -> 67.9 us
  starting transfers between devices: 15.6 us -> 23.5 us
  local copies, waits for them, and re-layouts: 1.99 us -> 7.09 us
  Pallas kernels: 15.3 us -> 10.8 us
  waiting for transfers between devices: 4.95 us -> 7.88 us
  other arithmetic: 1.34 us -> 0.06 us
    all_gather x2 -> x0, blocking collectives: 12.4 us -> none  [the longest x1 6.64 us: shards(): chip = lax.all_gather(entries, 'c', axis=0, tiled=True)]
    all_to_all x0 -> x1, blocking collectives: none -> 11.9 us  [shards(): parts = lax.all_to_all(part, ('tm', 'c'), 0, 0, tiled=True)]
    psum x1 -> x0, blocking collectives: 9.26 us -> none  [shards(): predicted = lax.psum(part, 'tm')]
    ppermute x2 -> x3, starting transfers between devices: 11.8 us -> 18 us  [the longest x2 9.26 us: neighbours(): lax.ppermute(own[:, :width], OBS, pairs + [(b, a) for a, b in pairs])]
    unnamed x4 -> x16, local copies, waits for them, and re-layouts: 1.22 us -> 6.31 us
    pallas_call x6 -> x5, Pallas kernels: 15.3 us -> 10.8 us  [the longest x1 4.72 us: shards(): call(adjoint_kernel, (shape(TRACERS, BLOCKS * SIGHTS), shape(YN, ZN, SUB,...]
    all_gather x2, blocking collectives: 7.9 us -> 3.68 us  [neighbours(): return (lax.all_gather(own, 'c'), other)]
    all_to_all x1, blocking collectives: 25.1 us -> 22.7 us  [shards(): by_z = lax.all_to_all(flux, 'z', 0, 0, tiled=True)]
  transfers between devices with their start and end apart: 3 -> 4, of which waited for: 1 -> 2; matrix products, arithmetic and copies ran while one was open for 1% -> 1% of each run, Pallas kernels for 0% -> 1%
where the time goes in v3:
time: 120 us; the launch traced here: 118 us
  blocking collectives  67.9 us (57%)
  starting transfers between devices  23.5 us (20%)
  Pallas kernels  10.8 us (9%)
  waiting for transfers between devices  7.88 us (7%)
  local copies, waits for them, and re-layouts  7.09 us (6%)
    all_to_all x1, blocking collectives, shards(): by_z = lax.all_to_all(flux, 'z', 0, 0, tiled=True)  22.7 us
    all_to_all x1, blocking collectives, shards(): total = lax.all_to_all(over_y, 'z', 0, 0, tiled=True).sum(axis=0)  16.1 us
    all_to_all x1, blocking collectives, shards(): over_y = lax.all_to_all(dense, 'y', 0, 0, tiled=True).sum(axis=0)  13.6 us
    all_to_all x1, blocking collectives, shards(): parts = lax.all_to_all(part, ('tm', 'c'), 0, 0, tiled=True)  11.9 us
    ppermute x2, starting transfers between devices, neighbours(): lax.ppermute(own[:, :width], OBS, pairs + [(b, a) for a, b in pairs])  9.26 us
    ppermute x1, starting transfers between devices, shards(): mate = lax.ppermute(footprints, 'c', [(0, 1), (1, 0)])  8.79 us
    all_to_all x1, waiting for transfers between devices, shards(): lax.all_to_all(jnp.broadcast_to(by_z[None], (YN,) + by_z.shape), 'y', 0,...  6.59 us
    unnamed x16, local copies, waits for them, and re-layouts  6.31 us
  transfers between devices with their start and end apart: 4, of which 2 were waited for; matrix products, arithmetic and copies ran while one was open for 1% of the time, Pallas kernels for 1%

profile of v3, /device:TPU:1, one launch (start us, length us, event | category | flops | bytes accessed | tf_op | source)
XLA Modules:
  0.0 118.0 jit_solution(5481283342428685120)
XLA Ops:
  0.6 8.8 %collective-permute-start.1 = (bf16[4,4,128,1024]{3,2,1,0:T(8,128)(2,1)}, bf16[4,4,128,1024]{3,2,1,0:T(8,128)(2,1)}, u32[]{:S(2)}, u32[]{:S(2)}) collective-permute-start(bf16[4,4,128,1024]{3,2,1,0:T(8,128)(2,1)} %own.3), channel_id=1, source_target_pairs={{0,1},{1,0},{2,3},{3,2},{4,5},{5,4},{6,7},{7,6},{8,9},{9,8},{10,11... | collective-permute-start | bytes 12582920 | tf_op jit(solution)/shard_map/ppermute | solution.py:230
  9.4 0.0 copy-start.2
  9.4 0.7 copy-done.2
  10.1 0.0 copy-start.3
  10.1 0.7 copy-done.3
  10.8 0.0 copy-start.4
  10.8 0.7 copy-done.4
  11.5 0.0 copy-start.5
  11.5 0.7 copy-done.5
  12.2 0.0 copy-start.6
  12.2 0.7 copy-done.6
  12.9 0.0 copy-start.7
  12.9 0.7 copy-done.7
  13.6 0.6 pack.1
  14.2 1.9 %collective-permute-start = (f32[8,512]{1,0:T(8,128)S(1)}, f32[8,512]{1,0:T(8,128)S(1)}, u32[]{:S(2)}, u32[]{:S(2)}) collective-permute-start(f32[8,512]{1,0:T(8,128)S(1)} %slice.8), channel_id=1, source_target_pairs={{1,2},{3,4},{5,6},{7,8},{9,10},{11,12},{13,14},{15,16},{17,18},{19... | collective-permute-start | bytes 49160 | tf_op jit(solution)/shard_map/ppermute | solution.py:221
  16.1 1.9 %all-gather = f32[16,1024]{1,0:T(8,128)S(1)} all-gather(f32[8,1024]{1,0:T(8,128)S(1)} %pack.1), channel_id=2, replica_groups=mesh['tm'=4,'z'=16,'y'=4,'c'=2] {'c'}, dimensions={0}, use_global_device_ids=true | all-gather | bytes 98304 | tf_op jit(solution)/shard_map/all_gather | solution.py:222
  18.0 1.3 %collective-permute-done.other = f32[8,512]{1,0:T(8,128)S(1)} collective-permute-done((f32[8,512]{1,0:T(8,128)S(1)}, f32[8,512]{1,0:T(8,128)S(1)}, u32[]{:S(2)}, u32[]{:S(2)}) %collective-permute-start) | collective-permute-done | bytes 16416 | tf_op jit(solution)/shard_map/ppermute | solution.py:221
  19.2 0.2 flux.1
  19.4 22.7 %all_to_all.25 = bf16[16,8,384]{2,1,0:T(8,128)(2,1)S(1)} all-to-all(bf16[16,8,384]{2,1,0:T(8,128)(2,1)S(1)} %flux.1), channel_id=1, replica_groups=mesh['tm'=4,'z'=16,'y'=4,'c'=2] {'z'}, dimensions={0} | all-to-all | bytes 196608 | tf_op jit(solution)/shard_map/all_to_all | solution.py:234
  42.1 0.8 broadcast_in_dim.2
  42.9 5.5 %all-to-all-start.1 = ((bf16[4,16,8,384]{3,2,1,0:T(8,128)(2,1)}), bf16[4,16,8,384]{3,2,1,0:T(8,128)(2,1)S(1)}, u32[]{:S(2)}, u32[]{:S(2)}) async-start(bf16[4,16,8,384]{3,2,1,0:T(8,128)(2,1)} %broadcast_in_dim.2), calls=%async_computation.1 | async-start | bytes 786432 | tf_op jit(solution)/shard_map/all_to_all | solution.py:235
  48.4 6.6 %all-to-all-done.1.panels = bf16[4,16,8,384]{3,2,1,0:T(8,128)(2,1)S(1)} async-done(((bf16[4,16,8,384]{3,2,1,0:T(8,128)(2,1)}), bf16[4,16,8,384]{3,2,1,0:T(8,128)(2,1)S(1)}, u32[]{:S(2)}, u32[]{:S(2)}) %all-to-all-start.1) | async-done | bytes 393248 | tf_op jit(solution)/shard_map/all_to_all | solution.py:235
  55.0 0.0 collective-permute-done.1.mate
  55.0 0.0 copy-start
  55.0 2.2 %copy-done = bf16[4,4,128,1024]{3,2,1,0:T(8,128)(2,1)S(1)} copy-done((bf16[4,4,128,1024]{3,2,1,0:T(8,128)(2,1)S(1)}, bf16[4,4,128,1024]{3,2,1,0:T(8,128)(2,1)}, u32[]{:S(2)}) %copy-start) | copy-done | bytes 4194328
  57.2 0.0 copy-start.1
  57.2 4.5 %predict.1 = f32[8,24,128]{2,1,0:T(8,128)S(1)} custom-call(bf16[4,16,8,384]{3,2,1,0:T(8,128)(2,1)S(1)} %all-to-all-done.1.panels, bf16[4,4,128,1024]{3,2,1,0:T(8,128)(2,1)S(1)} %copy-done, bf16[4,4,128,1024]{3,2,1,0:T(8,128)(2,1)} %collective-permute-done.1.mate, s32[2,16]{1,0:T(2,128)S(1)} %bitcast.8), custom_call_target="tpu_custom_call" | custom-call | tf_op jit(solution)/shard_map/predict/pallas_call | solution.py:238
  61.7 11.9 %all_to_all.26.parts = f32[8,24,128]{2,1,0:T(8,128)S(1)} all-to-all(f32[8,24,128]{2,1,0:T(8,128)S(1)} %predict.1), channel_id=1, replica_groups=mesh['tm'=4,'z'=16,'y'=4,'c'=2] {'tm','c'}, dimensions={0} | all-to-all | bytes 196608 | tf_op jit(solution)/shard_map/all_to_all | solution.py:246
  73.6 0.0 copy-done.1
  73.6 4.7 %adjoint.1 = (f32[3,512]{1,0:T(4,128)}, f32[4,16,8,384]{3,2,1,0:T(8,128)S(1)}) custom-call(f32[8,24,128]{2,1,0:T(8,128)S(1)} %all_to_all.26.parts, f32[2,8,1024]{2,1,0:T(8,128)S(1)} %bitcast.5, bf16[4,4,128,1024]{3,2,1,0:T(8,128)(2,1)S(1)} %copy-done.1, bf16[4,4,128,1024]{3,2,1,0:T(8,128)(2,1)} %collective-permute-done.1.mate, s32[2,16]{1,0:T(2,128)S(1)} %bitcast.9), custom_call_target="tpu_custom_call" | custom-call | tf_op jit(solution)/shard_map/adjoint/pallas_call | solution.py:247
  78.3 13.6 %all_to_all.27 = f32[4,16,8,384]{3,2,1,0:T(8,128)S(1)} all-to-all(f32[4,16,8,384]{3,2,1,0:T(8,128)S(1)} %get-tuple-element.4), channel_id=1, replica_groups=mesh['tm'=4,'z'=16,'y'=4,'c'=2] {'y'}, dimensions={0} | all-to-all | bytes 1572864 | tf_op jit(solution)/shard_map/all_to_all | solution.py:256
  92.0 16.1 %all_to_all.28 = f32[16,8,384]{2,1,0:T(8,128)S(1)} all-to-all(f32[16,8,384]{2,1,0:T(8,128)S(1)} %reduce_sum.18), channel_id=1, replica_groups=mesh['tm'=4,'z'=16,'y'=4,'c'=2] {'z'}, dimensions={0} | all-to-all | bytes 393216 | tf_op jit(solution)/shard_map/all_to_all | solution.py:257
  108.1 7.3 %collective-permute-start.2 = (f32[8,384]{1,0:T(8,128)S(1)}, f32[8,384]{1,0:T(8,128)S(1)}, u32[]{:S(2)}, u32[]{:S(2)}) collective-permute-start(f32[8,384]{1,0:T(8,128)S(1)} %reduce_sum.19), channel_id=1, source_target_pairs={{1,2},{3,4},{5,6},{7,8},{9,10},{11,12},{13,14},{15,16},{17,18},{19... | collective-permute-start | bytes 36872 | tf_op jit(solution)/shard_map/ppermute | solution.py:221
  115.4 1.8 %all-gather.1 = f32[16,384]{1,0:T(8,128)S(1)} all-gather(f32[8,384]{1,0:T(8,128)S(1)} %reduce_sum.19), channel_id=3, replica_groups=mesh['tm'=4,'z'=16,'y'=4,'c'=2] {'c'}, dimensions={0}, use_global_device_ids=true | all-gather | bytes 36864 | tf_op jit(solution)/shard_map/all_gather | solution.py:222
  117.2 0.0 collective-permute-done.2.total_other
  117.2 0.8 final.1
  (4 shorter events, 0.1 us)
Async XLA Ops:
  0.6 54.4 %collective-permute-start.1 = (bf16[4,4,128,1024]{3,2,1,0:T(8,128)(2,1)}, bf16[4,4,128,1024]{3,2,1,0:T(8,128)(2,1)}, u32[]{:S(2)}, u32[]{:S(2)}) collective-permute-start(bf16[4,4,128,1024]{3,2,1,0:T(8,128)(2,1)} %own.3), channel_id=1, source_target_pairs={{0,1},{1,0},{2,3},{3,2},{4,5},{5,4},{6,7},{7,6},{8,9},{9,8},{10,11... | collective-permute-start | bytes 12582920 | tf_op jit(solution)/shard_map/ppermute | solution.py:230
  9.4 0.7 copy-start.2
  10.1 0.7 copy-start.3
  10.8 0.7 copy-start.4
  11.5 0.7 copy-start.5
  12.2 0.7 copy-start.6
  12.9 0.7 copy-start.7
  14.2 5.1 %collective-permute-start = (f32[8,512]{1,0:T(8,128)S(1)}, f32[8,512]{1,0:T(8,128)S(1)}, u32[]{:S(2)}, u32[]{:S(2)}) collective-permute-start(f32[8,512]{1,0:T(8,128)S(1)} %slice.8), channel_id=1, source_target_pairs={{1,2},{3,4},{5,6},{7,8},{9,10},{11,12},{13,14},{15,16},{17,18},{19... | collective-permute-start | bytes 49160 | tf_op jit(solution)/shard_map/ppermute | solution.py:221
  42.9 12.1 %all-to-all-start.1 = ((bf16[4,16,8,384]{3,2,1,0:T(8,128)(2,1)}), bf16[4,16,8,384]{3,2,1,0:T(8,128)(2,1)S(1)}, u32[]{:S(2)}, u32[]{:S(2)}) async-start(bf16[4,16,8,384]{3,2,1,0:T(8,128)(2,1)} %broadcast_in_dim.2), calls=%async_computation.1 | async-start | bytes 786432 | tf_op jit(solution)/shard_map/all_to_all | solution.py:235
  55.0 2.2 %copy-start = (bf16[4,4,128,1024]{3,2,1,0:T(8,128)(2,1)S(1)}, bf16[4,4,128,1024]{3,2,1,0:T(8,128)(2,1)}, u32[]{:S(2)}) copy-start(bf16[4,4,128,1024]{3,2,1,0:T(8,128)(2,1)} %own.3) | copy-start | bytes 12582916
  57.2 16.4 %copy-start.1 = (bf16[4,4,128,1024]{3,2,1,0:T(8,128)(2,1)S(1)}, bf16[4,4,128,1024]{3,2,1,0:T(8,128)(2,1)}, u32[]{:S(2)}) copy-start(bf16[4,4,128,1024]{3,2,1,0:T(8,128)(2,1)} %own.3) | copy-start | bytes 12582916
  108.1 9.2 %collective-permute-start.2 = (f32[8,384]{1,0:T(8,128)S(1)}, f32[8,384]{1,0:T(8,128)S(1)}, u32[]{:S(2)}, u32[]{:S(2)}) collective-permute-start(f32[8,384]{1,0:T(8,128)S(1)} %reduce_sum.19), channel_id=1, source_target_pairs={{1,2},{3,4},{5,6},{7,8},{9,10},{11,12},{13,14},{15,16},{17,18},{19... | collective-permute-start | bytes 36872 | tf_op jit(solution)/shard_map/ppermute | solution.py:221

commit v4 on v3

--- a/solution.py
+++ b/solution.py
@@ -21,6 +21,7 @@
 
 VMEM = pl.BlockSpec(memory_space=pltpu.VMEM)
 SMEM = pl.BlockSpec(memory_space=pltpu.SMEM)
+ANY = pl.BlockSpec(memory_space=pl.ANY)
 MIB = 1 << 20
 
 
@@ -53,7 +54,15 @@
     return at % SUB, (SEEN + at // SUB) * LANES
 
 
-def pack_kernel(control, diffusivity, measured, weight, lists, counts, out):
+def pack_kernel(*refs):
+    sources, (lists, counts, out), targets, sem = refs[:4], refs[4:7], refs[7:11], refs[11]
+    copies = [pltpu.make_async_copy(a, b, sem.at[i]) for i, (a, b) in enumerate(zip(sources, targets))]
+    for copy in copies:
+        copy.start()
+    for copy in copies:
+        copy.wait()
+    control, diffusivity, measured, weight = targets
+
     def rows(read):
         return jnp.concatenate([read(s // CHUNKS, s % CHUNKS * LANES) for s in range(SUB)], axis=0)
 
@@ -128,39 +137,85 @@
     return row == lane // LANES
 
 
-def predict_kernel(panels, own, mate, ids, out, total):
+def copies_kernel(source, out):
+    for y in range(YN):
+        out[y] = source[...]
+
+
+STEP = 4
+
+
+def start_active(own, mate, ids, held, order, sem, core):
+    count = jnp.int32(0)
+    for source, c in ((own, core), (mate, 1 - core)):
+        for e in range(ENTRIES):
+            tile = ids[c, e]
+            active = (tile >= 0) & (tile % CN == core)
+            order[count] = c * ENTRIES + e
+
+            @pl.when(active)
+            def _(source=source, e=e, at=count):
+                pltpu.make_async_copy(source.at[e // REFS, e % REFS], held.at[at], sem.at[at]).start()
+
+            count = count + active.astype(jnp.int32)
+    return count
+
+
+def over_active(count, own, ids, held, order, sem, work):
+    def step(i, carry):
+        found = []
+        for u in range(STEP):
+            at = i * STEP + u
+            real = at < count
+
+            @pl.when(real)
+            def _(at=at):
+                pltpu.make_async_copy(own.at[0, 0], held.at[at], sem.at[at]).wait()
+
+            place = jnp.minimum(at, count - 1)
+            entry = order[place]
+            found.append((real, entry // REFS, ids[entry // ENTRIES, entry % ENTRIES], held.at[place]))
+        work(found)
+        return carry
+
+    lax.fori_loop(0, (count + STEP - 1) // STEP, step, 0)
+
+
+def predict_kernel(panels, own, mate, ids, out, held, order, sem, totals):
     core = lax.axis_index("c")
+    count = start_active(own, mate, ids, held, order, sem, core)
     match = diagonal()
-    for source, c in ((own, core), (mate, 1 - core)):
-        for b in range(BLOCKS):
-            total[...] = jnp.zeros_like(total)
-            for k in range(REFS):
-                tile = ids[c, b * REFS + k]
-
-                @pl.when((tile >= 0) & (tile % CN == core))
-                def _(tile=tile, source=source, b=b, k=k):
-                    panel = panels[tile // CN % YN, tile // (CN * YN)].astype(F32)
-                    left = jnp.concatenate(
-                        [
-                            jnp.where(match, jnp.concatenate([block(panel, t)] * SUB, axis=1), 0.0)
-                            for t in range(TRACERS)
-                        ],
-                        axis=0,
-                    ).astype(BF16)
-                    total[...] += lax.dot_general(
-                        left, source[b, k], (((1,), (1,)), ((), ())), preferred_element_type=F32
-                    )
-
-            for t in range(TRACERS):
-                row = jnp.sum(total[t * SUB : (t + 1) * SUB], axis=0, keepdims=True)
-                out[0, pl.ds(t * SUB + c * BLOCKS + b, 1), :] = row
-    whole = out[0]
-    for peer in range(1, out.shape[0]):
+    totals[...] = jnp.zeros_like(totals)
+
+    def work(found):
+        terms = []
+        for real, _, tile, footprint in found:
+            panel = panels[tile // CN % YN, tile // (CN * YN)].astype(F32)
+            panel = jnp.where(real, panel, 0.0)
+            left = jnp.concatenate(
+                [jnp.where(match, jnp.concatenate([block(panel, t)] * SUB, axis=1), 0.0) for t in range(TRACERS)],
+                axis=0,
+            ).astype(BF16)
+            terms.append(
+                lax.dot_general(left, footprint[...], (((1,), (1,)), ((), ())), preferred_element_type=F32)
+            )
+        for (_, b, _, _), term in zip(found, terms):
+            totals[b] = totals[b] + term
+
+    over_active(count, own, ids, held, order, sem, work)
+    rows = [
+        jnp.sum(totals[b, t * SUB : (t + 1) * SUB], axis=0, keepdims=True)
+        for t in range(TRACERS)
+        for b in range(CN * BLOCKS)
+    ]
+    whole = jnp.concatenate(rows, axis=0)
+    for peer in range(out.shape[0]):
         out[peer] = whole
 
 
-def adjoint_kernel(parts, both, own, mate, ids, residual, out, misfit):
+def adjoint_kernel(parts, both, own, mate, ids, residual, out, held, order, sem, lefts, sums):
     core = lax.axis_index("c")
+    count = start_active(own, mate, ids, held, order, sem, core)
     whole = parts[0]
     for peer in range(1, parts.shape[0]):
         whole = whole + parts[peer]
@@ -174,36 +229,36 @@
                     rows.append(both[c, r : r + 1, at : at + LANES])
         return jnp.concatenate(rows, axis=0)
 
-    misfit[...] = (whole - seen(0)) * seen(1)
+    misfit = (whole - seen(0)) * seen(1)
     for t in range(TRACERS):
         for b in range(BLOCKS):
-            residual[t : t + 1, b * SIGHTS : (b + 1) * SIGHTS] = misfit[pl.ds(t * SUB + core * BLOCKS + b, 1), :]
-    out[...] = jnp.zeros_like(out)
+            first, second = (misfit[t * SUB + c * BLOCKS + b : t * SUB + c * BLOCKS + b + 1] for c in range(CN))
+            residual[t : t + 1, b * SIGHTS : (b + 1) * SIGHTS] = jnp.where(core == 0, first, second)
+    for b in range(CN * BLOCKS):
+        lefts[b] = jnp.concatenate(
+            [jnp.broadcast_to(misfit[t * SUB + b : t * SUB + b + 1], (SUB, SIGHTS)) for t in range(TRACERS)], axis=0
+        )
+    sums[...] = jnp.zeros_like(sums)
     row = lax.broadcasted_iota(jnp.int32, (SUB, LANES), 0)
-    for source, c in ((own, core), (mate, 1 - core)):
-        for b in range(BLOCKS):
-            left = jnp.concatenate(
-                [
-                    jnp.broadcast_to(misfit[pl.ds(t * SUB + c * BLOCKS + b, 1), :], (SUB, SIGHTS))
-                    for t in range(TRACERS)
-                ],
-                axis=0,
-            ).astype(BF16)
-            for k in range(REFS):
-                tile = ids[c, b * REFS + k]
-
-                @pl.when((tile >= 0) & (tile % CN == core))
-                def _(tile=tile, source=source, b=b, k=k, left=left):
-                    full = jnp.dot(left, source[b, k], preferred_element_type=F32)
-                    values = []
-                    for t in range(TRACERS):
-                        mine = full[t * SUB : (t + 1) * SUB]
-                        value = block(mine, 0)
-                        for q in range(1, SUB):
-                            value = jnp.where(row == q, block(mine, q), value)
-                        values.append(value)
-                    y, z = tile // CN % YN, tile // (CN * YN)
-                    out[y, z] = out[y, z] + jnp.concatenate(values, axis=1)
+
+    def work(found):
+        values = []
+        for real, b, _, footprint in found:
+            full = jnp.dot(lefts[b].astype(BF16), footprint[...], preferred_element_type=F32)
+            blocks = []
+            for t in range(TRACERS):
+                mine = full[t * SUB : (t + 1) * SUB]
+                value = block(mine, 0)
+                for q in range(1, SUB):
+                    value = jnp.where(row == q, block(mine, q), value)
+                blocks.append(jnp.where(real, value, 0.0))
+            values.append(jnp.concatenate(blocks, axis=1))
+        for (_, _, tile, _), value in zip(found, values):
+            y, z = tile // CN % YN, tile // (CN * YN)
+            sums[y, z] = sums[y, z] + value
+
+    over_active(count, own, ids, held, order, sem, work)
+    out[...] = sums[...].astype(BF16)
 
 
 def final_kernel(total_both, total_other, both, other, out):
@@ -223,37 +278,46 @@
 
 
 def shards(control, diffusivity, footprints, tile_lists, tile_counts, measured, weight):
-    own = call(pack_kernel, shape(SUB, PACK), [VMEM] * 4 + [SMEM] * 2, 1, name="pack")(
-        control, diffusivity, measured, weight, tile_lists, tile_counts
-    )
+    given = (control, diffusivity, measured, weight)
+    own = call(
+        pack_kernel,
+        shape(SUB, PACK),
+        [ANY] * 4 + [SMEM] * 2,
+        1,
+        [pltpu.VMEM(a.shape, F32) for a in given] + [pltpu.SemaphoreType.DMA((4,))],
+        name="pack",
+    )(*given, tile_lists, tile_counts)
     both, other = neighbours(own, IDS * LANES)
+    both, footprints = lax.optimization_barrier((both, footprints))
     mate = lax.ppermute(footprints, "c", [(0, 1), (1, 0)])
     ids = both[:, 0, IDS * LANES : IDS * LANES + ENTRIES].astype(jnp.int32)
     flux = call(flux_kernel, shape(ZN, SUB, PAY, dtype=BF16), [VMEM] * 2, 2, name="flux")(both, other)
 
     by_z = lax.all_to_all(flux, "z", 0, 0, tiled=True)
-    panels = lax.all_to_all(jnp.broadcast_to(by_z[None], (YN,) + by_z.shape), "y", 0, 0, tiled=True)
+    copies = call(copies_kernel, shape(YN, *by_z.shape, dtype=BF16), [VMEM], 2, name="copies")(by_z)
+    panels = lax.all_to_all(copies, "y", 0, 0, tiled=True)
 
     peers = lax.axis_size("tm") * CN
+    active = [
+        pltpu.VMEM((CN * ENTRIES, SIGHTS, CELLS), BF16),
+        pltpu.SMEM((CN * ENTRIES + 1,), jnp.int32),
+        pltpu.SemaphoreType.DMA((CN * ENTRIES,)),
+        pltpu.VMEM((CN * BLOCKS, TRACERS * SUB, LANES), F32),
+    ]
     part = call(
-        predict_kernel,
-        shape(peers, TRACERS * SUB, LANES),
-        [VMEM] * 3 + [SMEM],
-        12,
-        [pltpu.VMEM((TRACERS * SUB, LANES), F32)],
-        name="predict",
+        predict_kernel, shape(peers, TRACERS * SUB, LANES), [VMEM, ANY, ANY, SMEM], 16, active, name="predict"
     )(panels, footprints, mate, ids)
     parts = lax.all_to_all(part, ("tm", "c"), 0, 0, tiled=True)
     residual, dense = call(
         adjoint_kernel,
-        (shape(TRACERS, BLOCKS * SIGHTS), shape(YN, ZN, SUB, PAY)),
-        [VMEM] * 4 + [SMEM],
-        12,
-        [pltpu.VMEM((TRACERS * SUB, LANES), F32)],
+        (shape(TRACERS, BLOCKS * SIGHTS), shape(YN, ZN, SUB, PAY, dtype=BF16)),
+        [VMEM, VMEM, ANY, ANY, SMEM],
+        16,
+        active + [pltpu.VMEM((YN, ZN, SUB, PAY), F32)],
         name="adjoint",
     )(parts, both, footprints, mate, ids)
 
-    over_y = lax.all_to_all(dense, "y", 0, 0, tiled=True).sum(axis=0)
+    over_y = lax.all_to_all(dense, "y", 0, 0, tiled=True).astype(F32).sum(axis=0)
     total = lax.all_to_all(over_y, "z", 0, 0, tiled=True).sum(axis=0)
 
     total_both, total_other = neighbours(total, PAY)

time: 120 us -> 115 us (0.958)
  starting transfers between devices: 23.5 us -> 18.9 us
  waiting for transfers between devices: 7.88 us -> 9.71 us
    ppermute x1, starting transfers between devices: 8.79 us -> 2.25 us  [shards(): mate = lax.ppermute(footprints, 'c', [(0, 1), (1, 0)])]
    all_gather x2, blocking collectives: 3.68 us -> 10.2 us  [neighbours(): return (lax.all_gather(own, 'c'), other)]
    all_to_all x1, blocking collectives: 13.6 us -> 10 us  [shards(): lax.all_to_all(dense, 'y', 0, 0, tiled=True).astype(F32).sum(axis=0)]
    ppermute x2, waiting for transfers between devices: 1.28 us -> 3.13 us  [neighbours(): lax.ppermute(own[:, :width], OBS, pairs + [(b, a) for a, b in pairs])]
    all_to_all x1, starting transfers between devices: 5.49 us -> 7.15 us  [shards(): panels = lax.all_to_all(copies, 'y', 0, 0, tiled=True)]
    all_to_all x1, blocking collectives: 22.7 us -> 21.2 us  [shards(): by_z = lax.all_to_all(flux, 'z', 0, 0, tiled=True)]
    pallas_call x2 -> x3, Pallas kernels: 5.12 us -> 5.15 us  [the longest x1 3.69 us: shards(): call(predict_kernel, shape(peers, TRACERS * SUB, LANES), [VMEM, ANY, ANY,...]
  transfers between devices with their start and end apart: 4 -> 4, of which waited for: 2 -> 2; matrix products, arithmetic and copies ran while one was open for 1% -> 0% of each run, Pallas kernels for 1% -> 1%
where the time goes in v4:
time: 115 us; the launch traced here: 113 us
  blocking collectives  67.6 us (59%)
  starting transfers between devices  18.9 us (16%)
  Pallas kernels  9.75 us (8%)
  waiting for transfers between devices  9.71 us (8%)
  local copies, waits for them, and re-layouts  6.31 us (5%)
    all_to_all x1, blocking collectives, shards(): by_z = lax.all_to_all(flux, 'z', 0, 0, tiled=True)  21.2 us
    all_to_all x1, blocking collectives, shards(): total = lax.all_to_all(over_y, 'z', 0, 0, tiled=True).sum(axis=0)  14.9 us
    all_to_all x1, blocking collectives, shards(): parts = lax.all_to_all(part, ('tm', 'c'), 0, 0, tiled=True)  11.3 us
    all_gather x2, blocking collectives, neighbours(): return (lax.all_gather(own, 'c'), other)  10.2 us
    all_to_all x1, blocking collectives, shards(): lax.all_to_all(dense, 'y', 0, 0, tiled=True).astype(F32).sum(axis=0)  10 us
    ppermute x2, starting transfers between devices, neighbours(): lax.ppermute(own[:, :width], OBS, pairs + [(b, a) for a, b in pairs])  9.51 us
    all_to_all x1, starting transfers between devices, shards(): panels = lax.all_to_all(copies, 'y', 0, 0, tiled=True)  7.15 us
    all_to_all x1, waiting for transfers between devices, shards(): panels = lax.all_to_all(copies, 'y', 0, 0, tiled=True)  6.58 us
  transfers between devices with their start and end apart: 4, of which 2 were waited for; matrix products, arithmetic and copies ran while one was open for 0% of the time, Pallas kernels for 1%

profile of v4, /device:TPU:1, one launch (start us, length us, event | category | flops | bytes accessed | tf_op | source)
XLA Modules:
  0.0 113.1 jit_solution(15935127960588711169)
XLA Ops:
  0.6 0.0 copy-start.2
  0.6 0.7 copy-done.2
  1.3 0.0 copy-start.3
  1.3 0.7 copy-done.3
  2.0 0.0 copy-start.4
  2.0 0.7 copy-done.4
  2.7 0.0 copy-start.5
  2.7 0.7 copy-done.5
  3.4 0.0 copy-start.6
  3.4 0.7 copy-done.6
  4.1 0.0 copy-start.7
  4.1 0.7 copy-done.7
  4.8 0.7 pack.1
  5.4 8.4 %all-gather = f32[16,1024]{1,0:T(8,128)S(1)} all-gather(f32[8,1024]{1,0:T(8,128)S(1)} %pack.1), channel_id=2, replica_groups=mesh['tm'=4,'z'=16,'y'=4,'c'=2] {'c'}, dimensions={0}, use_global_device_ids=true | all-gather | bytes 98304 | tf_op jit(solution)/shard_map/all_gather | solution.py:277
  13.8 2.2 %collective-permute-start.1 = (bf16[4,4,128,1024]{3,2,1,0:T(8,128)(2,1)}, bf16[4,4,128,1024]{3,2,1,0:T(8,128)(2,1)}, u32[]{:S(2)}, u32[]{:S(2)}) collective-permute-start(bf16[4,4,128,1024]{3,2,1,0:T(8,128)(2,1)} %own.1), channel_id=1, source_target_pairs={{0,1},{1,0},{2,3},{3,2},{4,5},{5,4},{6,7},{7,6},{8,9},{9,8},{10,11... | collective-permute-start | bytes 12582920 | tf_op jit(solution)/shard_map/ppermute | solution.py:292
  16.1 1.9 %collective-permute-start = (f32[8,512]{1,0:T(8,128)S(1)}, f32[8,512]{1,0:T(8,128)S(1)}, u32[]{:S(2)}, u32[]{:S(2)}) collective-permute-start(f32[8,512]{1,0:T(8,128)S(1)} %slice.8), channel_id=1, source_target_pairs={{1,2},{3,4},{5,6},{7,8},{9,10},{11,12},{13,14},{15,16},{17,18},{19... | collective-permute-start | bytes 49160 | tf_op jit(solution)/shard_map/ppermute | solution.py:276
  18.0 3.1 %collective-permute-done.other = f32[8,512]{1,0:T(8,128)S(1)} collective-permute-done((f32[8,512]{1,0:T(8,128)S(1)}, f32[8,512]{1,0:T(8,128)S(1)}, u32[]{:S(2)}, u32[]{:S(2)}) %collective-permute-start) | collective-permute-done | bytes 16416 | tf_op jit(solution)/shard_map/ppermute | solution.py:276
  21.2 0.2 flux.1
  21.4 21.2 %all_to_all.25.source = bf16[16,8,384]{2,1,0:T(8,128)(2,1)S(1)} all-to-all(bf16[16,8,384]{2,1,0:T(8,128)(2,1)S(1)} %flux.1), channel_id=1, replica_groups=mesh['tm'=4,'z'=16,'y'=4,'c'=2] {'z'}, dimensions={0} | all-to-all | bytes 196608 | tf_op jit(solution)/shard_map/all_to_all | solution.py:296
  42.5 0.8 copies.1
  43.3 7.2 %all-to-all-start.1 = ((bf16[4,16,8,384]{3,2,1,0:T(8,128)(2,1)}), bf16[4,16,8,384]{3,2,1,0:T(8,128)(2,1)S(1)}, u32[]{:S(2)}, u32[]{:S(2)}) async-start(bf16[4,16,8,384]{3,2,1,0:T(8,128)(2,1)} %copies.1), calls=%async_computation.1 | async-start | bytes 786432 | tf_op jit(solution)/shard_map/all_to_all | solution.py:298
  50.5 6.6 %all-to-all-done.1.panels = bf16[4,16,8,384]{3,2,1,0:T(8,128)(2,1)S(1)} async-done(((bf16[4,16,8,384]{3,2,1,0:T(8,128)(2,1)}), bf16[4,16,8,384]{3,2,1,0:T(8,128)(2,1)S(1)}, u32[]{:S(2)}, u32[]{:S(2)}) %all-to-all-start.1) | async-done | bytes 393248 | tf_op jit(solution)/shard_map/all_to_all | solution.py:298
  57.1 0.0 collective-permute-done.1.mate
  57.1 0.0 copy-start
  57.1 2.2 %copy-done = bf16[4,4,128,1024]{3,2,1,0:T(8,128)(2,1)S(1)} copy-done((bf16[4,4,128,1024]{3,2,1,0:T(8,128)(2,1)S(1)}, bf16[4,4,128,1024]{3,2,1,0:T(8,128)(2,1)}, u32[]{:S(2)}) %copy-start) | copy-done | bytes 4194328
  59.2 0.0 copy-start.1
  59.3 3.7 %predict.1 = f32[8,24,128]{2,1,0:T(8,128)S(1)} custom-call(bf16[4,16,8,384]{3,2,1,0:T(8,128)(2,1)S(1)} %all-to-all-done.1.panels, bf16[4,4,128,1024]{3,2,1,0:T(8,128)(2,1)S(1)} %copy-done, bf16[4,4,128,1024]{3,2,1,0:T(8,128)(2,1)} %collective-permute-done.1.mate, s32[2,16]{1,0:T(2,128)S(1)} %bitcast.8), custom_call_target="tpu_custom_call" | custom-call | tf_op jit(solution)/shard_map/predict/pallas_call | solution.py:307
  62.9 11.3 %all_to_all.26.parts = f32[8,24,128]{2,1,0:T(8,128)S(1)} all-to-all(f32[8,24,128]{2,1,0:T(8,128)S(1)} %predict.1), channel_id=1, replica_groups=mesh['tm'=4,'z'=16,'y'=4,'c'=2] {'tm','c'}, dimensions={0} | all-to-all | bytes 196608 | tf_op jit(solution)/shard_map/all_to_all | solution.py:310
  74.2 0.0 copy-done.1
  74.2 3.6 %adjoint.1 = (f32[3,512]{1,0:T(4,128)}, bf16[4,16,8,384]{3,2,1,0:T(8,128)(2,1)S(1)}) custom-call(f32[8,24,128]{2,1,0:T(8,128)S(1)} %all_to_all.26.parts, f32[2,8,1024]{2,1,0:T(8,128)S(1)} %bitcast.5, bf16[4,4,128,1024]{3,2,1,0:T(8,128)(2,1)S(1)} %copy-done.1, bf16[4,4,128,1024]{3,2,1,0:T(8,128)(2,1)} %collective-permute-done.1.mate, s32[2,16]{1,0:T(2,128)S(1)} %bitcast.9), custom_call_target="tpu_custom_call" | custom-call | tf_op jit(solution)/shard_map/adjoint/pallas_call | solution.py:311
  77.9 10.0 %all_to_all.27 = bf16[4,16,8,384]{3,2,1,0:T(8,128)(2,1)S(1)} all-to-all(bf16[4,16,8,384]{3,2,1,0:T(8,128)(2,1)S(1)} %get-tuple-element.8), channel_id=1, replica_groups=mesh['tm'=4,'z'=16,'y'=4,'c'=2] {'y'}, dimensions={0} | all-to-all | bytes 786432 | tf_op jit(solution)/shard_map/all_to_all | solution.py:320
  87.9 14.9 %all_to_all.28 = f32[16,8,384]{2,1,0:T(8,128)S(1)} all-to-all(f32[16,8,384]{2,1,0:T(8,128)S(1)} %convert_reduce_fusion), channel_id=1, replica_groups=mesh['tm'=4,'z'=16,'y'=4,'c'=2] {'z'}, dimensions={0} | all-to-all | bytes 393216 | tf_op jit(solution)/shard_map/all_to_all | solution.py:321
  102.9 7.6 %collective-permute-start.2 = (f32[8,384]{1,0:T(8,128)S(1)}, f32[8,384]{1,0:T(8,128)S(1)}, u32[]{:S(2)}, u32[]{:S(2)}) collective-permute-start(f32[8,384]{1,0:T(8,128)S(1)} %reduce_sum.19), channel_id=1, source_target_pairs={{1,2},{3,4},{5,6},{7,8},{9,10},{11,12},{13,14},{15,16},{17,18},{19... | collective-permute-start | bytes 36872 | tf_op jit(solution)/shard_map/ppermute | solution.py:276
  110.5 1.8 %all-gather.1 = f32[16,384]{1,0:T(8,128)S(1)} all-gather(f32[8,384]{1,0:T(8,128)S(1)} %reduce_sum.19), channel_id=3, replica_groups=mesh['tm'=4,'z'=16,'y'=4,'c'=2] {'c'}, dimensions={0}, use_global_device_ids=true | all-gather | bytes 36864 | tf_op jit(solution)/shard_map/all_gather | solution.py:277
  112.3 0.0 collective-permute-done.2.total_other
  112.3 0.8 final.1
  (4 shorter events, 0.1 us)
Async XLA Ops:
  0.6 0.7 copy-start.2
  1.3 0.7 copy-start.3
  2.0 0.7 copy-start.4
  2.7 0.7 copy-start.5
  3.4 0.7 copy-start.6
  4.1 0.7 copy-start.7
  13.8 43.2 %collective-permute-start.1 = (bf16[4,4,128,1024]{3,2,1,0:T(8,128)(2,1)}, bf16[4,4,128,1024]{3,2,1,0:T(8,128)(2,1)}, u32[]{:S(2)}, u32[]{:S(2)}) collective-permute-start(bf16[4,4,128,1024]{3,2,1,0:T(8,128)(2,1)} %own.1), channel_id=1, source_target_pairs={{0,1},{1,0},{2,3},{3,2},{4,5},{5,4},{6,7},{7,6},{8,9},{9,8},{10,11... | collective-permute-start | bytes 12582920 | tf_op jit(solution)/shard_map/ppermute | solution.py:292
  16.1 5.1 %collective-permute-start = (f32[8,512]{1,0:T(8,128)S(1)}, f32[8,512]{1,0:T(8,128)S(1)}, u32[]{:S(2)}, u32[]{:S(2)}) collective-permute-start(f32[8,512]{1,0:T(8,128)S(1)} %slice.8), channel_id=1, source_target_pairs={{1,2},{3,4},{5,6},{7,8},{9,10},{11,12},{13,14},{15,16},{17,18},{19... | collective-permute-start | bytes 49160 | tf_op jit(solution)/shard_map/ppermute | solution.py:276
  43.3 13.7 %all-to-all-start.1 = ((bf16[4,16,8,384]{3,2,1,0:T(8,128)(2,1)}), bf16[4,16,8,384]{3,2,1,0:T(8,128)(2,1)S(1)}, u32[]{:S(2)}, u32[]{:S(2)}) async-start(bf16[4,16,8,384]{3,2,1,0:T(8,128)(2,1)} %copies.1), calls=%async_computation.1 | async-start | bytes 786432 | tf_op jit(solution)/shard_map/all_to_all | solution.py:298
  57.1 2.2 %copy-start = (bf16[4,4,128,1024]{3,2,1,0:T(8,128)(2,1)S(1)}, bf16[4,4,128,1024]{3,2,1,0:T(8,128)(2,1)}, u32[]{:S(2)}) copy-start(bf16[4,4,128,1024]{3,2,1,0:T(8,128)(2,1)} %own.1) | copy-start | bytes 12582916
  59.2 15.0 %copy-start.1 = (bf16[4,4,128,1024]{3,2,1,0:T(8,128)(2,1)S(1)}, bf16[4,4,128,1024]{3,2,1,0:T(8,128)(2,1)}, u32[]{:S(2)}) copy-start(bf16[4,4,128,1024]{3,2,1,0:T(8,128)(2,1)} %own.1) | copy-start | bytes 12582916
  102.9 9.4 %collective-permute-start.2 = (f32[8,384]{1,0:T(8,128)S(1)}, f32[8,384]{1,0:T(8,128)S(1)}, u32[]{:S(2)}, u32[]{:S(2)}) collective-permute-start(f32[8,384]{1,0:T(8,128)S(1)} %reduce_sum.19), channel_id=1, source_target_pairs={{1,2},{3,4},{5,6},{7,8},{9,10},{11,12},{13,14},{15,16},{17,18},{19... | collective-permute-start | bytes 36872 | tf_op jit(solution)/shard_map/ppermute | solution.py:276

commit v5 on v4

--- a/solution.py
+++ b/solution.py
@@ -21,7 +21,7 @@
 
 VMEM = pl.BlockSpec(memory_space=pltpu.VMEM)
 SMEM = pl.BlockSpec(memory_space=pltpu.SMEM)
-ANY = pl.BlockSpec(memory_space=pl.ANY)
+HBM = pl.BlockSpec(memory_space=pltpu.HBM)
 MIB = 1 << 20
 
 
@@ -37,6 +37,10 @@
     )
 
 
+def in_hbm(array):
+    return pltpu.with_memory_space_constraint(array, pltpu.HBM)
+
+
 def shape(*dims, dtype=F32):
     return jax.ShapeDtypeStruct(dims, dtype)
 
@@ -55,26 +59,27 @@
 
 
 def pack_kernel(*refs):
-    sources, (lists, counts, out), targets, sem = refs[:4], refs[4:7], refs[7:11], refs[11]
+    sources, (out, head), targets, sem = refs[:6], refs[6:8], refs[8:14], refs[14]
     copies = [pltpu.make_async_copy(a, b, sem.at[i]) for i, (a, b) in enumerate(zip(sources, targets))]
     for copy in copies:
         copy.start()
     for copy in copies:
         copy.wait()
-    control, diffusivity, measured, weight = targets
+    control, diffusivity, measured, weight, lists, counts = targets
 
     def rows(read):
         return jnp.concatenate([read(s // CHUNKS, s % CHUNKS * LANES) for s in range(SUB)], axis=0)
 
     for t in range(TRACERS):
-        out[:, t * LANES : (t + 1) * LANES] = rows(lambda r, at, t=t: control[t, 0, r : r + 1, at : at + LANES])
-    out[:, TRACERS * LANES : 4 * LANES] = rows(lambda r, at: diffusivity[r : r + 1, at : at + LANES])
-    lane = lax.broadcasted_iota(jnp.int32, (1, LANES), 1)
-    ids = jnp.full((1, LANES), -1, jnp.int32)
+        head[:, t * LANES : (t + 1) * LANES] = rows(lambda r, at, t=t: control[t, 0, r : r + 1, at : at + LANES])
+    head[:, TRACERS * LANES :] = rows(lambda r, at: diffusivity[r : r + 1, at : at + LANES])
+    out[:, : IDS * LANES] = head[...]
+    lane = lax.broadcasted_iota(jnp.int32, (BLOCKS, REFS), 1)
+    row = lax.broadcasted_iota(jnp.int32, (BLOCKS, REFS), 0)
+    limit = jnp.zeros((BLOCKS, REFS), jnp.int32)
     for b in range(BLOCKS):
-        for k in range(REFS):
-            ids = jnp.where((lane == b * REFS + k) & (k < counts[b]), lists[b, k], ids)
-    out[:, IDS * LANES : SEEN * LANES] = jnp.broadcast_to(ids.astype(F32), (SUB, LANES))
+        limit = jnp.where(row == b, counts[0:1, b : b + 1], limit)
+    out[:BLOCKS, IDS * LANES : IDS * LANES + REFS] = jnp.where(lane < limit, lists[...], -1).astype(F32)
     for which, ref in enumerate((measured, weight)):
         for t in range(TRACERS):
             for b in range(BLOCKS):
@@ -123,7 +128,9 @@
         return self.once(jnp.where(self.inside, self.once(v), 0.0))[SUB : 2 * SUB]
 
 
-def flux_kernel(both, other, out):
+def flux_kernel(both, other, out, ids):
+    for c in range(CN):
+        ids[c] = both[c, :BLOCKS, IDS * LANES : SEEN * LANES].astype(jnp.int32)
     core, here = lax.axis_index("c"), lax.axis_index(OBS)
     sweeps = Sweeps(around(both, other, core, TRACERS), here)
     half = jnp.concatenate([sweeps.twice(around(both, other, core, t)) for t in range(TRACERS)], axis=1).astype(BF16)
@@ -145,37 +152,30 @@
 STEP = 4
 
 
-def start_active(own, mate, ids, held, order, sem, core):
+def list_active(ids, order, which, core, c, found=None):
     count = jnp.int32(0)
-    for source, c in ((own, core), (mate, 1 - core)):
-        for e in range(ENTRIES):
-            tile = ids[c, e]
-            active = (tile >= 0) & (tile % CN == core)
-            order[count] = c * ENTRIES + e
-
-            @pl.when(active)
-            def _(source=source, e=e, at=count):
-                pltpu.make_async_copy(source.at[e // REFS, e % REFS], held.at[at], sem.at[at]).start()
-
-            count = count + active.astype(jnp.int32)
+    for e in range(ENTRIES):
+        tile = ids[c, e // REFS, e % REFS]
+        active = (tile >= 0) & (tile % CN == core)
+        order[which, count] = e
+        if found is not None:
+            pl.when(active)(lambda e=e: found(e))
+        count = count + active.astype(jnp.int32)
     return count
 
 
-def over_active(count, own, ids, held, order, sem, work):
+def over_active(count, footprints, ids, order, which, c, work, ready=None):
     def step(i, carry):
-        found = []
+        entries = []
         for u in range(STEP):
             at = i * STEP + u
             real = at < count
-
-            @pl.when(real)
-            def _(at=at):
-                pltpu.make_async_copy(own.at[0, 0], held.at[at], sem.at[at]).wait()
-
-            place = jnp.minimum(at, count - 1)
-            entry = order[place]
-            found.append((real, entry // REFS, ids[entry // ENTRIES, entry % ENTRIES], held.at[place]))
-        work(found)
+            e = order[which, jnp.maximum(jnp.minimum(at, count - 1), 0)]
+            if ready is not None:
+                pl.when(real)(lambda e=e: ready(e))
+            b, k = e // REFS, e % REFS
+            entries.append((real, c * BLOCKS + b, ids[c, b, k], footprints.at[b, k]))
+        work(entries)
         return carry
 
     lax.fori_loop(0, (count + STEP - 1) // STEP, step, 0)
@@ -183,7 +183,13 @@
 
 def predict_kernel(panels, own, mate, ids, out, held, order, sem, totals):
     core = lax.axis_index("c")
-    count = start_active(own, mate, ids, held, order, sem, core)
+
+    def copy(e):
+        b, k = e // REFS, e % REFS
+        return pltpu.make_async_copy(own.at[b, k], held.at[b, k], sem.at[e])
+
+    count = list_active(ids, order, 0, core, core, lambda e: copy(e).start())
+    count_mate = list_active(ids, order, 1, core, 1 - core)
     match = diagonal()
     totals[...] = jnp.zeros_like(totals)
 
@@ -202,7 +208,8 @@
         for (_, b, _, _), term in zip(found, terms):
             totals[b] = totals[b] + term
 
-    over_active(count, own, ids, held, order, sem, work)
+    over_active(count_mate, mate, ids, order, 1, 1 - core, work)
+    over_active(count, held, ids, order, 0, core, work, lambda e: copy(e).wait())
     rows = [
         jnp.sum(totals[b, t * SUB : (t + 1) * SUB], axis=0, keepdims=True)
         for t in range(TRACERS)
@@ -213,9 +220,10 @@
         out[peer] = whole
 
 
-def adjoint_kernel(parts, both, own, mate, ids, residual, out, held, order, sem, lefts, sums):
+def adjoint_kernel(parts, both, held, mate, ids, residual, out, order, lefts, sums):
     core = lax.axis_index("c")
-    count = start_active(own, mate, ids, held, order, sem, core)
+    count = list_active(ids, order, 0, core, core)
+    count_mate = list_active(ids, order, 1, core, 1 - core)
     whole = parts[0]
     for peer in range(1, parts.shape[0]):
         whole = whole + parts[peer]
@@ -257,8 +265,43 @@
             y, z = tile // CN % YN, tile // (CN * YN)
             sums[y, z] = sums[y, z] + value
 
-    over_active(count, own, ids, held, order, sem, work)
+    over_active(count, held, ids, order, 0, core, work)
+    over_active(count_mate, mate, ids, order, 1, 1 - core, work)
     out[...] = sums[...].astype(BF16)
+
+
+LEVELS = 6
+FINE = 256.0
+
+
+def fold_y_kernel(parts, out):
+    for z in range(ZN):
+        value = parts[0, z].astype(F32)
+        for y in range(1, YN):
+            value = value + parts[y, z].astype(F32)
+        high = value.astype(BF16)
+        near = high.astype(F32)
+        size = jnp.abs(near)
+        part = (value - near) * (FINE / jnp.where(size == 0.0, 1.0, size))
+        level = jnp.clip(jnp.floor((part + 1.0) * (LEVELS / 2)), 0.0, LEVELS - 1.0)
+        code = block(level, 0) + LEVELS * block(level, 1) + LEVELS * LEVELS * block(level, 2)
+        out[z, :, :PAY] = high
+        out[z, :, PAY:] = code.astype(BF16)
+
+
+def fold_z_kernel(parts, out):
+    total = None
+    for z in range(ZN):
+        near = parts[z, :, :PAY].astype(F32)
+        code = parts[z, :, PAY:].astype(F32)
+        third = jnp.floor((code + 0.5) * (1.0 / (LEVELS * LEVELS)))
+        code = code - LEVELS * LEVELS * third
+        second = jnp.floor((code + 0.5) * (1.0 / LEVELS))
+        level = jnp.concatenate([code - LEVELS * second, second, third], axis=1)
+        part = (level + 0.5) * (2.0 / LEVELS) - 1.0
+        value = near + jnp.abs(near) * (part * (1.0 / FINE))
+        total = value if total is None else total + value
+    out[...] = total
 
 
 def final_kernel(total_both, total_other, both, other, out):
@@ -271,56 +314,70 @@
             out[t, 0, r : r + 1, at : at + LANES] = value[s : s + 1]
 
 
-def neighbours(own, width):
+def neighbours(own, head):
     pairs = [(i, i + 1) for i in range(1, TILES - 1, 2)]
-    other = lax.ppermute(own[:, :width], OBS, pairs + [(b, a) for a, b in pairs])
+    other = lax.ppermute(head, OBS, pairs + [(b, a) for a, b in pairs])
     return lax.all_gather(own, "c"), other
 
 
 def shards(control, diffusivity, footprints, tile_lists, tile_counts, measured, weight):
-    given = (control, diffusivity, measured, weight)
-    own = call(
+    given = (control, diffusivity, measured, weight, tile_lists, tile_counts.reshape(1, BLOCKS))
+    own, head = call(
         pack_kernel,
-        shape(SUB, PACK),
-        [ANY] * 4 + [SMEM] * 2,
+        (shape(SUB, PACK), shape(SUB, IDS * LANES)),
+        [HBM] * len(given),
         1,
-        [pltpu.VMEM(a.shape, F32) for a in given] + [pltpu.SemaphoreType.DMA((4,))],
+        [pltpu.VMEM(a.shape, a.dtype) for a in given] + [pltpu.SemaphoreType.DMA((len(given),))],
         name="pack",
-    )(*given, tile_lists, tile_counts)
-    both, other = neighbours(own, IDS * LANES)
-    both, footprints = lax.optimization_barrier((both, footprints))
+    )(*map(in_hbm, given))
+    both, other = neighbours(own, head)
+    flux, ids = call(
+        flux_kernel,
+        (shape(ZN, SUB, PAY, dtype=BF16), shape(CN, BLOCKS, LANES, dtype=jnp.int32)),
+        [VMEM] * 2,
+        2,
+        name="flux",
+    )(both, other)
+
+    by_z = lax.all_to_all(flux, "z", 0, 0, tiled=True)
+    by_z, footprints = lax.optimization_barrier((by_z, footprints))
     mate = lax.ppermute(footprints, "c", [(0, 1), (1, 0)])
-    ids = both[:, 0, IDS * LANES : IDS * LANES + ENTRIES].astype(jnp.int32)
-    flux = call(flux_kernel, shape(ZN, SUB, PAY, dtype=BF16), [VMEM] * 2, 2, name="flux")(both, other)
-
-    by_z = lax.all_to_all(flux, "z", 0, 0, tiled=True)
     copies = call(copies_kernel, shape(YN, *by_z.shape, dtype=BF16), [VMEM], 2, name="copies")(by_z)
     panels = lax.all_to_all(copies, "y", 0, 0, tiled=True)
 
     peers = lax.axis_size("tm") * CN
-    active = [
-        pltpu.VMEM((CN * ENTRIES, SIGHTS, CELLS), BF16),
-        pltpu.SMEM((CN * ENTRIES + 1,), jnp.int32),
-        pltpu.SemaphoreType.DMA((CN * ENTRIES,)),
-        pltpu.VMEM((CN * BLOCKS, TRACERS * SUB, LANES), F32),
-    ]
-    part = call(
-        predict_kernel, shape(peers, TRACERS * SUB, LANES), [VMEM, ANY, ANY, SMEM], 16, active, name="predict"
-    )(panels, footprints, mate, ids)
+    part, held = call(
+        predict_kernel,
+        (shape(peers, TRACERS * SUB, LANES), pltpu.VMEM(footprints.shape, BF16)),
+        [VMEM, HBM, VMEM, SMEM],
+        16,
+        [
+            pltpu.SMEM((CN, ENTRIES + 1), jnp.int32),
+            pltpu.SemaphoreType.DMA((ENTRIES,)),
+            pltpu.VMEM((CN * BLOCKS, TRACERS * SUB, LANES), F32),
+        ],
+        name="predict",
+    )(panels, in_hbm(footprints), mate, ids)
     parts = lax.all_to_all(part, ("tm", "c"), 0, 0, tiled=True)
     residual, dense = call(
         adjoint_kernel,
         (shape(TRACERS, BLOCKS * SIGHTS), shape(YN, ZN, SUB, PAY, dtype=BF16)),
-        [VMEM, VMEM, ANY, ANY, SMEM],
+        [VMEM] * 4 + [SMEM],
         16,
-        active + [pltpu.VMEM((YN, ZN, SUB, PAY), F32)],
+        [
+            pltpu.SMEM((CN, ENTRIES + 1), jnp.int32),
+            pltpu.VMEM((CN * BLOCKS, TRACERS * SUB, LANES), F32),
+            pltpu.VMEM((YN, ZN, SUB, PAY), F32),
+        ],
         name="adjoint",
-    )(parts, both, footprints, mate, ids)
-
-    over_y = lax.all_to_all(dense, "y", 0, 0, tiled=True).astype(F32).sum(axis=0)
-    total = lax.all_to_all(over_y, "z", 0, 0, tiled=True).sum(axis=0)
-
-    total_both, total_other = neighbours(total, PAY)
+    )(parts, both, held, mate, ids)
+
+    over_y = lax.all_to_all(dense, "y", 0, 0, tiled=True)
+    coded = call(fold_y_kernel, shape(ZN, SUB, PAY + LANES, dtype=BF16), [VMEM], 2, name="fold_y")(over_y)
+    over_z = lax.all_to_all(coded, "z", 0, 0, tiled=True)
+    total = call(fold_z_kernel, shape(SUB, PAY), [VMEM], 2, name="fold_z")(over_z)
+
+    total_both, total_other = neighbours(total, total)
     gradient = call(final_kernel, shape(*control.shape), [VMEM] * 4, 2, name="final")(
         total_both, total_other, both, other
     )

time: 115 us -> 102 us (0.89); the launches traced: 113 us -> 102 us
  waiting for transfers between devices: 9.71 us -> 0.01 us
  blocking collectives: 67.6 us -> 76.8 us
  local copies, waits for them, and re-layouts: 6.31 us -> 0 us
  Pallas kernels: 9.75 us -> 7.33 us
  starting transfers between devices: 18.9 us -> 16.8 us
    all_to_all x2 -> x3, blocking collectives: 24.9 us -> 35 us  [the longest x1 16 us: shards(): over_z = lax.all_to_all(coded, 'z', 0, 0, tiled=True)]
    all_to_all x1 -> x0, starting transfers between devices: 7.15 us -> none  [shards(): panels = lax.all_to_all(copies, 'y', 0, 0, tiled=True)]
    all_to_all x1 -> x0, waiting for transfers between devices: 6.58 us -> none  [shards(): panels = lax.all_to_all(copies, 'y', 0, 0, tiled=True)]
    unnamed x16 -> x0, local copies, waits for them, and re-layouts: 6.31 us -> none
    all_gather x2, blocking collectives: 10.2 us -> 6.28 us  [neighbours(): return (lax.all_gather(own, 'c'), other)]
    all_to_all x1, blocking collectives: 21.2 us -> 24.9 us  [shards(): by_z = lax.all_to_all(flux, 'z', 0, 0, tiled=True)]
    ppermute x1, starting transfers between devices: 2.25 us -> 5.95 us  [shards(): mate = lax.ppermute(footprints, 'c', [(0, 1), (1, 0)])]
    ppermute x2, waiting for transfers between devices: 3.13 us -> 0.01 us  [neighbours(): other = lax.ppermute(head, OBS, pairs + [(b, a) for a, b in pairs])]
  transfers between devices with their start and end apart: 4 -> 3, of which waited for: 2 -> 0; matrix products, arithmetic and copies ran while one was open for 0% -> 0% of each run, Pallas kernels for 1% -> 0%
where the time goes in v5:
time: 102 us
  blocking collectives  76.8 us (75%)
  starting transfers between devices  16.8 us (16%)
  Pallas kernels  7.33 us (7%)
    all_to_all x1, blocking collectives, shards(): by_z = lax.all_to_all(flux, 'z', 0, 0, tiled=True)  24.9 us
    all_to_all x1, blocking collectives, shards(): over_z = lax.all_to_all(coded, 'z', 0, 0, tiled=True)  16 us
    ppermute x2, starting transfers between devices, neighbours(): other = lax.ppermute(head, OBS, pairs + [(b, a) for a, b in pairs])  10.8 us
    all_to_all x1, blocking collectives, shards(): parts = lax.all_to_all(part, ('tm', 'c'), 0, 0, tiled=True)  10.6 us
    all_to_all x1, blocking collectives, shards(): panels = lax.all_to_all(copies, 'y', 0, 0, tiled=True)  10.3 us
    all_to_all x1, blocking collectives, shards(): over_y = lax.all_to_all(dense, 'y', 0, 0, tiled=True)  8.64 us
    all_gather x2, blocking collectives, neighbours(): return (lax.all_gather(own, 'c'), other)  6.28 us
    ppermute x1, starting transfers between devices, shards(): mate = lax.ppermute(footprints, 'c', [(0, 1), (1, 0)])  5.95 us
  transfers between devices with their start and end apart: 3, of which 0 were waited for; matrix products, arithmetic and copies ran while one was open for 0% of the time, Pallas kernels for 0%

profile of v5, /device:TPU:1, one launch (start us, length us, event | category | flops | bytes accessed | tf_op | source)
XLA Modules:
  0.0 101.6 jit_solution(7699193203582913713)
XLA Ops:
  0.6 0.9 pack.1
  1.5 4.6 %collective-permute-start = (f32[8,512]{1,0:T(8,128)S(1)}, f32[8,512]{1,0:T(8,128)S(1)}, u32[]{:S(2)}, u32[]{:S(2)}) collective-permute-start(f32[8,512]{1,0:T(8,128)S(1)} %get-tuple-element.13), channel_id=1, source_target_pairs={{1,2},{3,4},{5,6},{7,8},{9,10},{11,12},{13,14},{15,16},{17,18},{19... | collective-permute-start | bytes 49160 | tf_op jit(solution)/shard_map/ppermute | solution.py:319
  6.1 4.5 %all-gather = f32[16,1024]{1,0:T(8,128)S(1)} all-gather(f32[8,1024]{1,0:T(8,128)S(1)} %get-tuple-element.12), channel_id=2, replica_groups=mesh['tm'=4,'z'=16,'y'=4,'c'=2] {'c'}, dimensions={0}, use_global_device_ids=true | all-gather | bytes 98304 | tf_op jit(solution)/shard_map/all_gather | solution.py:320
  10.6 0.0 collective-permute-done.other
  10.6 0.2 flux.1
  10.8 24.9 %all_to_all.25.source = bf16[16,8,384]{2,1,0:T(8,128)(2,1)S(1)} all-to-all(bf16[16,8,384]{2,1,0:T(8,128)(2,1)S(1)} %get-tuple-element.14), channel_id=1, replica_groups=mesh['tm'=4,'z'=16,'y'=4,'c'=2] {'z'}, dimensions={0} | all-to-all | bytes 196608 | tf_op jit(solution)/shard_map/all_to_all | solution.py:342
  35.7 5.9 %collective-permute-start.1 = (bf16[4,4,128,1024]{3,2,1,0:T(8,128)(2,1)}, bf16[4,4,128,1024]{3,2,1,0:T(8,128)(2,1)S(1)}, u32[]{:S(2)}, u32[]{:S(2)}) collective-permute-start(bf16[4,4,128,1024]{3,2,1,0:T(8,128)(2,1)} %own), channel_id=1, source_target_pairs={{0,1},{1,0},{2,3},{3,2},{4,5},{5,4},{6,7},{7,6},{8,9},{9,8},{10,11... | collective-permute-start | bytes 12582920 | tf_op jit(solution)/shard_map/ppermute | solution.py:344
  41.7 10.3 %all_to_all.26.panels = bf16[4,16,8,384]{3,2,1,0:T(8,128)(2,1)S(1)} all-to-all(bf16[4,16,8,384]{3,2,1,0:T(8,128)(2,1)S(1)} %copies.1), channel_id=1, replica_groups=mesh['tm'=4,'z'=16,'y'=4,'c'=2] {'y'}, dimensions={0} | all-to-all | bytes 786432 | tf_op jit(solution)/shard_map/all_to_all | solution.py:346
  52.0 0.0 collective-permute-done.1.mate
  52.0 2.9 %predict.1 = (f32[8,24,128]{2,1,0:T(8,128)S(1)}, bf16[4,4,128,1024]{3,2,1,0:T(8,128)(2,1)S(1)}) custom-call(bf16[4,16,8,384]{3,2,1,0:T(8,128)(2,1)S(1)} %all_to_all.26.panels, bf16[4,4,128,1024]{3,2,1,0:T(8,128)(2,1)} %own, bf16[4,4,128,1024]{3,2,1,0:T(8,128)(2,1)S(1)} %collective-permute-done.1.mate, s32[2,4,128]{2,1,0:T(4,128)S(1)} %get-tuple-element.17.ids), custom_call_target="tpu_custom_call" | custom-call | tf_op jit(solution)/shard_map/predict/pallas_call | solution.py:349
  54.9 10.6 %all_to_all.27.parts = f32[8,24,128]{2,1,0:T(8,128)S(1)} all-to-all(f32[8,24,128]{2,1,0:T(8,128)S(1)} %get-tuple-element.18), channel_id=1, replica_groups=mesh['tm'=4,'z'=16,'y'=4,'c'=2] {'tm','c'}, dimensions={0} | all-to-all | bytes 196608 | tf_op jit(solution)/shard_map/all_to_all | solution.py:361
  65.6 2.3 %adjoint.1 = (f32[3,512]{1,0:T(4,128)}, bf16[4,16,8,384]{3,2,1,0:T(8,128)(2,1)S(1)}) custom-call(f32[8,24,128]{2,1,0:T(8,128)S(1)} %all_to_all.27.parts, f32[2,8,1024]{2,1,0:T(8,128)S(1)} %bitcast.4, bf16[4,4,128,1024]{3,2,1,0:T(8,128)(2,1)S(1)} %get-tuple-element.19.held, bf16[4,4,128,1024]{3,2,1,0:T(8,128)(2,1)S(1)} %collective-permute-done.1.mate, ...), custom_call_target="tpu_custom_call" | custom-call | tf_op jit(solution)/shard_map/adjoint/pallas_call | solution.py:362
  67.8 8.6 %all_to_all.28.parts = bf16[4,16,8,384]{3,2,1,0:T(8,128)(2,1)S(1)} all-to-all(bf16[4,16,8,384]{3,2,1,0:T(8,128)(2,1)S(1)} %get-tuple-element.20), channel_id=1, replica_groups=mesh['tm'=4,'z'=16,'y'=4,'c'=2] {'y'}, dimensions={0} | all-to-all | bytes 786432 | tf_op jit(solution)/shard_map/all_to_all | solution.py:375
  76.5 0.2 fold_y.1
  76.6 16.0 %all_to_all.29.parts = bf16[16,8,512]{2,1,0:T(8,128)(2,1)S(1)} all-to-all(bf16[16,8,512]{2,1,0:T(8,128)(2,1)S(1)} %fold_y.1), channel_id=1, replica_groups=mesh['tm'=4,'z'=16,'y'=4,'c'=2] {'z'}, dimensions={0} | all-to-all | bytes 262144 | tf_op jit(solution)/shard_map/all_to_all | solution.py:377
  92.6 0.1 fold_z.1
  92.7 6.2 %collective-permute-start.2 = (f32[8,384]{1,0:T(8,128)S(1)}, f32[8,384]{1,0:T(8,128)S(1)}, u32[]{:S(2)}, u32[]{:S(2)}) collective-permute-start(f32[8,384]{1,0:T(8,128)S(1)} %fold_z.1), channel_id=1, source_target_pairs={{1,2},{3,4},{5,6},{7,8},{9,10},{11,12},{13,14},{15,16},{17,18},{19... | collective-permute-start | bytes 36872 | tf_op jit(solution)/shard_map/ppermute | solution.py:319
  98.9 1.8 %all-gather.1 = f32[16,384]{1,0:T(8,128)S(1)} all-gather(f32[8,384]{1,0:T(8,128)S(1)} %fold_z.1), channel_id=3, replica_groups=mesh['tm'=4,'z'=16,'y'=4,'c'=2] {'c'}, dimensions={0}, use_global_device_ids=true | all-gather | bytes 36864 | tf_op jit(solution)/shard_map/all_gather | solution.py:320
  100.8 0.0 collective-permute-done.2.total_other
  100.8 0.8 final.1
  (1 shorter events, 0.0 us)
Async XLA Ops:
  1.5 9.1 %collective-permute-start = (f32[8,512]{1,0:T(8,128)S(1)}, f32[8,512]{1,0:T(8,128)S(1)}, u32[]{:S(2)}, u32[]{:S(2)}) collective-permute-start(f32[8,512]{1,0:T(8,128)S(1)} %get-tuple-element.13), channel_id=1, source_target_pairs={{1,2},{3,4},{5,6},{7,8},{9,10},{11,12},{13,14},{15,16},{17,18},{19... | collective-permute-start | bytes 49160 | tf_op jit(solution)/shard_map/ppermute | solution.py:319
  35.7 16.3 %collective-permute-start.1 = (bf16[4,4,128,1024]{3,2,1,0:T(8,128)(2,1)}, bf16[4,4,128,1024]{3,2,1,0:T(8,128)(2,1)S(1)}, u32[]{:S(2)}, u32[]{:S(2)}) collective-permute-start(bf16[4,4,128,1024]{3,2,1,0:T(8,128)(2,1)} %own), channel_id=1, source_target_pairs={{0,1},{1,0},{2,3},{3,2},{4,5},{5,4},{6,7},{7,6},{8,9},{9,8},{10,11... | collective-permute-start | bytes 12582920 | tf_op jit(solution)/shard_map/ppermute | solution.py:344
  92.7 8.1 %collective-permute-start.2 = (f32[8,384]{1,0:T(8,128)S(1)}, f32[8,384]{1,0:T(8,128)S(1)}, u32[]{:S(2)}, u32[]{:S(2)}) collective-permute-start(f32[8,384]{1,0:T(8,128)S(1)} %fold_z.1), channel_id=1, source_target_pairs={{1,2},{3,4},{5,6},{7,8},{9,10},{11,12},{13,14},{15,16},{17,18},{19... | collective-permute-start | bytes 36872 | tf_op jit(solution)/shard_map/ppermute | solution.py:319

commit v6 on v5

--- a/solution.py
+++ b/solution.py
@@ -30,7 +30,7 @@
         body,
         out_shape=out,
         in_specs=ins,
-        out_specs=jax.tree.map(lambda _: VMEM, out),
+        out_specs=jax.tree.map(lambda o: SMEM if getattr(o, "memory_space", None) == pltpu.SMEM else VMEM, out),
         scratch_shapes=list(scratch),
         compiler_params=pltpu.CompilerParams(vmem_limit_bytes=mib * MIB),
         name=name,
@@ -144,9 +144,12 @@
     return row == lane // LANES
 
 
-def copies_kernel(source, out):
+def copies_kernel(source, listed, out, ids, sem):
+    copy = pltpu.make_async_copy(listed, ids, sem)
+    copy.start()
     for y in range(YN):
         out[y] = source[...]
+    copy.wait()
 
 
 STEP = 4
@@ -220,7 +223,7 @@
         out[peer] = whole
 
 
-def adjoint_kernel(parts, both, held, mate, ids, residual, out, order, lefts, sums):
+def adjoint_kernel(parts, both, held, mate, ids, misfits, out, order, lefts, sums):
     core = lax.axis_index("c")
     count = list_active(ids, order, 0, core, core)
     count_mate = list_active(ids, order, 1, core, 1 - core)
@@ -238,10 +241,7 @@
         return jnp.concatenate(rows, axis=0)
 
     misfit = (whole - seen(0)) * seen(1)
-    for t in range(TRACERS):
-        for b in range(BLOCKS):
-            first, second = (misfit[t * SUB + c * BLOCKS + b : t * SUB + c * BLOCKS + b + 1] for c in range(CN))
-            residual[t : t + 1, b * SIGHTS : (b + 1) * SIGHTS] = jnp.where(core == 0, first, second)
+    misfits[...] = misfit
     for b in range(CN * BLOCKS):
         lefts[b] = jnp.concatenate(
             [jnp.broadcast_to(misfit[t * SUB + b : t * SUB + b + 1], (SUB, SIGHTS)) for t in range(TRACERS)], axis=0
@@ -279,13 +279,13 @@
         value = parts[0, z].astype(F32)
         for y in range(1, YN):
             value = value + parts[y, z].astype(F32)
-        high = value.astype(BF16)
-        near = high.astype(F32)
+        wide = value * 65537.0
+        near = wide - (wide - value)
         size = jnp.abs(near)
         part = (value - near) * (FINE / jnp.where(size == 0.0, 1.0, size))
         level = jnp.clip(jnp.floor((part + 1.0) * (LEVELS / 2)), 0.0, LEVELS - 1.0)
         code = block(level, 0) + LEVELS * block(level, 1) + LEVELS * LEVELS * block(level, 2)
-        out[z, :, :PAY] = high
+        out[z, :, :PAY] = near.astype(BF16)
         out[z, :, PAY:] = code.astype(BF16)
 
 
@@ -304,8 +304,12 @@
     out[...] = total
 
 
-def final_kernel(total_both, total_other, both, other, out):
+def final_kernel(total_both, total_other, both, other, misfits, out, residual):
     core, here = lax.axis_index("c"), lax.axis_index(OBS)
+    for t in range(TRACERS):
+        for b in range(BLOCKS):
+            first, second = (misfits[at : at + 1] for at in (t * SUB + b, t * SUB + BLOCKS + b))
+            residual[t : t + 1, b * SIGHTS : (b + 1) * SIGHTS] = jnp.where(core == 0, first, second)
     sweeps = Sweeps(around(both, other, core, TRACERS), here)
     for t in range(TRACERS):
         value = both[core, :, t * LANES : (t + 1) * LANES] + sweeps.twice(around(total_both, total_other, core, t))
@@ -318,6 +322,36 @@
     pairs = [(i, i + 1) for i in range(1, TILES - 1, 2)]
     other = lax.ppermute(head, OBS, pairs + [(b, a) for a, b in pairs])
     return lax.all_gather(own, "c"), other
+
+
+def run_predict(panels, footprints, mate, ids, peers):
+    return call(
+        predict_kernel,
+        (shape(peers, TRACERS * SUB, LANES), pltpu.VMEM(footprints.shape, BF16)),
+        [VMEM, HBM, VMEM, SMEM],
+        16,
+        [
+            pltpu.SMEM((CN, ENTRIES + 1), jnp.int32),
+            pltpu.SemaphoreType.DMA((ENTRIES,)),
+            pltpu.VMEM((CN * BLOCKS, TRACERS * SUB, LANES), F32),
+        ],
+        name="predict",
+    )(panels, in_hbm(footprints), mate, ids)
+
+
+def run_adjoint(parts, both, held, mate, ids):
+    return call(
+        adjoint_kernel,
+        (shape(TRACERS * SUB, SIGHTS), shape(YN, ZN, SUB, PAY, dtype=BF16)),
+        [VMEM] * 4 + [SMEM],
+        16,
+        [
+            pltpu.SMEM((CN, ENTRIES + 1), jnp.int32),
+            pltpu.VMEM((CN * BLOCKS, TRACERS * SUB, LANES), F32),
+            pltpu.VMEM((YN, ZN, SUB, PAY), F32),
+        ],
+        name="adjoint",
+    )(parts, both, held, mate, ids)
 
 
 def shards(control, diffusivity, footprints, tile_lists, tile_counts, measured, weight):
@@ -331,7 +365,7 @@
         name="pack",
     )(*map(in_hbm, given))
     both, other = neighbours(own, head)
-    flux, ids = call(
+    flux, listed = call(
         flux_kernel,
         (shape(ZN, SUB, PAY, dtype=BF16), shape(CN, BLOCKS, LANES, dtype=jnp.int32)),
         [VMEM] * 2,
@@ -342,35 +376,19 @@
     by_z = lax.all_to_all(flux, "z", 0, 0, tiled=True)
     by_z, footprints = lax.optimization_barrier((by_z, footprints))
     mate = lax.ppermute(footprints, "c", [(0, 1), (1, 0)])
-    copies = call(copies_kernel, shape(YN, *by_z.shape, dtype=BF16), [VMEM], 2, name="copies")(by_z)
+    copies, ids = call(
+        copies_kernel,
+        (shape(YN, *by_z.shape, dtype=BF16), pltpu.SMEM(listed.shape, jnp.int32)),
+        [VMEM] * 2,
+        2,
+        [pltpu.SemaphoreType.DMA],
+        name="copies",
+    )(by_z, listed)
     panels = lax.all_to_all(copies, "y", 0, 0, tiled=True)
 
-    peers = lax.axis_size("tm") * CN
-    part, held = call(
-        predict_kernel,
-        (shape(peers, TRACERS * SUB, LANES), pltpu.VMEM(footprints.shape, BF16)),
-        [VMEM, HBM, VMEM, SMEM],
-        16,
-        [
-            pltpu.SMEM((CN, ENTRIES + 1), jnp.int32),
-            pltpu.SemaphoreType.DMA((ENTRIES,)),
-            pltpu.VMEM((CN * BLOCKS, TRACERS * SUB, LANES), F32),
-        ],
-        name="predict",
-    )(panels, in_hbm(footprints), mate, ids)
+    part, held = run_predict(panels, footprints, mate, ids, lax.axis_size("tm") * CN)
     parts = lax.all_to_all(part, ("tm", "c"), 0, 0, tiled=True)
-    residual, dense = call(
-        adjoint_kernel,
-        (shape(TRACERS, BLOCKS * SIGHTS), shape(YN, ZN, SUB, PAY, dtype=BF16)),
-        [VMEM] * 4 + [SMEM],
-        16,
-        [
-            pltpu.SMEM((CN, ENTRIES + 1), jnp.int32),
-            pltpu.VMEM((CN * BLOCKS, TRACERS * SUB, LANES), F32),
-            pltpu.VMEM((YN, ZN, SUB, PAY), F32),
-        ],
-        name="adjoint",
-    )(parts, both, held, mate, ids)
+    misfits, dense = run_adjoint(parts, both, held, mate, ids)
 
     over_y = lax.all_to_all(dense, "y", 0, 0, tiled=True)
     coded = call(fold_y_kernel, shape(ZN, SUB, PAY + LANES, dtype=BF16), [VMEM], 2, name="fold_y")(over_y)
@@ -378,10 +396,13 @@
     total = call(fold_z_kernel, shape(SUB, PAY), [VMEM], 2, name="fold_z")(over_z)
 
     total_both, total_other = neighbours(total, total)
-    gradient = call(final_kernel, shape(*control.shape), [VMEM] * 4, 2, name="final")(
-        total_both, total_other, both, other
-    )
-    return gradient, residual
+    return call(
+        final_kernel,
+        (shape(*control.shape), shape(TRACERS, BLOCKS * SIGHTS)),
+        [VMEM] * 5,
+        2,
+        name="final",
+    )(total_both, total_other, both, other, misfits)
 
 
 def solution(mesh):

time: 102 us -> 102 us (level); the launches traced: 102 us -> 100 us
  Pallas kernels: 7.33 us -> 6.15 us
    pallas_call x4, Pallas kernels: 6.01 us -> 4.82 us  [the longest x1 2.32 us: run_predict(): call(predict_kernel, (shape(peers, TRACERS * SUB, LANES), pltpu.VMEM(foot...]
    all_to_all x1, blocking collectives: 8.64 us -> 9.71 us  [shards(): over_y = lax.all_to_all(dense, 'y', 0, 0, tiled=True)]
  transfers between devices with their start and end apart: 3 -> 3, of which waited for: 0 -> 0; matrix products, arithmetic and copies ran while one was open for 0% -> 0% of each run, Pallas kernels for 0% -> 1%
where the time goes in v6:
time: 102 us; the launch traced here: 100 us
  blocking collectives  77.1 us (76%)
  starting transfers between devices  16.2 us (16%)
  Pallas kernels  6.15 us (6%)
    all_to_all x1, blocking collectives, shards(): by_z = lax.all_to_all(flux, 'z', 0, 0, tiled=True)  24.9 us
    all_to_all x1, blocking collectives, shards(): over_z = lax.all_to_all(coded, 'z', 0, 0, tiled=True)  15.7 us
    all_to_all x1, blocking collectives, shards(): panels = lax.all_to_all(copies, 'y', 0, 0, tiled=True)  10.3 us
    ppermute x2, starting transfers between devices, neighbours(): other = lax.ppermute(head, OBS, pairs + [(b, a) for a, b in pairs])  10.3 us
    all_to_all x1, blocking collectives, shards(): parts = lax.all_to_all(part, ('tm', 'c'), 0, 0, tiled=True)  10.2 us
    all_to_all x1, blocking collectives, shards(): over_y = lax.all_to_all(dense, 'y', 0, 0, tiled=True)  9.71 us
    all_gather x2, blocking collectives, neighbours(): return (lax.all_gather(own, 'c'), other)  6.28 us
    ppermute x1, starting transfers between devices, shards(): mate = lax.ppermute(footprints, 'c', [(0, 1), (1, 0)])  5.95 us
  transfers between devices with their start and end apart: 3, of which 0 were waited for; matrix products, arithmetic and copies ran while one was open for 0% of the time, Pallas kernels for 1%

profile of v6, /device:TPU:1, one launch (start us, length us, event | category | flops | bytes accessed | tf_op | source)
XLA Modules:
  0.0 100.2 jit_solution(18231741217148931251)
XLA Ops:
  0.6 0.9 pack.1
  1.5 4.6 %collective-permute-start = (f32[8,512]{1,0:T(8,128)S(1)}, f32[8,512]{1,0:T(8,128)S(1)}, u32[]{:S(2)}, u32[]{:S(2)}) collective-permute-start(f32[8,512]{1,0:T(8,128)S(1)} %get-tuple-element.15), channel_id=1, source_target_pairs={{1,2},{3,4},{5,6},{7,8},{9,10},{11,12},{13,14},{15,16},{17,18},{19... | collective-permute-start | bytes 49160 | tf_op jit(solution)/shard_map/ppermute | solution.py:323
  6.1 4.5 %all-gather = f32[16,1024]{1,0:T(8,128)S(1)} all-gather(f32[8,1024]{1,0:T(8,128)S(1)} %get-tuple-element.14), channel_id=2, replica_groups=mesh['tm'=4,'z'=16,'y'=4,'c'=2] {'c'}, dimensions={0}, use_global_device_ids=true | all-gather | bytes 98304 | tf_op jit(solution)/shard_map/all_gather | solution.py:324
  10.6 0.0 collective-permute-done.other
  10.6 0.2 flux.1
  10.8 24.9 %all_to_all.25.source = bf16[16,8,384]{2,1,0:T(8,128)(2,1)S(1)} all-to-all(bf16[16,8,384]{2,1,0:T(8,128)(2,1)S(1)} %get-tuple-element.16), channel_id=1, replica_groups=mesh['tm'=4,'z'=16,'y'=4,'c'=2] {'z'}, dimensions={0} | all-to-all | bytes 196608 | tf_op jit(solution)/shard_map/all_to_all | solution.py:376
  35.7 5.9 %collective-permute-start.1 = (bf16[4,4,128,1024]{3,2,1,0:T(8,128)(2,1)}, bf16[4,4,128,1024]{3,2,1,0:T(8,128)(2,1)S(1)}, u32[]{:S(2)}, u32[]{:S(2)}) collective-permute-start(bf16[4,4,128,1024]{3,2,1,0:T(8,128)(2,1)} %own), channel_id=1, source_target_pairs={{0,1},{1,0},{2,3},{3,2},{4,5},{5,4},{6,7},{7,6},{8,9},{9,8},{10,11... | collective-permute-start | bytes 12582920 | tf_op jit(solution)/shard_map/ppermute | solution.py:378
  41.6 0.6 copies.1
  42.2 10.3 %all_to_all.26.panels = bf16[4,16,8,384]{3,2,1,0:T(8,128)(2,1)S(1)} all-to-all(bf16[4,16,8,384]{3,2,1,0:T(8,128)(2,1)S(1)} %get-tuple-element.19), channel_id=1, replica_groups=mesh['tm'=4,'z'=16,'y'=4,'c'=2] {'y'}, dimensions={0} | all-to-all | bytes 786432 | tf_op jit(solution)/shard_map/all_to_all | solution.py:387
  52.6 0.0 collective-permute-done.1.mate
  52.6 2.3 %predict.1 = (f32[8,24,128]{2,1,0:T(8,128)S(1)}, bf16[4,4,128,1024]{3,2,1,0:T(8,128)(2,1)S(1)}) custom-call(bf16[4,16,8,384]{3,2,1,0:T(8,128)(2,1)S(1)} %all_to_all.26.panels, bf16[4,4,128,1024]{3,2,1,0:T(8,128)(2,1)} %own, bf16[4,4,128,1024]{3,2,1,0:T(8,128)(2,1)S(1)} %collective-permute-done.1.mate, s32[2,4,128]{2,1,0:T(4,128)S(4)} %get-tuple-element.21.ids), custom_call_target="tpu_custom_call" | custom-call | tf_op jit(solution)/shard_map/predict/pallas_call | solution.py:328
  54.9 10.2 %all_to_all.27.parts = f32[8,24,128]{2,1,0:T(8,128)S(1)} all-to-all(f32[8,24,128]{2,1,0:T(8,128)S(1)} %get-tuple-element.22), channel_id=1, replica_groups=mesh['tm'=4,'z'=16,'y'=4,'c'=2] {'tm','c'}, dimensions={0} | all-to-all | bytes 196608 | tf_op jit(solution)/shard_map/all_to_all | solution.py:390
  65.1 1.1 %adjoint.1 = (f32[24,128]{1,0:T(8,128)S(1)}, bf16[4,16,8,384]{3,2,1,0:T(8,128)(2,1)S(1)}) custom-call(f32[8,24,128]{2,1,0:T(8,128)S(1)} %all_to_all.27.parts, f32[2,8,1024]{2,1,0:T(8,128)S(1)} %bitcast.4, bf16[4,4,128,1024]{3,2,1,0:T(8,128)(2,1)S(1)} %get-tuple-element.23.held, bf16[4,4,128,1024]{3,2,1,0:T(8,128)(2,1)S(1)} %collective-permute-done.1.mate, ...), custom_call_target="tpu_custom_call" | custom-call | tf_op jit(solution)/shard_map/adjoint/pallas_call | solution.py:343
  66.2 9.7 %all_to_all.28.parts = bf16[4,16,8,384]{3,2,1,0:T(8,128)(2,1)S(1)} all-to-all(bf16[4,16,8,384]{3,2,1,0:T(8,128)(2,1)S(1)} %get-tuple-element.24), channel_id=1, replica_groups=mesh['tm'=4,'z'=16,'y'=4,'c'=2] {'y'}, dimensions={0} | all-to-all | bytes 786432 | tf_op jit(solution)/shard_map/all_to_all | solution.py:393
  75.9 0.2 fold_y.1
  76.0 15.7 %all_to_all.29.parts = bf16[16,8,512]{2,1,0:T(8,128)(2,1)S(1)} all-to-all(bf16[16,8,512]{2,1,0:T(8,128)(2,1)S(1)} %fold_y.1), channel_id=1, replica_groups=mesh['tm'=4,'z'=16,'y'=4,'c'=2] {'z'}, dimensions={0} | all-to-all | bytes 262144 | tf_op jit(solution)/shard_map/all_to_all | solution.py:395
  91.8 0.1 fold_z.1
  91.8 5.7 %collective-permute-start.2 = (f32[8,384]{1,0:T(8,128)S(1)}, f32[8,384]{1,0:T(8,128)S(1)}, u32[]{:S(2)}, u32[]{:S(2)}) collective-permute-start(f32[8,384]{1,0:T(8,128)S(1)} %fold_z.1), channel_id=1, source_target_pairs={{1,2},{3,4},{5,6},{7,8},{9,10},{11,12},{13,14},{15,16},{17,18},{19... | collective-permute-start | bytes 36872 | tf_op jit(solution)/shard_map/ppermute | solution.py:323
  97.6 1.8 %all-gather.1 = f32[16,384]{1,0:T(8,128)S(1)} all-gather(f32[8,384]{1,0:T(8,128)S(1)} %fold_z.1), channel_id=3, replica_groups=mesh['tm'=4,'z'=16,'y'=4,'c'=2] {'c'}, dimensions={0}, use_global_device_ids=true | all-gather | bytes 36864 | tf_op jit(solution)/shard_map/all_gather | solution.py:324
  99.4 0.0 collective-permute-done.2.total_other
  99.4 0.8 final.1
Async XLA Ops:
  1.5 9.1 %collective-permute-start = (f32[8,512]{1,0:T(8,128)S(1)}, f32[8,512]{1,0:T(8,128)S(1)}, u32[]{:S(2)}, u32[]{:S(2)}) collective-permute-start(f32[8,512]{1,0:T(8,128)S(1)} %get-tuple-element.15), channel_id=1, source_target_pairs={{1,2},{3,4},{5,6},{7,8},{9,10},{11,12},{13,14},{15,16},{17,18},{19... | collective-permute-start | bytes 49160 | tf_op jit(solution)/shard_map/ppermute | solution.py:323
  35.7 16.9 %collective-permute-start.1 = (bf16[4,4,128,1024]{3,2,1,0:T(8,128)(2,1)}, bf16[4,4,128,1024]{3,2,1,0:T(8,128)(2,1)S(1)}, u32[]{:S(2)}, u32[]{:S(2)}) collective-permute-start(bf16[4,4,128,1024]{3,2,1,0:T(8,128)(2,1)} %own), channel_id=1, source_target_pairs={{0,1},{1,0},{2,3},{3,2},{4,5},{5,4},{6,7},{7,6},{8,9},{9,8},{10,11... | collective-permute-start | bytes 12582920 | tf_op jit(solution)/shard_map/ppermute | solution.py:378
  91.8 7.5 %collective-permute-start.2 = (f32[8,384]{1,0:T(8,128)S(1)}, f32[8,384]{1,0:T(8,128)S(1)}, u32[]{:S(2)}, u32[]{:S(2)}) collective-permute-start(f32[8,384]{1,0:T(8,128)S(1)} %fold_z.1), channel_id=1, source_target_pairs={{1,2},{3,4},{5,6},{7,8},{9,10},{11,12},{13,14},{15,16},{17,18},{19... | collective-permute-start | bytes 36872 | tf_op jit(solution)/shard_map/ppermute | solution.py:323

commit v7 on v6

--- a/solution.py
+++ b/solution.py
@@ -270,7 +270,7 @@
     out[...] = sums[...].astype(BF16)
 
 
-LEVELS = 6
+LEVELS, SPACING = 5, 0.4
 FINE = 256.0
 
 
@@ -282,8 +282,8 @@
         wide = value * 65537.0
         near = wide - (wide - value)
         size = jnp.abs(near)
-        part = (value - near) * (FINE / jnp.where(size == 0.0, 1.0, size))
-        level = jnp.clip(jnp.floor((part + 1.0) * (LEVELS / 2)), 0.0, LEVELS - 1.0)
+        part = (value - near) * (FINE / SPACING / jnp.where(size == 0.0, 1.0, size))
+        level = jnp.clip(jnp.floor(part + LEVELS / 2), 0.0, LEVELS - 1.0)
         code = block(level, 0) + LEVELS * block(level, 1) + LEVELS * LEVELS * block(level, 2)
         out[z, :, :PAY] = near.astype(BF16)
         out[z, :, PAY:] = code.astype(BF16)
@@ -298,8 +298,8 @@
         code = code - LEVELS * LEVELS * third
         second = jnp.floor((code + 0.5) * (1.0 / LEVELS))
         level = jnp.concatenate([code - LEVELS * second, second, third], axis=1)
-        part = (level + 0.5) * (2.0 / LEVELS) - 1.0
-        value = near + jnp.abs(near) * (part * (1.0 / FINE))
+        part = (level - LEVELS // 2) * (SPACING / FINE)
+        value = near + jnp.abs(near) * part
         total = value if total is None else total + value
     out[...] = total
 

time: 102 us -> 101 us (level); the launches traced: 100 us -> 100 us
  no operation moved by 1% of the time
where the time goes in v7:
time: 101 us; the launch traced here: 100 us
  blocking collectives  76.3 us (76%)
  starting transfers between devices  16.4 us (16%)
  Pallas kernels  6.88 us (7%)
    all_to_all x1, blocking collectives, shards(): by_z = lax.all_to_all(flux, 'z', 0, 0, tiled=True)  24.9 us
    all_to_all x1, blocking collectives, shards(): over_z = lax.all_to_all(coded, 'z', 0, 0, tiled=True)  15 us
    ppermute x2, starting transfers between devices, neighbours(): other = lax.ppermute(head, OBS, pairs + [(b, a) for a, b in pairs])  10.4 us
    all_to_all x1, blocking collectives, shards(): panels = lax.all_to_all(copies, 'y', 0, 0, tiled=True)  10.3 us
    all_to_all x1, blocking collectives, shards(): over_y = lax.all_to_all(dense, 'y', 0, 0, tiled=True)  10 us
    all_to_all x1, blocking collectives, shards(): parts = lax.all_to_all(part, ('tm', 'c'), 0, 0, tiled=True)  9.7 us
    all_gather x2, blocking collectives, neighbours(): return (lax.all_gather(own, 'c'), other)  6.28 us
    ppermute x1, starting transfers between devices, shards(): mate = lax.ppermute(footprints, 'c', [(0, 1), (1, 0)])  5.95 us
  transfers between devices with their start and end apart: 3, of which 0 were waited for; matrix products, arithmetic and copies ran while one was open for 0% of the time, Pallas kernels for 1%

profile of v7, /device:TPU:1, one launch (start us, length us, event | category | flops | bytes accessed | tf_op | source)
XLA Modules:
  0.0 100.2 jit_solution(231681822797724535)
XLA Ops:
  0.6 0.9 pack.1
  1.5 4.6 %collective-permute-start = (f32[8,512]{1,0:T(8,128)S(1)}, f32[8,512]{1,0:T(8,128)S(1)}, u32[]{:S(2)}, u32[]{:S(2)}) collective-permute-start(f32[8,512]{1,0:T(8,128)S(1)} %get-tuple-element.15), channel_id=1, source_target_pairs={{1,2},{3,4},{5,6},{7,8},{9,10},{11,12},{13,14},{15,16},{17,18},{19... | collective-permute-start | bytes 49160 | tf_op jit(solution)/shard_map/ppermute | solution.py:323
  6.1 4.5 %all-gather = f32[16,1024]{1,0:T(8,128)S(1)} all-gather(f32[8,1024]{1,0:T(8,128)S(1)} %get-tuple-element.14), channel_id=2, replica_groups=mesh['tm'=4,'z'=16,'y'=4,'c'=2] {'c'}, dimensions={0}, use_global_device_ids=true | all-gather | bytes 98304 | tf_op jit(solution)/shard_map/all_gather | solution.py:324
  10.6 0.0 collective-permute-done.other
  10.6 0.2 flux.1
  10.8 24.9 %all_to_all.25.source = bf16[16,8,384]{2,1,0:T(8,128)(2,1)S(1)} all-to-all(bf16[16,8,384]{2,1,0:T(8,128)(2,1)S(1)} %get-tuple-element.16), channel_id=1, replica_groups=mesh['tm'=4,'z'=16,'y'=4,'c'=2] {'z'}, dimensions={0} | all-to-all | bytes 196608 | tf_op jit(solution)/shard_map/all_to_all | solution.py:376
  35.7 5.9 %collective-permute-start.1 = (bf16[4,4,128,1024]{3,2,1,0:T(8,128)(2,1)}, bf16[4,4,128,1024]{3,2,1,0:T(8,128)(2,1)S(1)}, u32[]{:S(2)}, u32[]{:S(2)}) collective-permute-start(bf16[4,4,128,1024]{3,2,1,0:T(8,128)(2,1)} %own), channel_id=1, source_target_pairs={{0,1},{1,0},{2,3},{3,2},{4,5},{5,4},{6,7},{7,6},{8,9},{9,8},{10,11... | collective-permute-start | bytes 12582920 | tf_op jit(solution)/shard_map/ppermute | solution.py:378
  41.6 0.6 copies.1
  42.2 10.3 %all_to_all.26.panels = bf16[4,16,8,384]{3,2,1,0:T(8,128)(2,1)S(1)} all-to-all(bf16[4,16,8,384]{3,2,1,0:T(8,128)(2,1)S(1)} %get-tuple-element.19), channel_id=1, replica_groups=mesh['tm'=4,'z'=16,'y'=4,'c'=2] {'y'}, dimensions={0} | all-to-all | bytes 786432 | tf_op jit(solution)/shard_map/all_to_all | solution.py:387
  52.6 0.0 collective-permute-done.1.mate
  52.6 2.8 %predict.1 = (f32[8,24,128]{2,1,0:T(8,128)S(1)}, bf16[4,4,128,1024]{3,2,1,0:T(8,128)(2,1)S(1)}) custom-call(bf16[4,16,8,384]{3,2,1,0:T(8,128)(2,1)S(1)} %all_to_all.26.panels, bf16[4,4,128,1024]{3,2,1,0:T(8,128)(2,1)} %own, bf16[4,4,128,1024]{3,2,1,0:T(8,128)(2,1)S(1)} %collective-permute-done.1.mate, s32[2,4,128]{2,1,0:T(4,128)S(4)} %get-tuple-element.21.ids), custom_call_target="tpu_custom_call" | custom-call | tf_op jit(solution)/shard_map/predict/pallas_call | solution.py:328
  55.4 9.7 %all_to_all.27.parts = f32[8,24,128]{2,1,0:T(8,128)S(1)} all-to-all(f32[8,24,128]{2,1,0:T(8,128)S(1)} %get-tuple-element.22), channel_id=1, replica_groups=mesh['tm'=4,'z'=16,'y'=4,'c'=2] {'tm','c'}, dimensions={0} | all-to-all | bytes 196608 | tf_op jit(solution)/shard_map/all_to_all | solution.py:390
  65.1 1.4 %adjoint.1 = (f32[24,128]{1,0:T(8,128)S(1)}, bf16[4,16,8,384]{3,2,1,0:T(8,128)(2,1)S(1)}) custom-call(f32[8,24,128]{2,1,0:T(8,128)S(1)} %all_to_all.27.parts, f32[2,8,1024]{2,1,0:T(8,128)S(1)} %bitcast.4, bf16[4,4,128,1024]{3,2,1,0:T(8,128)(2,1)S(1)} %get-tuple-element.23.held, bf16[4,4,128,1024]{3,2,1,0:T(8,128)(2,1)S(1)} %collective-permute-done.1.mate, ...), custom_call_target="tpu_custom_call" | custom-call | tf_op jit(solution)/shard_map/adjoint/pallas_call | solution.py:343
  66.5 10.0 %all_to_all.28.parts = bf16[4,16,8,384]{3,2,1,0:T(8,128)(2,1)S(1)} all-to-all(bf16[4,16,8,384]{3,2,1,0:T(8,128)(2,1)S(1)} %get-tuple-element.24), channel_id=1, replica_groups=mesh['tm'=4,'z'=16,'y'=4,'c'=2] {'y'}, dimensions={0} | all-to-all | bytes 786432 | tf_op jit(solution)/shard_map/all_to_all | solution.py:393
  76.5 0.2 fold_y.1
  76.6 15.0 %all_to_all.29.parts = bf16[16,8,512]{2,1,0:T(8,128)(2,1)S(1)} all-to-all(bf16[16,8,512]{2,1,0:T(8,128)(2,1)S(1)} %fold_y.1), channel_id=1, replica_groups=mesh['tm'=4,'z'=16,'y'=4,'c'=2] {'z'}, dimensions={0} | all-to-all | bytes 262144 | tf_op jit(solution)/shard_map/all_to_all | solution.py:395
  91.7 0.1 fold_z.1
  91.8 5.9 %collective-permute-start.2 = (f32[8,384]{1,0:T(8,128)S(1)}, f32[8,384]{1,0:T(8,128)S(1)}, u32[]{:S(2)}, u32[]{:S(2)}) collective-permute-start(f32[8,384]{1,0:T(8,128)S(1)} %fold_z.1), channel_id=1, source_target_pairs={{1,2},{3,4},{5,6},{7,8},{9,10},{11,12},{13,14},{15,16},{17,18},{19... | collective-permute-start | bytes 36872 | tf_op jit(solution)/shard_map/ppermute | solution.py:323
  97.6 1.8 %all-gather.1 = f32[16,384]{1,0:T(8,128)S(1)} all-gather(f32[8,384]{1,0:T(8,128)S(1)} %fold_z.1), channel_id=3, replica_groups=mesh['tm'=4,'z'=16,'y'=4,'c'=2] {'c'}, dimensions={0}, use_global_device_ids=true | all-gather | bytes 36864 | tf_op jit(solution)/shard_map/all_gather | solution.py:324
  99.4 0.0 collective-permute-done.2.total_other
  99.4 0.8 final.1
Async XLA Ops:
  1.5 9.1 %collective-permute-start = (f32[8,512]{1,0:T(8,128)S(1)}, f32[8,512]{1,0:T(8,128)S(1)}, u32[]{:S(2)}, u32[]{:S(2)}) collective-permute-start(f32[8,512]{1,0:T(8,128)S(1)} %get-tuple-element.15), channel_id=1, source_target_pairs={{1,2},{3,4},{5,6},{7,8},{9,10},{11,12},{13,14},{15,16},{17,18},{19... | collective-permute-start | bytes 49160 | tf_op jit(solution)/shard_map/ppermute | solution.py:323
  35.7 16.9 %collective-permute-start.1 = (bf16[4,4,128,1024]{3,2,1,0:T(8,128)(2,1)}, bf16[4,4,128,1024]{3,2,1,0:T(8,128)(2,1)S(1)}, u32[]{:S(2)}, u32[]{:S(2)}) collective-permute-start(bf16[4,4,128,1024]{3,2,1,0:T(8,128)(2,1)} %own), channel_id=1, source_target_pairs={{0,1},{1,0},{2,3},{3,2},{4,5},{5,4},{6,7},{7,6},{8,9},{9,8},{10,11... | collective-permute-start | bytes 12582920 | tf_op jit(solution)/shard_map/ppermute | solution.py:378
  91.8 7.7 %collective-permute-start.2 = (f32[8,384]{1,0:T(8,128)S(1)}, f32[8,384]{1,0:T(8,128)S(1)}, u32[]{:S(2)}, u32[]{:S(2)}) collective-permute-start(f32[8,384]{1,0:T(8,128)S(1)} %fold_z.1), channel_id=1, source_target_pairs={{1,2},{3,4},{5,6},{7,8},{9,10},{11,12},{13,14},{15,16},{17,18},{19... | collective-permute-start | bytes 36872 | tf_op jit(solution)/shard_map/ppermute | solution.py:323

commit v8 on v7

--- a/solution.py
+++ b/solution.py
@@ -128,9 +128,7 @@
         return self.once(jnp.where(self.inside, self.once(v), 0.0))[SUB : 2 * SUB]
 
 
-def flux_kernel(both, other, out, ids):
-    for c in range(CN):
-        ids[c] = both[c, :BLOCKS, IDS * LANES : SEEN * LANES].astype(jnp.int32)
+def flux_kernel(both, other, out):
     core, here = lax.axis_index("c"), lax.axis_index(OBS)
     sweeps = Sweeps(around(both, other, core, TRACERS), here)
     half = jnp.concatenate([sweeps.twice(around(both, other, core, t)) for t in range(TRACERS)], axis=1).astype(BF16)
@@ -144,30 +142,33 @@
     return row == lane // LANES
 
 
-def copies_kernel(source, listed, out, ids, sem):
-    copy = pltpu.make_async_copy(listed, ids, sem)
-    copy.start()
+def copies_kernel(source, out):
     for y in range(YN):
         out[y] = source[...]
+
+
+def lists_kernel(both, ids, order, numbers, sem):
+    core = lax.axis_index("c")
+    for c in range(CN):
+        numbers[c] = both[c, :BLOCKS, IDS * LANES : SEEN * LANES].astype(jnp.int32)
+    copy = pltpu.make_async_copy(numbers, ids, sem)
+    copy.start()
     copy.wait()
+    for which, c in ((0, core), (1, 1 - core)):
+        count = jnp.int32(0)
+        for e in range(ENTRIES):
+            tile = ids[c, e // REFS, e % REFS]
+            order[which, count] = e
+            count = count + ((tile >= 0) & (tile % CN == core)).astype(jnp.int32)
+        order[which, ENTRIES] = count
 
 
 STEP = 4
 
 
-def list_active(ids, order, which, core, c, found=None):
-    count = jnp.int32(0)
-    for e in range(ENTRIES):
-        tile = ids[c, e // REFS, e % REFS]
-        active = (tile >= 0) & (tile % CN == core)
-        order[which, count] = e
-        if found is not None:
-            pl.when(active)(lambda e=e: found(e))
-        count = count + active.astype(jnp.int32)
-    return count
-
-
-def over_active(count, footprints, ids, order, which, c, work, ready=None):
+def over_active(footprints, ids, order, which, c, work, ready=None):
+    count = order[which, ENTRIES]
+
     def step(i, carry):
         entries = []
         for u in range(STEP):
@@ -184,15 +185,18 @@
     lax.fori_loop(0, (count + STEP - 1) // STEP, step, 0)
 
 
-def predict_kernel(panels, own, mate, ids, out, held, order, sem, totals):
+def predict_kernel(panels, own, mate, ids, order, out, held, sem, totals):
     core = lax.axis_index("c")
 
     def copy(e):
         b, k = e // REFS, e % REFS
         return pltpu.make_async_copy(own.at[b, k], held.at[b, k], sem.at[e])
 
-    count = list_active(ids, order, 0, core, core, lambda e: copy(e).start())
-    count_mate = list_active(ids, order, 1, core, 1 - core)
+    def start(i, carry):
+        copy(order[0, i]).start()
+        return carry
+
+    lax.fori_loop(0, order[0, ENTRIES], start, 0)
     match = diagonal()
     totals[...] = jnp.zeros_like(totals)
 
@@ -211,8 +215,8 @@
         for (_, b, _, _), term in zip(found, terms):
             totals[b] = totals[b] + term
 
-    over_active(count_mate, mate, ids, order, 1, 1 - core, work)
-    over_active(count, held, ids, order, 0, core, work, lambda e: copy(e).wait())
+    over_active(mate, ids, order, 1, 1 - core, work)
+    over_active(held, ids, order, 0, core, work, lambda e: copy(e).wait())
     rows = [
         jnp.sum(totals[b, t * SUB : (t + 1) * SUB], axis=0, keepdims=True)
         for t in range(TRACERS)
@@ -223,10 +227,8 @@
         out[peer] = whole
 
 
-def adjoint_kernel(parts, both, held, mate, ids, misfits, out, order, lefts, sums):
+def adjoint_kernel(parts, both, held, mate, ids, order, misfits, out, lefts, sums):
     core = lax.axis_index("c")
-    count = list_active(ids, order, 0, core, core)
-    count_mate = list_active(ids, order, 1, core, 1 - core)
     whole = parts[0]
     for peer in range(1, parts.shape[0]):
         whole = whole + parts[peer]
@@ -265,8 +267,8 @@
             y, z = tile // CN % YN, tile // (CN * YN)
             sums[y, z] = sums[y, z] + value
 
-    over_active(count, held, ids, order, 0, core, work)
-    over_active(count_mate, mate, ids, order, 1, 1 - core, work)
+    over_active(held, ids, order, 0, core, work)
+    over_active(mate, ids, order, 1, 1 - core, work)
     out[...] = sums[...].astype(BF16)
 
 
@@ -324,34 +326,32 @@
     return lax.all_gather(own, "c"), other
 
 
-def run_predict(panels, footprints, mate, ids, peers):
+def run_predict(panels, footprints, mate, ids, order, peers):
     return call(
         predict_kernel,
         (shape(peers, TRACERS * SUB, LANES), pltpu.VMEM(footprints.shape, BF16)),
-        [VMEM, HBM, VMEM, SMEM],
+        [VMEM, HBM, VMEM, SMEM, SMEM],
         16,
         [
-            pltpu.SMEM((CN, ENTRIES + 1), jnp.int32),
             pltpu.SemaphoreType.DMA((ENTRIES,)),
             pltpu.VMEM((CN * BLOCKS, TRACERS * SUB, LANES), F32),
         ],
         name="predict",
-    )(panels, in_hbm(footprints), mate, ids)
-
-
-def run_adjoint(parts, both, held, mate, ids):
+    )(panels, in_hbm(footprints), mate, ids, order)
+
+
+def run_adjoint(parts, both, held, mate, ids, order):
     return call(
         adjoint_kernel,
         (shape(TRACERS * SUB, SIGHTS), shape(YN, ZN, SUB, PAY, dtype=BF16)),
-        [VMEM] * 4 + [SMEM],
+        [VMEM] * 4 + [SMEM] * 2,
         16,
         [
-            pltpu.SMEM((CN, ENTRIES + 1), jnp.int32),
             pltpu.VMEM((CN * BLOCKS, TRACERS * SUB, LANES), F32),
             pltpu.VMEM((YN, ZN, SUB, PAY), F32),
         ],
         name="adjoint",
-    )(parts, both, held, mate, ids)
+    )(parts, both, held, mate, ids, order)
 
 
 def shards(control, diffusivity, footprints, tile_lists, tile_counts, measured, weight):
@@ -365,30 +365,26 @@
         name="pack",
     )(*map(in_hbm, given))
     both, other = neighbours(own, head)
-    flux, listed = call(
-        flux_kernel,
-        (shape(ZN, SUB, PAY, dtype=BF16), shape(CN, BLOCKS, LANES, dtype=jnp.int32)),
-        [VMEM] * 2,
-        2,
-        name="flux",
-    )(both, other)
+    ids, order = call(
+        lists_kernel,
+        (pltpu.SMEM((CN, BLOCKS, LANES), jnp.int32), pltpu.SMEM((CN, ENTRIES + 1), jnp.int32)),
+        [VMEM],
+        1,
+        [pltpu.VMEM((CN, BLOCKS, LANES), jnp.int32), pltpu.SemaphoreType.DMA],
+        name="lists",
+    )(both)
+    both, ids, order = lax.optimization_barrier((both, ids, order))
+    flux = call(flux_kernel, shape(ZN, SUB, PAY, dtype=BF16), [VMEM] * 2, 2, name="flux")(both, other)
 
     by_z = lax.all_to_all(flux, "z", 0, 0, tiled=True)
     by_z, footprints = lax.optimization_barrier((by_z, footprints))
     mate = lax.ppermute(footprints, "c", [(0, 1), (1, 0)])
-    copies, ids = call(
-        copies_kernel,
-        (shape(YN, *by_z.shape, dtype=BF16), pltpu.SMEM(listed.shape, jnp.int32)),
-        [VMEM] * 2,
-        2,
-        [pltpu.SemaphoreType.DMA],
-        name="copies",
-    )(by_z, listed)
+    copies = call(copies_kernel, shape(YN, *by_z.shape, dtype=BF16), [VMEM], 2, name="copies")(by_z)
     panels = lax.all_to_all(copies, "y", 0, 0, tiled=True)
 
-    part, held = run_predict(panels, footprints, mate, ids, lax.axis_size("tm") * CN)
+    part, held = run_predict(panels, footprints, mate, ids, order, lax.axis_size("tm") * CN)
     parts = lax.all_to_all(part, ("tm", "c"), 0, 0, tiled=True)
-    misfits, dense = run_adjoint(parts, both, held, mate, ids)
+    misfits, dense = run_adjoint(parts, both, held, mate, ids, order)
 
     over_y = lax.all_to_all(dense, "y", 0, 0, tiled=True)
     coded = call(fold_y_kernel, shape(ZN, SUB, PAY + LANES, dtype=BF16), [VMEM], 2, name="fold_y")(over_y)

time: 101 us -> 101 us (level)
    all_to_all x1, blocking collectives: 15 us -> 16.4 us  [shards(): over_z = lax.all_to_all(coded, 'z', 0, 0, tiled=True)]
    all_to_all x1, blocking collectives: 10 us -> 8.86 us  [shards(): over_y = lax.all_to_all(dense, 'y', 0, 0, tiled=True)]
where the time goes in v8:
time: 101 us; the launch traced here: 99.5 us
  blocking collectives  76.9 us (76%)
  starting transfers between devices  15.7 us (16%)
  Pallas kernels  6.21 us (6%)
    all_to_all x1, blocking collectives, shards(): by_z = lax.all_to_all(flux, 'z', 0, 0, tiled=True)  24.9 us
    all_to_all x1, blocking collectives, shards(): over_z = lax.all_to_all(coded, 'z', 0, 0, tiled=True)  16.4 us
    ppermute x2, starting transfers between devices, neighbours(): other = lax.ppermute(head, OBS, pairs + [(b, a) for a, b in pairs])  10.4 us
    all_to_all x1, blocking collectives, shards(): panels = lax.all_to_all(copies, 'y', 0, 0, tiled=True)  10.3 us
    all_to_all x1, blocking collectives, shards(): parts = lax.all_to_all(part, ('tm', 'c'), 0, 0, tiled=True)  10.2 us
    all_to_all x1, blocking collectives, shards(): over_y = lax.all_to_all(dense, 'y', 0, 0, tiled=True)  8.86 us
    all_gather x2, blocking collectives, neighbours(): return (lax.all_gather(own, 'c'), other)  6.28 us
    ppermute x1, starting transfers between devices, shards(): mate = lax.ppermute(footprints, 'c', [(0, 1), (1, 0)])  5.23 us
  transfers between devices with their start and end apart: 3, of which 0 were waited for; matrix products, arithmetic and copies ran while one was open for 0% of the time, Pallas kernels for 1%

profile of v8, /device:TPU:1, one launch (start us, length us, event | category | flops | bytes accessed | tf_op | source)
XLA Modules:
  0.0 99.5 jit_solution(7802253172886609373)
XLA Ops:
  0.6 0.9 pack.1
  1.5 4.6 %collective-permute-start = (f32[8,512]{1,0:T(8,128)S(1)}, f32[8,512]{1,0:T(8,128)S(1)}, u32[]{:S(2)}, u32[]{:S(2)}) collective-permute-start(f32[8,512]{1,0:T(8,128)S(1)} %get-tuple-element.19), channel_id=1, source_target_pairs={{1,2},{3,4},{5,6},{7,8},{9,10},{11,12},{13,14},{15,16},{17,18},{19... | collective-permute-start | bytes 49160 | tf_op jit(solution)/shard_map/ppermute | solution.py:325
  6.1 4.5 %all-gather = f32[16,1024]{1,0:T(8,128)S(1)} all-gather(f32[8,1024]{1,0:T(8,128)S(1)} %get-tuple-element.15), channel_id=2, replica_groups=mesh['tm'=4,'z'=16,'y'=4,'c'=2] {'c'}, dimensions={0}, use_global_device_ids=true | all-gather | bytes 98304 | tf_op jit(solution)/shard_map/all_gather | solution.py:326
  10.6 0.8 lists.1
  11.4 0.0 collective-permute-done.other
  11.4 0.2 flux.1
  11.6 24.9 %all_to_all.25.source = bf16[16,8,384]{2,1,0:T(8,128)(2,1)S(1)} all-to-all(bf16[16,8,384]{2,1,0:T(8,128)(2,1)S(1)} %flux.1), channel_id=1, replica_groups=mesh['tm'=4,'z'=16,'y'=4,'c'=2] {'z'}, dimensions={0} | all-to-all | bytes 196608 | tf_op jit(solution)/shard_map/all_to_all | solution.py:379
  36.5 5.2 %collective-permute-start.1 = (bf16[4,4,128,1024]{3,2,1,0:T(8,128)(2,1)}, bf16[4,4,128,1024]{3,2,1,0:T(8,128)(2,1)S(1)}, u32[]{:S(2)}, u32[]{:S(2)}) collective-permute-start(bf16[4,4,128,1024]{3,2,1,0:T(8,128)(2,1)} %own), channel_id=1, source_target_pairs={{0,1},{1,0},{2,3},{3,2},{4,5},{5,4},{6,7},{7,6},{8,9},{9,8},{10,11... | collective-permute-start | bytes 12582920 | tf_op jit(solution)/shard_map/ppermute | solution.py:381
  41.8 10.3 %all_to_all.26.panels = bf16[4,16,8,384]{3,2,1,0:T(8,128)(2,1)S(1)} all-to-all(bf16[4,16,8,384]{3,2,1,0:T(8,128)(2,1)S(1)} %copies.1), channel_id=1, replica_groups=mesh['tm'=4,'z'=16,'y'=4,'c'=2] {'y'}, dimensions={0} | all-to-all | bytes 786432 | tf_op jit(solution)/shard_map/all_to_all | solution.py:383
  52.1 0.0 collective-permute-done.1.mate
  52.1 2.3 %predict.1 = (f32[8,24,128]{2,1,0:T(8,128)S(1)}, bf16[4,4,128,1024]{3,2,1,0:T(8,128)(2,1)S(1)}) custom-call(bf16[4,16,8,384]{3,2,1,0:T(8,128)(2,1)S(1)} %all_to_all.26.panels, bf16[4,4,128,1024]{3,2,1,0:T(8,128)(2,1)} %own, bf16[4,4,128,1024]{3,2,1,0:T(8,128)(2,1)S(1)} %collective-permute-done.1.mate, s32[2,4,128]{2,1,0:T(4,128)S(4)} %get-tuple-element.22.ids, ...), custom_call_target="tpu_custom_call" | custom-call | tf_op jit(solution)/shard_map/predict/pallas_call | solution.py:330
  54.4 10.2 %all_to_all.27.parts = f32[8,24,128]{2,1,0:T(8,128)S(1)} all-to-all(f32[8,24,128]{2,1,0:T(8,128)S(1)} %get-tuple-element.24), channel_id=1, replica_groups=mesh['tm'=4,'z'=16,'y'=4,'c'=2] {'tm','c'}, dimensions={0} | all-to-all | bytes 196608 | tf_op jit(solution)/shard_map/all_to_all | solution.py:386
  64.6 1.0 adjoint.1
  65.6 8.9 %all_to_all.28.parts = bf16[4,16,8,384]{3,2,1,0:T(8,128)(2,1)S(1)} all-to-all(bf16[4,16,8,384]{3,2,1,0:T(8,128)(2,1)S(1)} %get-tuple-element.26), channel_id=1, replica_groups=mesh['tm'=4,'z'=16,'y'=4,'c'=2] {'y'}, dimensions={0} | all-to-all | bytes 786432 | tf_op jit(solution)/shard_map/all_to_all | solution.py:389
  74.4 0.2 fold_y.1
  74.6 16.4 %all_to_all.29.parts = bf16[16,8,512]{2,1,0:T(8,128)(2,1)S(1)} all-to-all(bf16[16,8,512]{2,1,0:T(8,128)(2,1)S(1)} %fold_y.1), channel_id=1, replica_groups=mesh['tm'=4,'z'=16,'y'=4,'c'=2] {'z'}, dimensions={0} | all-to-all | bytes 262144 | tf_op jit(solution)/shard_map/all_to_all | solution.py:391
  90.9 0.1 fold_z.1
  91.0 5.8 %collective-permute-start.2 = (f32[8,384]{1,0:T(8,128)S(1)}, f32[8,384]{1,0:T(8,128)S(1)}, u32[]{:S(2)}, u32[]{:S(2)}) collective-permute-start(f32[8,384]{1,0:T(8,128)S(1)} %fold_z.1), channel_id=1, source_target_pairs={{1,2},{3,4},{5,6},{7,8},{9,10},{11,12},{13,14},{15,16},{17,18},{19... | collective-permute-start | bytes 36872 | tf_op jit(solution)/shard_map/ppermute | solution.py:325
  96.9 1.8 %all-gather.1 = f32[16,384]{1,0:T(8,128)S(1)} all-gather(f32[8,384]{1,0:T(8,128)S(1)} %fold_z.1), channel_id=3, replica_groups=mesh['tm'=4,'z'=16,'y'=4,'c'=2] {'c'}, dimensions={0}, use_global_device_ids=true | all-gather | bytes 36864 | tf_op jit(solution)/shard_map/all_gather | solution.py:326
  98.7 0.0 collective-permute-done.2.total_other
  98.7 0.8 final.1
  (1 shorter events, 0.0 us)
Async XLA Ops:
  1.5 9.9 %collective-permute-start = (f32[8,512]{1,0:T(8,128)S(1)}, f32[8,512]{1,0:T(8,128)S(1)}, u32[]{:S(2)}, u32[]{:S(2)}) collective-permute-start(f32[8,512]{1,0:T(8,128)S(1)} %get-tuple-element.19), channel_id=1, source_target_pairs={{1,2},{3,4},{5,6},{7,8},{9,10},{11,12},{13,14},{15,16},{17,18},{19... | collective-permute-start | bytes 49160 | tf_op jit(solution)/shard_map/ppermute | solution.py:325
  36.5 15.6 %collective-permute-start.1 = (bf16[4,4,128,1024]{3,2,1,0:T(8,128)(2,1)}, bf16[4,4,128,1024]{3,2,1,0:T(8,128)(2,1)S(1)}, u32[]{:S(2)}, u32[]{:S(2)}) collective-permute-start(bf16[4,4,128,1024]{3,2,1,0:T(8,128)(2,1)} %own), channel_id=1, source_target_pairs={{0,1},{1,0},{2,3},{3,2},{4,5},{5,4},{6,7},{7,6},{8,9},{9,8},{10,11... | collective-permute-start | bytes 12582920 | tf_op jit(solution)/shard_map/ppermute | solution.py:381
  91.0 7.7 %collective-permute-start.2 = (f32[8,384]{1,0:T(8,128)S(1)}, f32[8,384]{1,0:T(8,128)S(1)}, u32[]{:S(2)}, u32[]{:S(2)}) collective-permute-start(f32[8,384]{1,0:T(8,128)S(1)} %fold_z.1), channel_id=1, source_target_pairs={{1,2},{3,4},{5,6},{7,8},{9,10},{11,12},{13,14},{15,16},{17,18},{19... | collective-permute-start | bytes 36872 | tf_op jit(solution)/shard_map/ppermute | solution.py:325

commit v9 on v8

--- a/solution.py
+++ b/solution.py
@@ -79,6 +79,7 @@
     limit = jnp.zeros((BLOCKS, REFS), jnp.int32)
     for b in range(BLOCKS):
         limit = jnp.where(row == b, counts[0:1, b : b + 1], limit)
+    out[:, IDS * LANES : SEEN * LANES] = jnp.zeros((SUB, LANES), F32)
     out[:BLOCKS, IDS * LANES : IDS * LANES + REFS] = jnp.where(lane < limit, lists[...], -1).astype(F32)
     for which, ref in enumerate((measured, weight)):
         for t in range(TRACERS):

time: 101 us -> 101 us (level)
  no operation moved by 1% of the time
where the time goes in v9:
time: 101 us; the launch traced here: 99.8 us
  blocking collectives  76.8 us (76%)
  starting transfers between devices  15.7 us (16%)
  Pallas kernels  6.51 us (6%)
    all_to_all x1, blocking collectives, shards(): by_z = lax.all_to_all(flux, 'z', 0, 0, tiled=True)  24.9 us
    all_to_all x1, blocking collectives, shards(): over_z = lax.all_to_all(coded, 'z', 0, 0, tiled=True)  15.6 us
    ppermute x2, starting transfers between devices, neighbours(): other = lax.ppermute(head, OBS, pairs + [(b, a) for a, b in pairs])  10.5 us
    all_to_all x1, blocking collectives, shards(): panels = lax.all_to_all(copies, 'y', 0, 0, tiled=True)  10.3 us
    all_to_all x1, blocking collectives, shards(): parts = lax.all_to_all(part, ('tm', 'c'), 0, 0, tiled=True)  10.2 us
    all_to_all x1, blocking collectives, shards(): over_y = lax.all_to_all(dense, 'y', 0, 0, tiled=True)  9.53 us
    all_gather x2, blocking collectives, neighbours(): return (lax.all_gather(own, 'c'), other)  6.28 us
    ppermute x1, starting transfers between devices, shards(): mate = lax.ppermute(footprints, 'c', [(0, 1), (1, 0)])  5.23 us
  transfers between devices with their start and end apart: 3, of which 0 were waited for; matrix products, arithmetic and copies ran while one was open for 0% of the time, Pallas kernels for 1%

profile of v9, /device:TPU:1, one launch (start us, length us, event | category | flops | bytes accessed | tf_op | source)
XLA Modules:
  0.0 99.8 jit_solution(10550563732314610735)
XLA Ops:
  0.6 0.9 pack.1
  1.5 4.6 %collective-permute-start = (f32[8,512]{1,0:T(8,128)S(1)}, f32[8,512]{1,0:T(8,128)S(1)}, u32[]{:S(2)}, u32[]{:S(2)}) collective-permute-start(f32[8,512]{1,0:T(8,128)S(1)} %get-tuple-element.19), channel_id=1, source_target_pairs={{1,2},{3,4},{5,6},{7,8},{9,10},{11,12},{13,14},{15,16},{17,18},{19... | collective-permute-start | bytes 49160 | tf_op jit(solution)/shard_map/ppermute | solution.py:326
  6.1 4.5 %all-gather = f32[16,1024]{1,0:T(8,128)S(1)} all-gather(f32[8,1024]{1,0:T(8,128)S(1)} %get-tuple-element.15), channel_id=2, replica_groups=mesh['tm'=4,'z'=16,'y'=4,'c'=2] {'c'}, dimensions={0}, use_global_device_ids=true | all-gather | bytes 98304 | tf_op jit(solution)/shard_map/all_gather | solution.py:327
  10.6 0.8 lists.1
  11.4 0.0 collective-permute-done.other
  11.4 0.2 flux.1
  11.6 24.9 %all_to_all.25.source = bf16[16,8,384]{2,1,0:T(8,128)(2,1)S(1)} all-to-all(bf16[16,8,384]{2,1,0:T(8,128)(2,1)S(1)} %flux.1), channel_id=1, replica_groups=mesh['tm'=4,'z'=16,'y'=4,'c'=2] {'z'}, dimensions={0} | all-to-all | bytes 196608 | tf_op jit(solution)/shard_map/all_to_all | solution.py:380
  36.5 5.2 %collective-permute-start.1 = (bf16[4,4,128,1024]{3,2,1,0:T(8,128)(2,1)}, bf16[4,4,128,1024]{3,2,1,0:T(8,128)(2,1)S(1)}, u32[]{:S(2)}, u32[]{:S(2)}) collective-permute-start(bf16[4,4,128,1024]{3,2,1,0:T(8,128)(2,1)} %own), channel_id=1, source_target_pairs={{0,1},{1,0},{2,3},{3,2},{4,5},{5,4},{6,7},{7,6},{8,9},{9,8},{10,11... | collective-permute-start | bytes 12582920 | tf_op jit(solution)/shard_map/ppermute | solution.py:382
  41.8 10.3 %all_to_all.26.panels = bf16[4,16,8,384]{3,2,1,0:T(8,128)(2,1)S(1)} all-to-all(bf16[4,16,8,384]{3,2,1,0:T(8,128)(2,1)S(1)} %copies.1), channel_id=1, replica_groups=mesh['tm'=4,'z'=16,'y'=4,'c'=2] {'y'}, dimensions={0} | all-to-all | bytes 786432 | tf_op jit(solution)/shard_map/all_to_all | solution.py:384
  52.1 0.0 collective-permute-done.1.mate
  52.1 2.3 %predict.1 = (f32[8,24,128]{2,1,0:T(8,128)S(1)}, bf16[4,4,128,1024]{3,2,1,0:T(8,128)(2,1)S(1)}) custom-call(bf16[4,16,8,384]{3,2,1,0:T(8,128)(2,1)S(1)} %all_to_all.26.panels, bf16[4,4,128,1024]{3,2,1,0:T(8,128)(2,1)} %own, bf16[4,4,128,1024]{3,2,1,0:T(8,128)(2,1)S(1)} %collective-permute-done.1.mate, s32[2,4,128]{2,1,0:T(4,128)S(4)} %get-tuple-element.22.ids, ...), custom_call_target="tpu_custom_call" | custom-call | tf_op jit(solution)/shard_map/predict/pallas_call | solution.py:331
  54.4 10.2 %all_to_all.27.parts = f32[8,24,128]{2,1,0:T(8,128)S(1)} all-to-all(f32[8,24,128]{2,1,0:T(8,128)S(1)} %get-tuple-element.24), channel_id=1, replica_groups=mesh['tm'=4,'z'=16,'y'=4,'c'=2] {'tm','c'}, dimensions={0} | all-to-all | bytes 196608 | tf_op jit(solution)/shard_map/all_to_all | solution.py:387
  64.6 1.3 %adjoint.1 = (f32[24,128]{1,0:T(8,128)S(1)}, bf16[4,16,8,384]{3,2,1,0:T(8,128)(2,1)S(1)}) custom-call(f32[8,24,128]{2,1,0:T(8,128)S(1)} %all_to_all.27.parts, f32[2,8,1024]{2,1,0:T(8,128)S(1)} %bitcast.5, bf16[4,4,128,1024]{3,2,1,0:T(8,128)(2,1)S(1)} %get-tuple-element.25.held, bf16[4,4,128,1024]{3,2,1,0:T(8,128)(2,1)S(1)} %collective-permute-done.1.mate, ...), custom_call_target="tpu_custom_call" | custom-call | tf_op jit(solution)/shard_map/adjoint/pallas_call | solution.py:345
  65.9 9.5 %all_to_all.28.parts = bf16[4,16,8,384]{3,2,1,0:T(8,128)(2,1)S(1)} all-to-all(bf16[4,16,8,384]{3,2,1,0:T(8,128)(2,1)S(1)} %get-tuple-element.26), channel_id=1, replica_groups=mesh['tm'=4,'z'=16,'y'=4,'c'=2] {'y'}, dimensions={0} | all-to-all | bytes 786432 | tf_op jit(solution)/shard_map/all_to_all | solution.py:390
  75.4 0.2 fold_y.1
  75.5 15.6 %all_to_all.29.parts = bf16[16,8,512]{2,1,0:T(8,128)(2,1)S(1)} all-to-all(bf16[16,8,512]{2,1,0:T(8,128)(2,1)S(1)} %fold_y.1), channel_id=1, replica_groups=mesh['tm'=4,'z'=16,'y'=4,'c'=2] {'z'}, dimensions={0} | all-to-all | bytes 262144 | tf_op jit(solution)/shard_map/all_to_all | solution.py:392
  91.2 0.1 fold_z.1
  91.2 5.9 %collective-permute-start.2 = (f32[8,384]{1,0:T(8,128)S(1)}, f32[8,384]{1,0:T(8,128)S(1)}, u32[]{:S(2)}, u32[]{:S(2)}) collective-permute-start(f32[8,384]{1,0:T(8,128)S(1)} %fold_z.1), channel_id=1, source_target_pairs={{1,2},{3,4},{5,6},{7,8},{9,10},{11,12},{13,14},{15,16},{17,18},{19... | collective-permute-start | bytes 36872 | tf_op jit(solution)/shard_map/ppermute | solution.py:326
  97.1 1.8 %all-gather.1 = f32[16,384]{1,0:T(8,128)S(1)} all-gather(f32[8,384]{1,0:T(8,128)S(1)} %fold_z.1), channel_id=3, replica_groups=mesh['tm'=4,'z'=16,'y'=4,'c'=2] {'c'}, dimensions={0}, use_global_device_ids=true | all-gather | bytes 36864 | tf_op jit(solution)/shard_map/all_gather | solution.py:327
  99.0 0.0 collective-permute-done.2.total_other
  99.0 0.8 final.1
  (1 shorter events, 0.0 us)
Async XLA Ops:
  1.5 9.9 %collective-permute-start = (f32[8,512]{1,0:T(8,128)S(1)}, f32[8,512]{1,0:T(8,128)S(1)}, u32[]{:S(2)}, u32[]{:S(2)}) collective-permute-start(f32[8,512]{1,0:T(8,128)S(1)} %get-tuple-element.19), channel_id=1, source_target_pairs={{1,2},{3,4},{5,6},{7,8},{9,10},{11,12},{13,14},{15,16},{17,18},{19... | collective-permute-start | bytes 49160 | tf_op jit(solution)/shard_map/ppermute | solution.py:326
  36.5 15.6 %collective-permute-start.1 = (bf16[4,4,128,1024]{3,2,1,0:T(8,128)(2,1)}, bf16[4,4,128,1024]{3,2,1,0:T(8,128)(2,1)S(1)}, u32[]{:S(2)}, u32[]{:S(2)}) collective-permute-start(bf16[4,4,128,1024]{3,2,1,0:T(8,128)(2,1)} %own), channel_id=1, source_target_pairs={{0,1},{1,0},{2,3},{3,2},{4,5},{5,4},{6,7},{7,6},{8,9},{9,8},{10,11... | collective-permute-start | bytes 12582920 | tf_op jit(solution)/shard_map/ppermute | solution.py:382
  91.2 7.7 %collective-permute-start.2 = (f32[8,384]{1,0:T(8,128)S(1)}, f32[8,384]{1,0:T(8,128)S(1)}, u32[]{:S(2)}, u32[]{:S(2)}) collective-permute-start(f32[8,384]{1,0:T(8,128)S(1)} %fold_z.1), channel_id=1, source_target_pairs={{1,2},{3,4},{5,6},{7,8},{9,10},{11,12},{13,14},{15,16},{17,18},{19... | collective-permute-start | bytes 36872 | tf_op jit(solution)/shard_map/ppermute | solution.py:326
